TPU v7x, 32 devices: a whole 2x2x4 slice. The times are simulated.
32 devices in a mesh: dp: 16 (over z, y, x), tensor: 2 (over core).
Axes of the slice: x: 2, y: 2, z: 4, core: 2. Of those that a mesh axis runs over, the one named last changes fastest.
Arguments:
- tokens: bfloat16 [32768, 768], P(('dp', 'tensor')), may hold values from -6 to 6
- pre_gain: bfloat16 [768], replicated, may hold values from 0.5 to 1.5
- w_zx: bfloat16 [768, 2, 1536], P('dp', None, 'tensor'), may hold values from -0.21875 to 0.21875
- w_bc: bfloat16 [768, 256], P('dp'), may hold values from -0.21875 to 0.21875
- w_dt: bfloat16 [768, 24], P('dp', 'tensor'), may hold values from -0.21875 to 0.21875
- conv_x: bfloat16 [5, 1536], P(None, 'tensor'), may hold values from -3 to 3
- conv_bc: bfloat16 [5, 256], replicated, may hold values from -3 to 3
- a_log: float32 [24], P('tensor'), may hold values from -3 to 1
- dt_bias: float32 [24], P('tensor'), may hold values from -5 to -1
- skip_gain: float32 [24], P('tensor'), may hold values from 0.5 to 1.5
- norm_gain: bfloat16 [1536], P('tensor'), may hold values from 0.5 to 1.5
- w_out: bfloat16 [1536, 768], P('tensor', 'dp'), may hold values from -0.15625 to 0.15625
- cotangent: bfloat16 [32768, 768], P(('dp', 'tensor')), may hold values from -6 to 6
Outputs:
- out: bfloat16 [32768, 768], P(('dp', 'tensor'))
- grad_tokens: bfloat16 [32768, 768], P(('dp', 'tensor'))
- grad_pre_gain: float32 [768], replicated
- grad_w_zx: float32 [768, 2, 1536], P('dp', None, 'tensor')
- grad_w_bc: float32 [768, 256], P('dp')
- grad_w_dt: float32 [768, 24], P('dp', 'tensor')
- grad_conv_x: float32 [5, 1536], P(None, 'tensor')
- grad_conv_bc: float32 [5, 256], replicated
- grad_a_log: float32 [24], P('tensor')
- grad_dt_bias: float32 [24], P('tensor')
- grad_skip_gain: float32 [24], P('tensor')
- grad_norm_gain: float32 [1536], P('tensor')
- grad_w_out: float32 [1536, 768], P('tensor', 'dp')
All inputs are finite; a program needn't handle non-finite values.
Results may differ from a plain program's by a relative error of at most 0.014.
Values may be sent and summed in bfloat16 or wider, within the bound.
No kernel may reach another device: no remote copies, remote signals or barrier semaphores. Data moves between devices by JAX's collectives and lax.ppermute only.
A program may use at most 256 MiB of HBM per device.

v0:
```python
import functools

import jax
import jax.numpy as jnp
from jax import lax
from jax.experimental import pallas as pl
from jax.experimental.pallas import tpu as pltpu
from jax.sharding import PartitionSpec as P

LEN = 1024
Q = 128
HEAD = 64
STATE = 128
epsilon = 1e-05
f32 = jnp.float32
b16 = jnp.bfloat16
exact = lax.Precision.HIGHEST
MIB = 1024 * 1024


def nn(a, b, precision=None):
    return lax.dot_general(
        a, b, (((1,), (0,)), ((), ())), preferred_element_type=f32, precision=precision
    )


def nt(a, b, precision=None):
    return lax.dot_general(
        a, b, (((1,), (1,)), ((), ())), preferred_element_type=f32, precision=precision
    )


def tn(a, b):
    return lax.dot_general(a, b, (((0,), (0,)), ((), ())), preferred_element_type=f32)


def sigmoid(v):
    return 0.5 * jnp.tanh(0.5 * v) + 0.5


def softplus(v):
    return jnp.maximum(v, 0.0) + jnp.log1p(jnp.exp(-jnp.abs(v)))


def iota(axis):
    return lax.broadcasted_iota(jnp.int32, (Q, Q), axis)


def token(row):
    return ((row & 7) << 4) | (row >> 3)


def sublane(width):
    return lax.broadcasted_iota(jnp.int32, (24, width), 0) & 7


def with_past(here, past):
    mixed = jnp.where(
        sublane(here.shape[1]) == 0, pltpu.roll(past, 17, 0), pltpu.roll(here[Q - 24 :], 1, 0)
    )
    return jnp.concatenate([mixed, here], axis=0)


def with_future(here, future):
    mixed = jnp.where(
        sublane(here.shape[1]) == 7, pltpu.roll(future, 7, 0), pltpu.roll(here[:24], 23, 0)
    )
    return jnp.concatenate([here, mixed], axis=0)


def conv(padded, taps, lanes):
    total = taps[4:5, lanes]
    for k in range(4):
        total = total + taps[k : k + 1, lanes] * padded[8 * k : 8 * k + Q]
    return total


def fold(value):
    return jnp.sum(value.reshape(Q // 8, 8, value.shape[1]), axis=0)


def split_low(value, count):
    pieces = []
    for _ in range(count):
        piece = value.astype(b16)
        pieces.append(piece)
        value = value - piece.astype(f32)
    return jnp.concatenate(pieces, axis=1)


def head_rates(dt_raw, heads_ref, low_tri):
    step = softplus(dt_raw + heads_ref[0:1, :])
    decay = -step * heads_ref[1:2, :]
    sums = nn(low_tri, split_low(decay, 3))
    cum = sums[:, :Q] + sums[:, Q : 2 * Q] + sums[:, 2 * Q :]
    return step, decay, cum


def scan_forward_kernel(
    per_seq, pairs, base, resumed, *refs
):
    xin_ref, xhalo_ref, bd_ref, bdhalo_ref, cx_ref, cb_ref, heads_ref = refs[:7]
    y_ref, state_out_ref, pre_ref, rates_ref, state = refs[-5:]
    first = ((base + pl.program_id(0)) % per_seq) == 0

    if resumed:

        @pl.when(pl.program_id(0) == 0)
        def _():
            state[...] = refs[7][...]

    @pl.when(first)
    def _():
        state[...] = jnp.zeros_like(state)

    keep = jnp.where(first, 0.0, 1.0)
    rows, cols = token(iota(0)), token(iota(1))
    lower = rows >= cols
    low_tri = jnp.where(lower, 1.0, 0.0).astype(b16)
    left = iota(1) < HEAD
    bs = with_past(bd_ref[:, : 2 * STATE], bdhalo_ref[8:32, : 2 * STATE] * keep)
    pre_bc = conv(bs, cb_ref, slice(0, 2 * STATE))
    bc = pre_bc * sigmoid(pre_bc)
    b_low, c_low = bc[:, :STATE].astype(b16), bc[:, STATE:].astype(b16)
    gram = jnp.where(lower, nt(c_low, b_low), 0.0)
    step, decay, cum = head_rates(bd_ref[:, 2 * STATE :], heads_ref, low_tri)
    cum_rows = cum.T
    rates_ref[:, :Q] = step
    rates_ref[:, Q:] = cum
    b_turned = bc[:, :STATE].T.astype(b16)
    for p in range(pairs):
        sl = slice(p * Q, (p + 1) * Q)
        past = xhalo_ref[:, sl].astype(f32)[8:32] * keep
        pre = conv(with_past(xin_ref[:, sl].astype(f32), past), cx_ref, sl)
        pre_ref[:, sl] = pre.astype(b16)
        x = pre * sigmoid(pre)
        step2 = jnp.where(left, step[:, 2 * p : 2 * p + 1], step[:, 2 * p + 1 : 2 * p + 2])
        scaled = x * step2
        c0 = jnp.broadcast_to(cum[:, 2 * p : 2 * p + 1], (Q, Q))
        c1 = jnp.broadcast_to(cum[:, 2 * p + 1 : 2 * p + 2], (Q, Q))
        w0 = jnp.exp(jnp.minimum(c0 - cum_rows[2 * p : 2 * p + 1, :], 0.0)) * gram
        w1 = jnp.exp(jnp.minimum(c1 - cum_rows[2 * p + 1 : 2 * p + 2, :], 0.0)) * gram
        weights = jnp.concatenate([w0.astype(b16), w1.astype(b16)], axis=1)
        split = jnp.concatenate(
            [jnp.where(left, scaled, 0.0).astype(b16), jnp.where(left, 0.0, scaled).astype(b16)], axis=0
        )
        both = jnp.where(left, c0, c1)
        entering = state[:, sl]
        held = entering.astype(b16)
        state_out_ref[0, :, sl] = held
        y = nn(weights, split) + nn(c_low, held) * jnp.exp(both) + cx_ref[5:6, sl] * x
        y_ref[:, sl] = y.astype(b16)
        leaving = (scaled * jnp.exp(both[Q - 1 : Q, :] - both)).astype(b16)
        state[:, sl] = entering * jnp.exp(both[Q - 1 : Q, :]) + nn(b_turned, leaving)


def scan_forward(xin, bd, cx, cb, heads, base, count, before):
    rows, inner = xin.shape
    blocks, per_seq, pairs = rows // Q, LEN // Q, inner // Q
    wide = bd.shape[1]
    kept = [] if before is None else [before[4], *before[:4]]
    return pl.pallas_call(
        functools.partial(scan_forward_kernel, per_seq, pairs, base, before is not None),
        grid=(count,),
        in_specs=[
            pl.BlockSpec((Q, inner), lambda k: (base + k, 0)),
            pl.BlockSpec((32, inner), lambda k: (jnp.maximum((base + k) * (Q // 32) - 1, 0), 0)),
            pl.BlockSpec((Q, wide), lambda k: (base + k, 0)),
            pl.BlockSpec((32, wide), lambda k: (jnp.maximum((base + k) * (Q // 32) - 1, 0), 0)),
            pl.BlockSpec(cx.shape, lambda k: (0, 0)),
            pl.BlockSpec(cb.shape, lambda k: (0, 0)),
            pl.BlockSpec(heads.shape, lambda k: (0, 0)),
        ]
        + ([pl.BlockSpec((STATE, inner), lambda k: (0, 0))] + [pl.BlockSpec(memory_space=pl.ANY)] * 4 if kept else []),
        out_specs=[
            pl.BlockSpec((Q, inner), lambda k: (base + k, 0)),
            pl.BlockSpec((1, STATE, inner), lambda k: (base + k, 0, 0)),
            pl.BlockSpec((Q, inner), lambda k: (base + k, 0)),
            pl.BlockSpec((Q, 2 * Q), lambda k: (base + k, 0)),
            pl.BlockSpec((STATE, inner), lambda k: (0, 0)),
        ],
        out_shape=[
            jax.ShapeDtypeStruct((rows, inner), b16),
            jax.ShapeDtypeStruct((blocks, STATE, inner), b16),
            jax.ShapeDtypeStruct((rows, inner), b16),
            jax.ShapeDtypeStruct((rows, 2 * Q), f32),
            jax.ShapeDtypeStruct((STATE, inner), f32),
        ],
        input_output_aliases={8: 0, 9: 1, 10: 2, 11: 3} if kept else {},
        compiler_params=pltpu.CompilerParams(vmem_limit_bytes=56 * MIB),
        cost_estimate=pl.CostEstimate(flops=count * Q * inner * 6000, bytes_accessed=count * Q * inner * 8, transcendentals=count * Q * inner * 8),
        name="scan_forward",
    )(xin, xin, bd, bd, cx, cb, heads, *kept)


def scan_backward_kernel(
    per_seq, pairs, base, count, resumed, *refs
):
    (dy_ref, xin_ref, pre_ref, bd_ref, bdhalo_ref, held_ref, rates_ref, cx_ref, cb_ref, heads_ref, pick_ref) = refs[:11]
    (
        dxin_ref, dbd_ref, adjoint, xnext, bnext, gx_ref, gb_ref, gh_ref,
        xt, dye, lam_low, products, row_sums,
    ) = refs[-13:]
    step_id = pl.program_id(0)
    block = base + count - 1 - step_id
    first = (block % per_seq) == 0
    last = (block % per_seq) == per_seq - 1

    @pl.when(step_id == 0)
    def _():
        row_sums[...] = jnp.zeros_like(row_sums)
        for here, ref in enumerate((adjoint, xnext, bnext, gx_ref, gb_ref, gh_ref)):
            ref[...] = refs[11 + here][...] if resumed else jnp.zeros_like(ref)

    @pl.when(last)
    def _():
        adjoint[...] = jnp.zeros_like(adjoint)
        xnext[...] = jnp.zeros_like(xnext)
        bnext[...] = jnp.zeros_like(bnext)

    keep = jnp.where(first, 0.0, 1.0)
    rows, cols = token(iota(0)), token(iota(1))
    upper = cols >= rows
    left = iota(1) < HEAD
    left_low = jnp.where(left, 1.0, 0.0).astype(b16)
    right_low = jnp.where(left, 0.0, 1.0).astype(b16)
    ones_low = jnp.ones((8, Q), b16)
    lane_of = lax.broadcasted_iota(jnp.int32, (2 * Q, Q), 1)
    half_of = lax.broadcasted_iota(jnp.int32, (2 * Q, Q), 0) // Q
    bs = with_past(bd_ref[:, : 2 * STATE], bdhalo_ref[8:32, : 2 * STATE] * keep)
    pre_bc = conv(bs, cb_ref, slice(0, 2 * STATE))
    sig_bc = sigmoid(pre_bc)
    bc = pre_bc * sig_bc
    b_low, c_low = bc[:, :STATE].astype(b16), bc[:, STATE:].astype(b16)
    gram = jnp.where(upper, nt(b_low, c_low), 0.0)
    raw = bd_ref[:, 2 * STATE :]
    step, cum = rates_ref[:, :Q], rates_ref[:, Q:]
    cum_rows = cum.T
    c_turned = bc[:, STATE:].T.astype(b16)
    inner_states = []
    dgram = jnp.zeros((Q, Q), f32)
    col_sums = jnp.zeros((Q, Q), f32)
    for p in range(pairs):
        sl = slice(p * Q, (p + 1) * Q)
        pre = pre_ref[:, sl].astype(f32)
        sig = sigmoid(pre)
        x = pre * sig
        step2 = jnp.where(left, step[:, 2 * p : 2 * p + 1], step[:, 2 * p + 1 : 2 * p + 2])
        scaled = x * step2
        dy_low = dy_ref[:, sl]
        dy = dy_low.astype(f32)
        split = jnp.concatenate([dy_low * left_low, dy_low * right_low], axis=0)
        dweights = nt(scaled.astype(b16), split)
        c0 = jnp.broadcast_to(cum[:, 2 * p : 2 * p + 1], (Q, Q))
        c1 = jnp.broadcast_to(cum[:, 2 * p + 1 : 2 * p + 2], (Q, Q))
        weights, crossing = [], []
        for half, column in ((0, c0), (1, c1)):
            head = 2 * p + half
            fade = jnp.exp(jnp.minimum(cum_rows[head : head + 1, :] - column, 0.0))
            weights.append((fade * gram).astype(b16))
            faded = dweights[:, half * Q : (half + 1) * Q] * fade
            dgram = dgram + faded
            crossing.append((faded * gram).astype(b16))
        crossing = jnp.concatenate(crossing, axis=1)
        over_rows = nn(ones_low, crossing)
        row_sums[2 * p : 2 * p + 1, :] = over_rows[0:1, :Q]
        row_sums[2 * p + 1 : 2 * p + 2, :] = over_rows[0:1, Q:]
        col_sums = col_sums + nn(crossing, jnp.where(lane_of == 2 * p + half_of, 1.0, 0.0).astype(b16))
        both = jnp.where(left, c0, c1)
        tail = jnp.exp(both[Q - 1 : Q, :] - both)
        rise = jnp.exp(both)
        held = held_ref[0, :, sl]
        lam = adjoint[:, sl]
        lam_here = lam.astype(b16)
        lam_low[:, sl] = lam_here
        inner_states.append(jnp.sum(lam * held.astype(f32), axis=0, keepdims=True))
        dx_state = nn(b_low, lam_here) * tail
        dscaled = nn(jnp.concatenate(weights, axis=1), split) + dx_state
        dye_here = dy * rise
        products[0:Q, sl] = (dye_here * nn(c_low, held)).astype(b16)
        products[Q : 2 * Q, sl] = (scaled * dx_state).astype(b16)
        products[2 * Q :, sl] = (dscaled * x).astype(b16)
        xt[:, sl] = (scaled * tail).astype(b16)
        dye_low = dye_here.astype(b16)
        dye[:, sl] = dye_low
        adjoint[:, sl] = lam * rise[Q - 1 : Q, :] + nn(c_turned, dye_low)
        dx = dscaled * step2 + cx_ref[5:6, sl] * dy
        dpre = dx * (sig + x * (1.0 - sig))
        padded = with_future(dpre, xnext[:, sl])
        xnext[:, sl] = dpre[:24]
        dxin = jnp.zeros((Q, Q), f32)
        xin = xin_ref[:, sl].astype(f32)
        for k in range(4):
            ahead = padded[24 - 8 * k : 24 - 8 * k + Q]
            dxin = dxin + cx_ref[k : k + 1, sl] * ahead
            gx_ref[8 * k : 8 * k + 8, sl] += fold(ahead * xin)
        dxin_ref[:, sl] = dxin.astype(b16)
        gx_ref[32:40, sl] += fold(dpre)
        gx_ref[40:48, sl] += fold(dy * x)
    dgram_low = jnp.where(upper, dgram, 0.0)
    db = nn(dgram_low.astype(b16), c_low) + nt(xt[...], lam_low[...])
    dc = nn(dgram_low.T.astype(b16), b_low) + nt(dye[...], held_ref[0])
    total = cum[Q - 1 : Q, :]
    inner_states = jnp.concatenate(inner_states, axis=1)
    pick = pick_ref[...]
    summed = nn(products[...], pick)
    high = inner_states.astype(b16)
    low = (inner_states - high.astype(f32)).astype(b16)
    both_states = jnp.concatenate([jnp.broadcast_to(high, (8, high.shape[1])), jnp.broadcast_to(low, (8, low.shape[1]))], axis=0)
    state_sums = nn(both_states, pick)
    constant = jnp.exp(total) * (state_sums[0:1, :] + state_sums[8:9, :])
    up_tri = jnp.where(upper, 1.0, 0.0).astype(b16)
    strict = jnp.where(rows > cols, 1.0, 0.0).astype(b16)
    moved = jnp.concatenate([summed[:Q] - col_sums + row_sums[...].T, summed[Q : 2 * Q]], axis=0)
    crossed = nn(jnp.concatenate([up_tri, strict], axis=1), split_low(moved, 3))
    ddecay = crossed[:, :Q] + crossed[:, Q : 2 * Q] + crossed[:, 2 * Q :] + constant
    summed3 = summed[2 * Q :]
    dstep = summed3 - ddecay * heads_ref[1:2, :]
    draw = dstep * sigmoid(raw + heads_ref[0:1, :])
    gh_ref[0:1, :] += jnp.sum(ddecay * step, axis=0, keepdims=True) * -heads_ref[1:2, :]
    gh_ref[1:2, :] += jnp.sum(draw, axis=0, keepdims=True)
    dbc = jnp.concatenate([db, dc], axis=1)
    dpre_bc = dbc * sig_bc * (1.0 + pre_bc * (1.0 - sig_bc))
    padded = with_future(dpre_bc, bnext[...])
    bnext[...] = dpre_bc[:24]
    dbc_in = jnp.zeros((Q, 2 * STATE), f32)
    for k in range(4):
        ahead = padded[24 - 8 * k : 24 - 8 * k + Q]
        dbc_in = dbc_in + cb_ref[k : k + 1, :] * ahead
        gb_ref[8 * k : 8 * k + 8, :] += fold(ahead * bd_ref[:, : 2 * STATE])
    gb_ref[32:40, :] += fold(dpre_bc)
    dbd_ref[:, : 2 * STATE] = dbc_in.astype(b16)
    dbd_ref[:, 2 * STATE :] = draw.astype(b16)


def scan_backward(dy, xin, pre, bd, held, rates, cx, cb, heads, pick, base, count, before):
    rows, inner = xin.shape
    blocks, per_seq, pairs = rows // Q, LEN // Q, inner // Q
    wide = bd.shape[1]
    back = lambda k: base + count - 1 - k
    fixed = lambda shape: pl.BlockSpec(shape, lambda k: (0, 0))
    carry = [(STATE, inner), (24, inner), (24, 2 * STATE), (48, inner), (40, 2 * STATE), (8, Q)]
    kept = [] if before is None else [*before[2:], before[0], before[1]]
    return pl.pallas_call(
        functools.partial(scan_backward_kernel, per_seq, pairs, base, count, before is not None),
        grid=(count,),
        in_specs=[
            pl.BlockSpec((Q, inner), lambda k: (back(k), 0)),
            pl.BlockSpec((Q, inner), lambda k: (back(k), 0)),
            pl.BlockSpec((Q, inner), lambda k: (back(k), 0)),
            pl.BlockSpec((Q, wide), lambda k: (back(k), 0)),
            pl.BlockSpec((32, wide), lambda k: (jnp.maximum(back(k) * (Q // 32) - 1, 0), 0)),
            pl.BlockSpec((1, STATE, inner), lambda k: (back(k), 0, 0)),
            pl.BlockSpec((Q, 2 * Q), lambda k: (back(k), 0)),
            fixed(cx.shape),
            fixed(cb.shape),
            fixed(heads.shape),
            fixed(pick.shape),
        ]
        + ([fixed(shape) for shape in carry] + [pl.BlockSpec(memory_space=pl.ANY)] * 2 if kept else []),
        out_specs=[
            pl.BlockSpec((Q, inner), lambda k: (back(k), 0)),
            pl.BlockSpec((Q, wide), lambda k: (back(k), 0)),
        ]
        + [fixed(shape) for shape in carry],
        out_shape=[
            jax.ShapeDtypeStruct((rows, inner), b16),
            jax.ShapeDtypeStruct((rows, wide), b16),
        ]
        + [jax.ShapeDtypeStruct(shape, f32) for shape in carry],
        input_output_aliases={17: 0, 18: 1} if kept else {},
        scratch_shapes=[
            pltpu.VMEM((Q, inner), b16),
            pltpu.VMEM((Q, inner), b16),
            pltpu.VMEM((STATE, inner), b16),
            pltpu.VMEM((3 * Q, inner), b16),
            pltpu.VMEM((Q, Q), f32),
        ],
        compiler_params=pltpu.CompilerParams(vmem_limit_bytes=56 * MIB),
        cost_estimate=pl.CostEstimate(flops=count * Q * inner * 12000, bytes_accessed=count * Q * inner * 10, transcendentals=count * Q * inner * 8),
        name="scan_backward",
    )(dy, xin, pre, bd, bd, held, rates, cx, cb, heads, pick, *kept)


def gate_kernel(y, normed, cot, w_z, w_out_t, gain, mixed, dz, dssd, grad_norm, zs, hats, dhats):
    @pl.when(pl.program_id(0) == 0)
    def _():
        grad_norm[...] = jnp.zeros_like(grad_norm)

    rows, inner = y.shape
    chunks = [slice(begin, begin + 256) for begin in range(0, inner, 256)]
    squares = jnp.zeros((rows, 128), f32)
    for sl in chunks:
        z = nn(normed[...], w_z[:, sl])
        zs[:, sl] = z
        gated = y[:, sl].astype(f32) * (z * sigmoid(z))
        hats[:, sl] = gated
        square = gated * gated
        squares = squares + square[:, :128] + square[:, 128:]
    inv = lax.rsqrt(jnp.sum(squares, axis=1, keepdims=True) / inner + epsilon)
    crosses = jnp.zeros((rows, 128), f32)
    for sl in chunks:
        hat = hats[:, sl] * inv
        hats[:, sl] = hat
        mixed[:, sl] = (hat * gain[:, sl]).astype(b16)
        dmixed = nn(cot[...], w_out_t[:, sl])
        dhat = dmixed * gain[:, sl]
        dhats[:, sl] = dhat
        product = dmixed * hat
        grad_norm[:, sl] += jnp.sum(product.reshape(rows // 8, 8, 256), axis=0)
        product = dhat * hat
        crosses = crosses + product[:, :128] + product[:, 128:]
    cross = jnp.sum(crosses, axis=1, keepdims=True) / inner
    for sl in chunks:
        dgated = inv * (dhats[:, sl] - hats[:, sl] * cross)
        z = zs[:, sl]
        sig = sigmoid(z)
        gate = z * sig
        dz[:, sl] = (dgated * y[:, sl].astype(f32) * (sig + gate * (1.0 - sig))).astype(b16)
        dssd[:, sl] = (dgated * gate).astype(b16)


def gate_both(y, normed, cot, w_z, w_out_t, gain):
    rows, inner = y.shape
    model = normed.shape[1]
    size = 256
    tall = lambda width: pl.BlockSpec((size, width), lambda k: (k, 0))
    fixed = lambda shape: pl.BlockSpec(shape, lambda k: (0, 0))
    return pl.pallas_call(
        gate_kernel,
        grid=(rows // size,),
        in_specs=[tall(inner), tall(model), tall(model), fixed(w_z.shape), fixed(w_out_t.shape), fixed(gain.shape)],
        out_specs=[tall(inner)] * 3 + [fixed((8, inner))],
        out_shape=[jax.ShapeDtypeStruct((rows, inner), b16)] * 3 + [jax.ShapeDtypeStruct((8, inner), f32)],
        scratch_shapes=[pltpu.VMEM((size, inner), f32)] * 3,
        compiler_params=pltpu.CompilerParams(vmem_limit_bytes=56 * MIB),
        cost_estimate=pl.CostEstimate(flops=rows * inner * 8000, bytes_accessed=rows * inner * 10, transcendentals=rows * inner * 2),
        name="gate_both",
    )(y, normed, cot, w_z, w_out_t, gain)


def swap(value, bit, axis="dp"):
    count = lax.axis_size(axis)
    return lax.ppermute(value, axis, [(i, i ^ bit) for i in range(count)])


def tie(value, *others):
    return lax.optimization_barrier((value, *others))[0]


def fast(rows):
    return lax.axis_size("dp") == 16 and rows % 16 == 0


def along_z(shard):
    return jnp.stack([shard] + [swap(shard, z << 2) for z in (1, 2, 3)])


def around(column):
    return [column] + [swap(column, q) for q in (1, 2, 3)]


def merge_kernel(rows, layout, where_ref, *refs):
    mine, other, outs = refs[:4], refs[4:8], refs[8:]
    me, side = where_ref[0], where_ref[1]
    for q in range(4):
        for z in range(4):
            start = pl.multiple_of((me ^ (4 * z + q)) * rows, 16)
            for piece, half in ((mine[q], side), (other[q], 1 - side)):
                for out, (begin, width) in zip(outs, layout):
                    lane = pl.multiple_of(half * width, 128)
                    out[pl.ds(start, rows), pl.ds(lane, width)] = piece[z, :, begin : begin + width]


def merge(where, mine, other, layout):
    rows = mine[0].shape[1]
    whole = pl.BlockSpec(memory_space=pltpu.VMEM)
    return pl.pallas_call(
        functools.partial(merge_kernel, rows, layout),
        in_specs=[pl.BlockSpec(memory_space=pltpu.SMEM)] + [whole] * 8,
        out_specs=[whole] * len(layout),
        out_shape=[jax.ShapeDtypeStruct((16 * rows, 2 * width), b16) for _, width in layout],
        compiler_params=pltpu.CompilerParams(vmem_limit_bytes=16 * MIB),
        name="merge_weights",
    )(where, *mine, *other)


def gather_plain(shard, layout):
    full = lax.all_gather(shard, "dp", axis=0, tiled=True)
    return [
        lax.all_gather(full[:, begin : begin + width], "tensor", axis=1, tiled=True)
        for begin, width in layout
    ]


def put(where_ref, rows, piece, keep, send, lane, width, owner):
    me, side = where_ref[0], where_ref[1]

    def store(out):
        for q in range(4):
            for z in range(4):
                start = pl.multiple_of((me ^ (4 * z + q)) * rows, 16)
                out[q, z * rows : (z + 1) * rows, pl.ds(lane, width)] = piece[pl.ds(start, rows), :width]

    if owner is None:
        store(keep)
        store(send)
    else:
        pl.when(side == owner)(lambda: store(keep))
        pl.when(side != owner)(lambda: store(send))


def product_sums(weight, grad):
    total = jnp.zeros((weight.shape[0], 128), f32)
    for begin in range(0, weight.shape[1], 128):
        lanes = slice(begin, begin + 128)
        total = total + weight[:, lanes].astype(f32) * grad[:, lanes]
    return total


TILE = 256


def pack_early_kernel(rows, where_ref, normed_t, cot_t, dz, mixed, w_z, keep, send, sums, piece):
    step = pl.program_id(0)
    width = piece.shape[1]

    @pl.when(step == 0)
    def _():
        sums[...] = jnp.zeros_like(sums)

    @pl.when(step < 2)
    def _():
        grad = nn(normed_t[...], dz[...])
        sums[...] += product_sums(w_z, grad)
        piece[...] = grad.astype(b16)

    @pl.when(step >= 2)
    def _():
        piece[...] = nn(cot_t[...], mixed[...]).astype(b16)

    put(where_ref, rows, piece, keep, send, pl.multiple_of((step // 2) * width, 128), width, step % 2)


def pack_early(where, normed_t, cot_t, dz, mixed, w_z):
    model, tokens = normed_t.shape
    rows = model // 16
    inner = dz.shape[1]
    half = inner // 2
    fixed = lambda shape: pl.BlockSpec(shape, lambda t: (0,) * len(shape))
    first = lambda t: (0, jnp.minimum(t, 1))
    second = lambda t: (0, jnp.maximum(t - 2, 0))
    packed = (4, 4 * rows, inner)
    return pl.pallas_call(
        functools.partial(pack_early_kernel, rows),
        grid=(4,),
        in_specs=[
            pl.BlockSpec(memory_space=pltpu.SMEM),
            fixed((model, tokens)),
            fixed((model, tokens)),
            pl.BlockSpec((tokens, half), first),
            pl.BlockSpec((tokens, half), second),
            pl.BlockSpec((model, half), first),
        ],
        out_specs=[fixed(packed), fixed(packed), fixed((model, 128))],
        out_shape=[jax.ShapeDtypeStruct(packed, b16)] * 2 + [jax.ShapeDtypeStruct((model, 128), f32)],
        scratch_shapes=[pltpu.VMEM((model, half), b16)],
        compiler_params=pltpu.CompilerParams(vmem_limit_bytes=56 * MIB),
        cost_estimate=pl.CostEstimate(flops=4 * model * tokens * inner, bytes_accessed=4 * tokens * inner, transcendentals=0),
        name="pack_early",
    )(where, normed_t, cot_t, dz, mixed, w_z)


def pack_first_kernel(rows, where_ref, normed_t, dxin, dbd, w_x, w_s, sums_in, keep, send, sums, piece):
    step = pl.program_id(0)

    @pl.when(step == 0)
    def _():
        sums[...] = sums_in[...]

    @pl.when(step < 2)
    def _():
        grad = nn(normed_t[...], dxin[...])
        sums[...] += product_sums(w_x, grad)
        piece[:, :TILE] = grad.astype(b16)
        put(where_ref, rows, piece, keep, send, 0, TILE, step)

    @pl.when(step == 2)
    def _():
        grad = nn(normed_t[...], dbd[...])
        sums[...] += product_sums(w_s, grad)
        piece[...] = grad.astype(b16)
        put(where_ref, rows, piece, keep, send, TILE, piece.shape[1], None)


def pack_first(where, normed_t, dxin, dbd, w_x, w_s, sums):
    model, tokens = normed_t.shape
    rows = model // 16
    tiles = dxin.shape[1] // TILE
    shared = dbd.shape[1]
    fixed = lambda shape: pl.BlockSpec(shape, lambda t: (0,) * len(shape))
    chosen = lambda t: (0, jnp.minimum(t, 1) * (tiles // 2))
    packed = (4, 4 * rows, TILE + shared)
    return pl.pallas_call(
        functools.partial(pack_first_kernel, rows),
        grid=(3,),
        in_specs=[
            pl.BlockSpec(memory_space=pltpu.SMEM),
            fixed((model, tokens)),
            pl.BlockSpec((tokens, TILE), chosen),
            fixed(dbd.shape),
            pl.BlockSpec((model, TILE), chosen),
            fixed(w_s.shape),
            fixed((model, 128)),
        ],
        out_specs=[fixed(packed), fixed(packed), fixed((model, 128))],
        out_shape=[jax.ShapeDtypeStruct(packed, b16)] * 2 + [jax.ShapeDtypeStruct((model, 128), f32)],
        scratch_shapes=[pltpu.VMEM((model, shared), b16)],
        compiler_params=pltpu.CompilerParams(vmem_limit_bytes=20 * MIB),
        cost_estimate=pl.CostEstimate(flops=2 * model * tokens * (2 * TILE + shared), bytes_accessed=4 * tokens * TILE, transcendentals=0),
        name="pack_first",
    )(where, normed_t, dxin, dbd, w_x, w_s, sums)


def pack_second_kernel(
    rows, each, where_ref, normed_t, dxin, w_x, sums_in, gx, gb, gh, grad_norm, gain_pre, keep, send, sums, piece, flat
):
    step = pl.program_id(0)

    @pl.when(step == 0)
    def _():
        sums[...] = sums_in[...]

    grad = nn(normed_t[...], dxin[...])
    sums[...] += product_sums(w_x, grad)
    piece[...] = grad.astype(b16)
    put(where_ref, rows, piece, keep, send, pl.multiple_of((step % each) * TILE, 128), TILE, step // each)

    @pl.when(step == 2 * each - 1)
    def _():
        model = piece.shape[0]
        width = each * TILE
        lines = gx.shape[1] // width
        flat[...] = jnp.zeros_like(flat)
        for r in range(7):
            source = gx[8 * r : 8 * r + 8, :] if r < 6 else grad_norm[...]
            line = jnp.sum(source, axis=0, keepdims=True)
            for k in range(lines):
                flat[lines * r + k : lines * r + k + 1, :] = line[:, k * width : (k + 1) * width]
        for k in range(5):
            row, lane = 7 * lines + k // 2, 2 * STATE * (k % 2)
            flat[row : row + 1, lane : lane + 2 * STATE] = jnp.sum(
                gb[8 * k : 8 * k + 8, :], axis=0, keepdims=True
            )
        row = 7 * lines + 2
        flat[row : row + 1, 256:384] = gh[0:1, :]
        flat[row : row + 1, 384:512] = gh[1:2, :]
        total = sums[...]
        high = total.astype(b16)
        low = (total - high.astype(f32)).astype(b16)
        ones = jnp.ones((8, 128), b16)
        over = (nt(ones, high) + nt(ones, low))[0:1, :] / gain_pre[...]
        flat[row + 1 : row + 2, :] = over[:, :width]
        flat[row + 2 : row + 3, : model - width] = over[:, width:]
        flat_low = flat[...].astype(b16)
        for q in range(4):
            keep[q, 4 * rows :, :] = flat_low
            send[q, 4 * rows :, :] = flat_low


def pack_second(where, normed_t, dxin, w_x, sums, gx, gb, gh, grad_norm, gain_pre):
    model, tokens = normed_t.shape
    rows = model // 16
    half = dxin.shape[1] // TILE // 2
    each = half - 1
    fixed = lambda shape: pl.BlockSpec(shape, lambda t: (0,) * len(shape))
    chosen = lambda t: (0, (t // each) * half + 1 + t % each)
    packed = (4, 4 * rows + 32, each * TILE)
    return pl.pallas_call(
        functools.partial(pack_second_kernel, rows, each),
        grid=(2 * each,),
        in_specs=[
            pl.BlockSpec(memory_space=pltpu.SMEM),
            fixed((model, tokens)),
            pl.BlockSpec((tokens, TILE), chosen),
            pl.BlockSpec((model, TILE), chosen),
            fixed((model, 128)),
            fixed(gx.shape),
            fixed(gb.shape),
            fixed(gh.shape),
            fixed(grad_norm.shape),
            fixed(gain_pre.shape),
        ],
        out_specs=[fixed(packed), fixed(packed)],
        out_shape=[jax.ShapeDtypeStruct(packed, b16)] * 2,
        scratch_shapes=[
            pltpu.VMEM((model, 128), f32),
            pltpu.VMEM((model, TILE), b16),
            pltpu.VMEM((32, each * TILE), f32),
        ],
        compiler_params=pltpu.CompilerParams(vmem_limit_bytes=20 * MIB),
        cost_estimate=pl.CostEstimate(flops=4 * model * tokens * each * TILE, bytes_accessed=4 * tokens * each * TILE, transcendentals=0),
        name="pack_second",
    )(where, normed_t, dxin, w_x, sums, gx, gb, gh, grad_norm, gain_pre)


def finish_kernel(half, side_ref, *refs):
    early, first, second, pick = refs[:4], refs[4:8], refs[8:12], refs[12]
    (z_out, bc_out, dt_out, cx_out, cb_out, alog_out, bias_out, skip_out, norm_out, pre_out, w_out, lines) = refs[13:]
    side = side_ref[1]
    rows = early[0].shape[0]

    def total(parts):
        value = parts[0][...].astype(f32)
        for k in range(1, 4):
            value = value + parts[k][...].astype(f32)
        return value

    one, two, three = total(early), total(first), total(second)
    width = three.shape[1]
    z_out[:, 0, :] = one[:, :half]
    z_out[:, 1, :TILE] = two[:, :TILE]
    z_out[:, 1, TILE:] = three[:rows]
    w_out[...] = one[:, half:]
    bc_out[...] = two[:, TILE : TILE + 2 * STATE]
    heads = half // HEAD

    def own(value):
        return jnp.where(side == 0, value[:, :heads], value[:, heads : 2 * heads])

    dt_out[...] = own(two[:, TILE + 2 * STATE :]).T
    flat = three[rows:]
    count = 2 * half // width
    for r in range(7):
        for k in range(count):
            lines[r : r + 1, k * width : (k + 1) * width] = flat[count * r + k : count * r + k + 1, :]
    mine = lines[:, pl.ds(pl.multiple_of(side * half, 128), half)]
    cx_out[...] = mine[:5]
    high = mine[5:6].astype(b16)
    low = (mine[5:6] - high.astype(f32)).astype(b16)
    pair = jnp.concatenate([jnp.broadcast_to(high, (8, half)), jnp.broadcast_to(low, (8, half))], axis=0)
    sums = nn(pair, pick[...])
    skip_out[...] = (sums[0:1] + sums[8:9])[:, :heads]
    norm_out[...] = mine[6]
    row = 7 * count
    for k in range(5):
        lane = 2 * STATE * (k % 2)
        cb_out[k : k + 1, :] = flat[row + k // 2 : row + k // 2 + 1, lane : lane + 2 * STATE]
    alog_out[...] = own(flat[row + 2 : row + 3, 256:384])
    bias_out[...] = own(flat[row + 2 : row + 3, 384:512])
    model = pre_out.shape[0]
    pre_out[...] = jnp.concatenate([flat[row + 3], flat[row + 4, : model - width]])


def finish(where, early, first, second, pick, model, half):
    rows = early[0].shape[0]
    heads = half // HEAD
    whole = pl.BlockSpec(memory_space=pltpu.VMEM)
    shapes = [
        (rows, 2, half), (rows, 2 * STATE), (heads, rows), (5, half), (5, 2 * STATE),
        (1, heads), (1, heads), (1, heads), (half,), (model,), (rows, half),
    ]
    return pl.pallas_call(
        functools.partial(finish_kernel, half),
        in_specs=[pl.BlockSpec(memory_space=pltpu.SMEM)] + [whole] * 13,
        out_specs=[whole] * len(shapes),
        out_shape=[jax.ShapeDtypeStruct(shape, f32) for shape in shapes],
        scratch_shapes=[pltpu.VMEM((8, 2 * half), f32)],
        compiler_params=pltpu.CompilerParams(vmem_limit_bytes=16 * MIB),
        name="finish",
    )(where, *early, *first, *second, pick)


def sum_tensor(keep, send):
    got = swap(send, 1, "tensor")
    return (keep.astype(f32) + got.astype(f32)).astype(b16)


def sum_around(parts, rows):
    total = parts[0].astype(f32)
    for value in [swap(parts[q], q) for q in (1, 2, 3)]:
        total = total + value.astype(f32)
    split = total[: 4 * rows].reshape(4, rows, total.shape[1])
    if total.shape[0] > 4 * rows:
        shared = jnp.broadcast_to(total[None, 4 * rows :], (4, *total[4 * rows :].shape))
        split = jnp.concatenate([split, shared], axis=1)
    return split.astype(b16)


def along_z_parts(parts):
    return [parts[0]] + [swap(parts[z], z << 2) for z in (1, 2, 3)]


def scatter_plain(arrays, parts):
    halves = []
    for which, base, width, shared in parts:
        array = arrays[which][:, base : base + (width if shared else 2 * width)]
        if shared:
            array = lax.psum(array, "tensor")
        else:
            array = lax.psum_scatter(array, "tensor", scatter_dimension=1, tiled=True)
        halves.append(array)
    return lax.psum_scatter(
        jnp.concatenate(halves, axis=1).astype(f32), "dp", scatter_dimension=0, tiled=True
    )


def prepare_kernel(tokens, cot, gain, x_out, cot_out, normed_out, normed_t, cot_t):
    order = jnp.where(iota(1) == token(iota(0)), 1.0, 0.0).astype(b16)
    x = nn(order, tokens[...])
    x_out[...] = x.astype(b16)
    moved = nn(order, cot[...])
    cot_out[...] = moved.astype(b16)
    cot_t[...] = moved.T.astype(b16)
    normed = x * lax.rsqrt(jnp.mean(x * x, axis=1, keepdims=True) + epsilon) * gain[...]
    normed_out[...] = normed.astype(b16)
    normed_t[...] = normed.T.astype(b16)


def prepare(tokens, cot, gain):
    rows, model = tokens.shape
    tall = pl.BlockSpec((Q, model), lambda k: (k, 0))
    flat = pl.BlockSpec((model, Q), lambda k: (0, k))
    return pl.pallas_call(
        prepare_kernel,
        grid=(rows // Q,),
        in_specs=[tall, tall, pl.BlockSpec((1, model), lambda k: (0, 0))],
        out_specs=[tall, tall, tall, flat, flat],
        out_shape=[jax.ShapeDtypeStruct((rows, model), b16)] * 3 + [jax.ShapeDtypeStruct((model, rows), b16)] * 2,
        compiler_params=pltpu.CompilerParams(vmem_limit_bytes=56 * MIB),
        name="prepare",
    )(tokens, cot, gain)


def restore(value, out):
    order = jnp.where(iota(0) == token(iota(1)), 1.0, 0.0).astype(b16)
    value = value.astype(b16)
    for begin in range(0, value.shape[0], Q):
        out[begin : begin + Q, :] = nn(order, value[begin : begin + Q]).astype(b16)


def token_grads_kernel(dz, dxin, dbd, x, cot, w_z, w_x, w_s, gain, out):
    dn = nt(dz[...], w_z[...]) + nt(dxin[...], w_x[...]) + nt(dbd[...], w_s[...])
    dn = dn * gain[...]
    value = x[...].astype(f32)
    scale = lax.rsqrt(jnp.mean(value * value, axis=1, keepdims=True) + epsilon)
    inner = jnp.mean(dn * value, axis=1, keepdims=True)
    grad = cot[...].astype(f32) + scale * dn - value * (scale * scale * scale * inner)
    restore(grad, out)


def token_grads(dz, dxin, dbd, x, cot, w_z, w_x, w_s, gain):
    rows, model = x.shape
    tall = lambda value: pl.BlockSpec((256, value.shape[1]), lambda k: (k, 0))
    fixed = lambda value: pl.BlockSpec(value.shape, lambda k: (0, 0))
    return pl.pallas_call(
        token_grads_kernel,
        grid=(rows // 256,),
        in_specs=[tall(v) for v in (dz, dxin, dbd, x, cot)] + [fixed(v) for v in (w_z, w_x, w_s, gain)],
        out_specs=tall(x),
        out_shape=jax.ShapeDtypeStruct(x.shape, b16),
        compiler_params=pltpu.CompilerParams(vmem_limit_bytes=32 * MIB),
        cost_estimate=pl.CostEstimate(flops=rows * model * 8000, bytes_accessed=rows * model * 20, transcendentals=0),
        name="token_grads",
    )(dz, dxin, dbd, x, cot, w_z, w_x, w_s, gain)


def add_branch_kernel(mixed, x, w_out_t, out):
    restore(x[...].astype(f32) + nt(mixed[...], w_out_t[...]), out)


def add_branch(mixed, x, w_out_t):
    rows, model = x.shape
    tall = lambda value: pl.BlockSpec((256, value.shape[1]), lambda k: (k, 0))
    return pl.pallas_call(
        add_branch_kernel,
        grid=(rows // 256,),
        in_specs=[tall(mixed), tall(x), pl.BlockSpec(w_out_t.shape, lambda k: (0, 0))],
        out_specs=tall(x),
        out_shape=jax.ShapeDtypeStruct(x.shape, b16),
        compiler_params=pltpu.CompilerParams(vmem_limit_bytes=24 * MIB),
        cost_estimate=pl.CostEstimate(flops=rows * model * 4000, bytes_accessed=rows * model * 10, transcendentals=0),
        name="add_branch",
    )(mixed, x, w_out_t)


def both_sides(value, side, axis):
    other = swap(value, 1, "tensor")
    return jnp.where(
        side == 0, jnp.concatenate([value, other], axis), jnp.concatenate([other, value], axis)
    )


def body(
    tokens, pre_gain, w_zx, w_bc, w_dt, conv_x, conv_bc, a_log, dt_bias, skip_gain, norm_gain, w_out, cotangent,
):
    side = lax.axis_index("tensor")
    where = jnp.stack([lax.axis_index("dp"), side]).astype(jnp.int32)
    model, half = tokens.shape[1], conv_x.shape[1]
    inner = 2 * half
    half_heads = a_log.shape[0]
    heads_count = 2 * half_heads
    shard_rows = w_zx.shape[0]

    dt_pad = lax.dynamic_update_slice(
        jnp.zeros((shard_rows, 128), b16), w_dt, (0, side * half_heads)
    )
    bc_half = lax.dynamic_slice(w_bc, (0, side * STATE), (shard_rows, STATE))
    quick = fast(shard_rows)
    first = jnp.concatenate([w_zx[:, 1], bc_half, dt_pad], axis=1)
    second = jnp.concatenate([w_zx[:, 0], w_out.T], axis=1)
    first_layout = ((0, half), (half, STATE), (half + STATE, 128))
    second_layout = ((0, half), (half, half))
    gain_row = pre_gain.astype(f32)[None]
    if quick:
        column = along_z(first)
        tokens, cotangent, _ = lax.optimization_barrier((tokens, cotangent, column))
    ready = prepare(tokens, cotangent, gain_row)
    if quick:
        mine_first = around(column)
        later = along_z(tie(second, column))
        mine_first[3], *ready = lax.optimization_barrier((mine_first[3], *ready))
        other_first = [swap(part, 1, "tensor") for part in mine_first]
        mine_second = around(tie(later, *mine_first))
        w_x, full_bc, full_dt = merge(where, mine_first, other_first, first_layout)
    else:
        w_x, full_bc, full_dt = gather_plain(first, first_layout)
        w_z, w_out_t = gather_plain(second, second_layout)
    small = jnp.concatenate(
        [
            conv_x.astype(f32),
            norm_gain.astype(f32)[None],
            jnp.pad(jnp.concatenate([a_log, dt_bias, skip_gain]), (0, half - 3 * half_heads))[None],
            jnp.zeros((1, half), f32),
        ],
        axis=0,
    )
    small = both_sides(small[None], side, 0)
    wide = jnp.concatenate([small[0, :6], small[1, :6]], axis=1)
    gain_norm = wide[5:6]
    per_head = small[:, 6, : 3 * half_heads].reshape(2, 3, half_heads).transpose(1, 0, 2)
    per_head = per_head.reshape(3, heads_count)
    cx = jnp.concatenate(
        [wide[:5], jnp.repeat(per_head[2], HEAD)[None], jnp.zeros((2, inner), f32)], axis=0
    )
    cb = jnp.pad(conv_bc.astype(f32), ((0, 3), (0, 0)))
    heads = jnp.pad(
        jnp.stack([per_head[1], jnp.exp(per_head[0])]), ((0, 6), (0, Q - heads_count))
    )
    pick = (jnp.arange(inner)[:, None] // HEAD == jnp.arange(Q)[None, :]).astype(b16)

    w_s = jnp.concatenate([full_bc, full_dt[:, :128] + full_dt[:, 128:]], axis=1)
    x, cotangent, normed, normed_t, cot_t = ready
    xin = nn(normed, w_x).astype(b16)
    bd = nn(normed, w_s)
    blocks = tokens.shape[0] // Q
    started = list(scan_forward(xin, bd, cx, cb, heads, 0, blocks // 2, None))
    if quick:
        started[4], *mine_second = lax.optimization_barrier((started[4], *mine_second))
        other_second = [swap(part, 1, "tensor") for part in mine_second]
    ssd, held, pre, rates, ended = scan_forward(
        xin, bd, cx, cb, heads, blocks // 2, blocks - blocks // 2, started
    )
    if quick:
        other_second = lax.optimization_barrier((ended, *other_second))[1:]
        w_z, w_out_t = merge(where, mine_second, other_second, second_layout)
    mixed, dz, dssd, grad_norm = gate_both(ssd, normed, cotangent, w_z, w_out_t, gain_norm)
    scan = lambda base, count, before: list(
        scan_backward(dssd, xin, pre, bd, held, rates, cx, cb, heads, pick, base, count, before)
    )
    if quick:
        keep, send, sums = pack_early(where, normed_t, cot_t, dz, mixed, w_z)
        dssd, keep, send = lax.optimization_barrier((dssd, keep, send))
        parts = sum_tensor(keep, send)
        carry = scan(blocks * 7 // 8, blocks // 8, None)
        carry[2], parts = lax.optimization_barrier((carry[2], parts))
        parts = sum_around(parts, shard_rows)
        carry = scan(blocks // 4, blocks * 5 // 8, carry)
        carry[2], parts = lax.optimization_barrier((carry[2], parts))
        early = along_z_parts(parts)
        carry = scan(0, blocks // 4, carry)
        carry[0], carry[1], *early = lax.optimization_barrier((carry[0], carry[1], *early))
    else:
        early = scatter_plain(
            [nn(normed_t, dz).astype(b16), nn(cot_t, mixed).astype(b16)],
            ((0, 0, half, False), (1, 0, half, False)),
        )
        carry = scan(0, blocks, None)
    dxin, dbd, _, _, _, gx, gb, gh = carry
    if quick:
        keep, send, sums = pack_first(where, normed_t, dxin, dbd, w_x, w_s, sums)
        sums, keep, send = lax.optimization_barrier((sums, keep, send))
        parts_first = sum_tensor(keep, send)
        keep, send = pack_second(where, normed_t, dxin, w_x, sums, gx, gb, gh, grad_norm, gain_row)
        dxin, dz, mixed, keep, send, parts_first = lax.optimization_barrier(
            (dxin, dz, mixed, keep, send, parts_first)
        )
        parts_second = sum_tensor(keep, send)
        parts_first = sum_around(parts_first, shard_rows)
    grad_tokens = token_grads(dz, dxin, dbd, x, cotangent, w_z, w_x, w_s, gain_row)
    if quick:
        grad_tokens, mixed, parts_first, parts_second = lax.optimization_barrier(
            (grad_tokens, mixed, parts_first, parts_second)
        )
        second = sum_around(parts_second, shard_rows)
        first = along_z_parts(parts_first)
    out = add_branch(mixed, x, w_out_t)
    if quick:
        out, second, *first = lax.optimization_barrier((out, second, *first))
        second = along_z_parts(second)
        z_out, bc_out, dt_out, cx_out, cb_out, alog, bias, skip, norm, pre_sum, w_out_grad = finish(
            where, early, first, second, pick[:half], model, half
        )
        return (
            out, grad_tokens, pre_sum, z_out, bc_out, dt_out.T,
            cx_out, cb_out, alog[0], bias[0], skip[0], norm, w_out_grad.T,
        )
    late = scatter_plain(
        [nn(normed_t, dxin).astype(b16), nn(normed_t, dbd).astype(b16)],
        ((0, 0, half, False), (1, 0, 2 * STATE + 128, True)),
    )
    dnormed = nt(dz, w_z) + nt(dxin, w_x) + nt(dbd, w_s)
    wide_x = x.astype(f32)
    scale = lax.rsqrt(jnp.mean(wide_x * wide_x, axis=1, keepdims=True) + epsilon)
    grad_pre = jnp.sum(dnormed * wide_x * scale, axis=0)
    lines = jnp.sum(gx.reshape(6, 8, inner), axis=1)
    lines, norm, convbc, rates, grad_pre = lax.psum(
        (lines, jnp.sum(grad_norm, axis=0), jnp.sum(gb.reshape(5, 8, 2 * STATE), axis=1), gh[:2], grad_pre), ("dp", "tensor")
    )

    def mine(vector, width):
        return lax.dynamic_slice_in_dim(vector, side * width, width, vector.ndim - 1)

    skip = jnp.sum(lines[5].reshape(heads_count, HEAD), axis=1)
    return (
        out,
        grad_tokens,
        grad_pre,
        jnp.stack([early[:, :half], late[:, :half]], axis=1),
        late[:, half : half + 2 * STATE],
        mine(late[:, half + 2 * STATE :], half_heads),
        mine(lines[:5], half),
        convbc,
        mine(rates[0], half_heads),
        mine(rates[1], half_heads),
        mine(skip, half_heads),
        mine(norm, half),
        early[:, half:].T,
    )


def solution(mesh):
    placed = (
        P(("dp", "tensor"), None),
        P(),
        P("dp", None, "tensor"),
        P("dp", None),
        P("dp", "tensor"),
        P(None, "tensor"),
        P(),
        P("tensor"),
        P("tensor"),
        P("tensor"),
        P("tensor"),
        P("tensor", "dp"),
        P(("dp", "tensor"), None),
    )
    return jax.shard_map(
        body,
        mesh=mesh,
        in_specs=placed,
        out_specs=(
            P(("dp", "tensor"), None),
            P(("dp", "tensor"), None),
            P(),
            P("dp", None, "tensor"),
            P("dp", None),
            P("dp", "tensor"),
            P(None, "tensor"),
            P(),
            P("tensor"),
            P("tensor"),
            P("tensor"),
            P("tensor"),
            P("tensor", "dp"),
        ),
        check_vma=False,
    )
```

profile of v0, /device:TPU:0, one launch (start us, length us, event | category | flops | bytes accessed | tf_op | source)
XLA Modules:
  0.0 221.9 jit_solution(12684864168070646292)
XLA Ops:
  1.5 1.2 fusion.15
  3.0 3.1 %collective-permute-start = (bf16[48,1024]{1,0:T(8,128)(2,1)S(1)}, bf16[48,1024]{1,0:T(8,128)(2,1)S(1)}, u32[]{:S(2)}, u32[]{:S(2)}) collective-permute-start(bf16[48,1024]{1,0:T(8,128)(2,1)S(1)} %get-tuple-element.268), channel_id=1, source_target_pairs={{0,8},{2,10},{4,12},{6,14},{8,0},{10,2},{12,4},{14,6},{16,24},{18,... | collective-permute-start | bytes 294920 | tf_op jit(solution)/shard_map/ppermute | solution.py:444
  6.1 2.6 %collective-permute-start.1 = (bf16[48,1024]{1,0:T(8,128)(2,1)S(1)}, bf16[48,1024]{1,0:T(8,128)(2,1)S(1)}, u32[]{:S(2)}, u32[]{:S(2)}) collective-permute-start(bf16[48,1024]{1,0:T(8,128)(2,1)S(1)} %get-tuple-element.268), channel_id=1, source_target_pairs={{0,16},{2,18},{4,20},{6,22},{8,24},{10,26},{12,28},{14,30},{16,0},... | collective-permute-start | bytes 294920 | tf_op jit(solution)/shard_map/ppermute | solution.py:444
  11.0 1.3 pad_convert_fusion.refs_5_.refs_8_
  13.3 1.3 reshape.96.gain.gain_pre
  16.7 2.5 %collective-permute-start.3 = (bf16[4,48,1024]{2,1,0:T(8,128)(2,1)S(1)}, bf16[4,48,1024]{2,1,0:T(8,128)(2,1)S(1)}, u32[]{:S(2)}, u32[]{:S(2)}) collective-permute-start(bf16[4,48,1024]{2,1,0:T(8,128)(2,1)S(1)} %pad_maximum_fusion.2.refs_0_), channel_id=1, source_target_pairs={{0,6},{2,4},{4,2},{6,0},{8,14},{10,12},{12,10},{14,8},{16,22},{18,... | collective-permute-start | bytes 1179656 | tf_op jit(solution)/shard_map/ppermute | solution.py:444
  20.3 1.6 collective-permute-start.11
  21.9 2.2 collective-permute-start.12
  24.1 8.2 %prepare.1 = (bf16[1024,768]{1,0:T(8,128)(2,1)}, bf16[1024,768]{1,0:T(8,128)(2,1)}, bf16[1024,768]{1,0:T(8,128)(2,1)}, bf16[768,1024]{1,0:T(8,128)(2,1)}, bf16[768,1024]{1,0:T(8,128)(2,1)}) custom-call(bf16[1024,768]{1,0:T(8,128)(2,1)} %tokens, bf16[1024,768]{1,0:T(8,128)(2,1)} %cot, f32[1,768]{1,0:T(1,128)} %reshape.96.gain.gain_pre), custom_call_target="tpu_custom_call" | custom-call | tf_op jit(solution)/shard_map/prepare/pallas_call | solution.py:824
  33.2 4.2 %collective-permute-done.4.refs_1_ = bf16[4,48,1024]{2,1,0:T(8,128)(2,1)S(1)} collective-permute-done((bf16[4,48,1024]{2,1,0:T(8,128)(2,1)S(1)}, bf16[4,48,1024]{2,1,0:T(8,128)(2,1)S(1)}, u32[]{:S(2)}, u32[]{:S(2)}) %collective-permute-start.4) | collective-permute-done | bytes 393248 | tf_op jit(solution)/shard_map/ppermute | solution.py:444
  41.8 1.6 collective-permute-start.14
  43.3 1.5 collective-permute-start.15
  48.5 4.0 %convolution_convert_fusion.refs_0_.refs_1_ = bf16[1024,1536]{1,0:T(8,128)(2,1)} fusion(bf16[1024,768]{1,0:T(8,128)(2,1)S(1)} %copy-done.27, bf16[768,1536]{1,0:T(8,128)(2,1)S(1)} %get-tuple-element.136.w_x), kind=kOutput, calls=%fused_computation.1 | convolution fusion | flops 2417491968 | bytes 7077888 | tf_op jit(solution)/shard_map/dot_general | solution.py:22
  52.5 2.2 fusion.14.refs_2_.refs_3_.refs_4_
  54.6 9.6 %scan_forward.2 = (bf16[1024,1536]{1,0:T(8,128)(2,1)}, bf16[8,128,1536]{2,1,0:T(8,128)(2,1)}, bf16[1024,1536]{1,0:T(8,128)(2,1)}, f32[1024,256]{1,0:T(8,128)}, f32[128,1536]{1,0:T(8,128)}) custom-call(bf16[1024,1536]{1,0:T(8,128)(2,1)} %convolution_convert_fusion.refs_0_.refs_1_, bf16[1024,1536]{1,0:T(8,128)(2,1)} %convolution_convert_fusion.refs_0_.refs_1_, ...), custom_call_target="tpu_custom_call" | custom-call | flops 4718592000 | bytes 6291456 | tf_op jit(solution)/shard_map/scan_forward/pallas_call | solution.py:162
  64.3 6.2 %collective-permute-done.15.refs_2_ = bf16[4,48,1536]{2,1,0:T(8,128)(2,1)S(1)} collective-permute-done((bf16[4,48,1536]{2,1,0:T(8,128)(2,1)S(1)}, bf16[4,48,1536]{2,1,0:T(8,128)(2,1)S(1)}, u32[]{:S(2)}, u32[]{:S(2)}) %collective-permute-start.15) | collective-permute-done | bytes 589856 | tf_op jit(solution)/shard_map/ppermute | solution.py:444
  72.1 9.9 %scan_forward.3 = (bf16[1024,1536]{1,0:T(8,128)(2,1)}, bf16[8,128,1536]{2,1,0:T(8,128)(2,1)}, bf16[1024,1536]{1,0:T(8,128)(2,1)}, f32[1024,256]{1,0:T(8,128)}, f32[128,1536]{1,0:T(8,128)}) custom-call(bf16[1024,1536]{1,0:T(8,128)(2,1)} %convolution_convert_fusion.refs_0_.refs_1_, ...), custom_call_target="tpu_custom_call", output_to_operand_aliasing={{0}: (8, {}), {1}: (9, {}), {2}: (10, {}), {3}: (11, {})} | custom-call | flops 4718592000 | bytes 6291456 | tf_op jit(solution)/shard_map/scan_forward/pallas_call | solution.py:162
  83.0 1.5 copy-done.17
  84.5 1.4 copy-done.19
  85.9 12.8 %gate_both.1 = (bf16[1024,1536]{1,0:T(8,128)(2,1)}, bf16[1024,1536]{1,0:T(8,128)(2,1)}, bf16[1024,1536]{1,0:T(8,128)(2,1)}, f32[8,1536]{1,0:T(8,128)}) custom-call(bf16[1024,1536]{1,0:T(8,128)(2,1)} %get-tuple-element.147.y, bf16[1024,768]{1,0:T(8,128)(2,1)} %get-tuple-element.134.normed, bf16[1024,768]{1,0:T(8,128)(2,1)} %get-tuple-element.148.cot, ...), custom_call_target="tpu_custom_call" | custom-call | flops 12582912000 | bytes 15728640 | tf_op jit(solution)/shard_map/gate_both/pallas_call | solution.py:429
  98.7 11.9 %pack_early.1 = (bf16[4,192,1536]{2,1,0:T(8,128)(2,1)}, bf16[4,192,1536]{2,1,0:T(8,128)(2,1)}, f32[768,128]{1,0:T(8,128)}) custom-call(s32[2]{0:T(128)} %copy-done.14, bf16[768,1024]{1,0:T(8,128)(2,1)} %get-tuple-element.160.normed_t, bf16[768,1024]{1,0:T(8,128)(2,1)} %get-tuple-element.161.cot_t, bf16[1024,1536]{1,0:T(8,128)(2,1)} %get-tuple-element.209.dz, ...), custom_call_target="tpu_custom_call" | custom-call | flops 4831838208 | bytes 6291456 | tf_op jit(solution)/shard_map/pack_early/pallas_call | solution.py:554
  111.7 6.3 %scan_backward.3 = (bf16[1024,1536]{1,0:T(8,128)(2,1)}, bf16[1024,384]{1,0:T(8,128)(2,1)}, f32[128,1536]{1,0:T(8,128)}, f32[24,1536]{1,0:T(8,128)}, f32[24,256]{...) custom-call(bf16[1024,1536]{1,0:T(8,128)(2,1)} %get-tuple-element.166.refs_0_, ...), custom_call_target="tpu_custom_call" | custom-call | flops 2359296000 | bytes 1966080 | tf_op jit(solution)/shard_map/scan_backward/pallas_call | solution.py:344
  118.0 3.0 %add_convert_fusion = bf16[4,192,1536]{2,1,0:T(8,128)(2,1)S(1)} fusion(bf16[4,192,1536]{2,1,0:T(8,128)(2,1)} %collective-permute-done.21, bf16[4,192,1536]{2,1,0:T(8,128)(2,1)} %get-tuple-element.171), kind=kLoop, calls=%fused_computation | loop fusion | flops 4718592 | bytes 7077888 | tf_op jit(solution)/shard_map/convert_element_type | solution.py:776
  121.1 1.3 collective-permute-start.22
  123.3 1.4 collective-permute-start.24
  124.7 22.3 %scan_backward.4 = (bf16[1024,1536]{1,0:T(8,128)(2,1)}, bf16[1024,384]{1,0:T(8,128)(2,1)}, f32[128,1536]{1,0:T(8,128)}, f32[24,1536]{1,0:T(8,128)}, f32[24,256]{...) custom-call(bf16[1024,1536]{1,0:T(8,128)(2,1)} %get-tuple-element.16, ...), custom_call_target="tpu_custom_call", output_to_operand_aliasing={{0}: (17, {}), {1}: (18, {})} | custom-call | flops 11796480000 | bytes 9830400 | tf_op jit(solution)/shard_map/scan_backward/pallas_call | solution.py:344
  147.0 1.9 collective-permute-done.23
  148.9 1.7 collective-permute-done.24
  150.7 1.5 fusion.2
  152.2 2.2 collective-permute-start.25
  154.4 1.7 collective-permute-start.26
  156.9 11.0 %scan_backward.5 = (bf16[1024,1536]{1,0:T(8,128)(2,1)}, bf16[1024,384]{1,0:T(8,128)(2,1)}, f32[128,1536]{1,0:T(8,128)}, f32[24,1536]{1,0:T(8,128)}, f32[24,256]{...) custom-call(bf16[1024,1536]{1,0:T(8,128)(2,1)} %get-tuple-element.16, ...), custom_call_target="tpu_custom_call", output_to_operand_aliasing={{0}: (17, {}), {1}: (18, {})} | custom-call | flops 4718592000 | bytes 3932160 | tf_op jit(solution)/shard_map/scan_backward/pallas_call | solution.py:344
  168.1 1.9 copy-done.2
  171.1 3.1 %pack_first.1 = (bf16[4,192,640]{2,1,0:T(8,128)(2,1)S(1)}, bf16[4,192,640]{2,1,0:T(8,128)(2,1)S(1)}, f32[768,128]{1,0:T(8,128)S(1)}) custom-call(s32[2]{0:T(128)S(1)} %copy-done.15, bf16[768,1024]{1,0:T(8,128)(2,1)S(1)} %copy-done.4, bf16[1024,1536]{1,0:T(8,128)(2,1)S(1)} %copy-done.2, bf16[1024,384]{1,0:T(8,128)(2,1)S(1)} %copy-done.5, ...), custom_call_target="tpu_custom_call" | custom-call | flops 1409286144 | bytes 1048576 | tf_op jit(solution)/shard_map/pack_first/pallas_call | solution.py:604
  174.4 3.7 %pack_second.1 = (bf16[4,224,512]{2,1,0:T(8,128)(2,1)S(1)}, bf16[4,224,512]{2,1,0:T(8,128)(2,1)S(1)}) custom-call(s32[2]{0:T(128)S(1)} %copy-done.15, bf16[768,1024]{1,0:T(8,128)(2,1)S(1)} %copy-done.4, bf16[1024,1536]{1,0:T(8,128)(2,1)S(1)} %copy-done.3, bf16[768,1536]{1,0:T(8,128)(2,1)S(1)} %get-tuple-element.136.w_x, ...), custom_call_target="tpu_custom_call" | custom-call | flops 1610612736 | bytes 2097152 | tf_op jit(solution)/shard_map/pack_second/pallas_call | solution.py:679
  179.7 1.5 collective-permute-start.30
  181.2 1.3 collective-permute-start.31
  182.5 9.3 %token_grads.1 = bf16[1024,768]{1,0:T(8,128)(2,1)} custom-call(bf16[1024,1536]{1,0:T(8,128)(2,1)S(1)} %copy-done.24, bf16[1024,1536]{1,0:T(8,128)(2,1)S(1)} %copy-done.3, bf16[1024,384]{1,0:T(8,128)(2,1)S(1)} %copy-done.6, bf16[1024,768]{1,0:T(8,128)(2,1)S(1)} %copy-done.21, bf16[1024,768]{1,0:T(8,128)(2,1)S(1)} %copy-done.22, ...), custom_call_target="tpu_custom_call" | custom-call | flops 6291456000 | bytes 15728640 | tf_op jit(solution)/shard_map/token_grads/pallas_call | solution.py:856
  193.1 1.4 collective-permute-start.33
  195.2 1.4 collective-permute-start.35
  196.7 2.5 %collective-permute-start.36 = (bf16[48,640]{1,0:T(8,128)(2,1)S(1)}, bf16[48,640]{1,0:T(8,128)(2,1)S(1)}, u32[]{:S(2)}, u32[]{:S(2)}) collective-permute-start(bf16[48,640]{1,0:T(8,128)(2,1)S(1)} %get-tuple-element.263), channel_id=1, source_target_pairs={{0,8},{2,10},{4,12},{6,14},{8,0},{10,2},{12,4},{14,6},{16,24},{18,... | collective-permute-start | bytes 184328 | tf_op jit(solution)/shard_map/ppermute | solution.py:444
  199.2 1.3 collective-permute-start.37
  200.5 5.4 %add_branch.1 = bf16[1024,768]{1,0:T(8,128)(2,1)} custom-call(bf16[1024,1536]{1,0:T(8,128)(2,1)S(1)} %copy-done.23, bf16[1024,768]{1,0:T(8,128)(2,1)S(1)} %copy-done.21, bf16[768,1536]{1,0:T(8,128)(2,1)S(1)} %copy-done.18), custom_call_target="tpu_custom_call" | custom-call | flops 3145728000 | bytes 7864320 | tf_op jit(solution)/shard_map/add_branch/pallas_call | solution.py:875
  207.3 5.0 %collective-permute-done.38.refs_7_ = bf16[48,640]{1,0:T(8,128)(2,1)S(1)} collective-permute-done((bf16[48,640]{1,0:T(8,128)(2,1)S(1)}, bf16[48,640]{1,0:T(8,128)(2,1)S(1)}, u32[]{:S(2)}, u32[]{:S(2)}) %collective-permute-start.38) | collective-permute-done | bytes 61472 | tf_op jit(solution)/shard_map/ppermute | solution.py:444
  212.3 1.5 collective-permute-start.40
  213.9 2.8 %collective-permute-start.41 = (bf16[80,512]{1,0:T(8,128)(2,1)S(1)}, bf16[80,512]{1,0:T(8,128)(2,1)S(1)}, u32[]{:S(2)}, u32[]{:S(2)}) collective-permute-start(bf16[80,512]{1,0:T(8,128)(2,1)S(1)} %get-tuple-element.257), channel_id=1, source_target_pairs={{0,24},{2,26},{4,28},{6,30},{8,16},{10,18},{12,20},{14,22},{16,8},... | collective-permute-start | bytes 245768 | tf_op jit(solution)/shard_map/ppermute | solution.py:444
  217.7 2.4 %collective-permute-done.41.refs_11_ = bf16[80,512]{1,0:T(8,128)(2,1)S(1)} collective-permute-done((bf16[80,512]{1,0:T(8,128)(2,1)S(1)}, bf16[80,512]{1,0:T(8,128)(2,1)S(1)}, u32[]{:S(2)}, u32[]{:S(2)}) %collective-permute-start.41) | collective-permute-done | bytes 81952 | tf_op jit(solution)/shard_map/ppermute | solution.py:444
  220.2 1.6 finish.1
  (166 shorter events, 29.2 us)
Async XLA Ops:
  3.0 13.1 %collective-permute-start = (bf16[48,1024]{1,0:T(8,128)(2,1)S(1)}, bf16[48,1024]{1,0:T(8,128)(2,1)S(1)}, u32[]{:S(2)}, u32[]{:S(2)}) collective-permute-start(bf16[48,1024]{1,0:T(8,128)(2,1)S(1)} %get-tuple-element.268), channel_id=1, source_target_pairs={{0,8},{2,10},{4,12},{6,14},{8,0},{10,2},{12,4},{14,6},{16,24},{18,... | collective-permute-start | bytes 294920 | tf_op jit(solution)/shard_map/ppermute | solution.py:444
  6.1 10.6 %collective-permute-start.1 = (bf16[48,1024]{1,0:T(8,128)(2,1)S(1)}, bf16[48,1024]{1,0:T(8,128)(2,1)S(1)}, u32[]{:S(2)}, u32[]{:S(2)}) collective-permute-start(bf16[48,1024]{1,0:T(8,128)(2,1)S(1)} %get-tuple-element.268), channel_id=1, source_target_pairs={{0,16},{2,18},{4,20},{6,22},{8,24},{10,26},{12,28},{14,30},{16,0},... | collective-permute-start | bytes 294920 | tf_op jit(solution)/shard_map/ppermute | solution.py:444
  8.6 8.0 %collective-permute-start.2 = (bf16[48,1024]{1,0:T(8,128)(2,1)S(1)}, bf16[48,1024]{1,0:T(8,128)(2,1)S(1)}, u32[]{:S(2)}, u32[]{:S(2)}) collective-permute-start(bf16[48,1024]{1,0:T(8,128)(2,1)S(1)} %get-tuple-element.268), channel_id=1, source_target_pairs={{0,24},{2,26},{4,28},{6,30},{8,16},{10,18},{12,20},{14,22},{16,8},... | collective-permute-start | bytes 294920 | tf_op jit(solution)/shard_map/ppermute | solution.py:444
  11.0 4.2 %collective-permute-start.10 = (f32[1,8,768]{2,1,0:T(8,128)S(1)}, f32[1,8,768]{2,1,0:T(8,128)S(1)}, u32[]{:S(2)}, u32[]{:S(2)}) collective-permute-start(f32[1,8,768]{2,1,0:T(8,128)S(1)} %maximum_bitcast_fusion), channel_id=1, source_target_pairs={{0,1},{1,0},{2,3},{3,2},{4,5},{5,4},{6,7},{7,6},{8,9},{9,8},{10,11... | collective-permute-start | bytes 73736 | tf_op jit(solution)/shard_map/ppermute | solution.py:444
  13.3 68.8 %copy-start.14 = (s32[2]{0:T(128)}, s32[2]{0:T(128)S(1)}, u32[]{:S(2)}) copy-start(s32[2]{0:T(128)S(1)} %pad_add_fusion.where_ref.side_ref) | copy-start | bytes 28
  16.7 21.2 %copy-start.26 = (f32[8]{0:T(128)S(1)}, f32[8]{0:T(128)}, u32[]{:S(2)}) copy-start(f32[8]{0:T(128)} %pad.30.clone) | copy-start | bytes 100
  16.7 15.6 %collective-permute-start.3 = (bf16[4,48,1024]{2,1,0:T(8,128)(2,1)S(1)}, bf16[4,48,1024]{2,1,0:T(8,128)(2,1)S(1)}, u32[]{:S(2)}, u32[]{:S(2)}) collective-permute-start(bf16[4,48,1024]{2,1,0:T(8,128)(2,1)S(1)} %pad_maximum_fusion.2.refs_0_), channel_id=1, source_target_pairs={{0,6},{2,4},{4,2},{6,0},{8,14},{10,12},{12,10},{14,8},{16,22},{18,... | collective-permute-start | bytes 1179656 | tf_op jit(solution)/shard_map/ppermute | solution.py:444
  19.2 18.1 %collective-permute-start.4 = (bf16[4,48,1024]{2,1,0:T(8,128)(2,1)S(1)}, bf16[4,48,1024]{2,1,0:T(8,128)(2,1)S(1)}, u32[]{:S(2)}, u32[]{:S(2)}) collective-permute-start(bf16[4,48,1024]{2,1,0:T(8,128)(2,1)S(1)} %pad_maximum_fusion.2.refs_0_), channel_id=1, source_target_pairs={{0,2},{2,0},{4,6},{6,4},{8,10},{10,8},{12,14},{14,12},{16,18},{18,... | collective-permute-start | bytes 1179656 | tf_op jit(solution)/shard_map/ppermute | solution.py:444
  19.8 17.6 %collective-permute-start.5 = (bf16[4,48,1024]{2,1,0:T(8,128)(2,1)S(1)}, bf16[4,48,1024]{2,1,0:T(8,128)(2,1)S(1)}, u32[]{:S(2)}, u32[]{:S(2)}) collective-permute-start(bf16[4,48,1024]{2,1,0:T(8,128)(2,1)S(1)} %pad_maximum_fusion.2.refs_0_), channel_id=1, source_target_pairs={{0,4},{2,6},{4,0},{6,2},{8,12},{10,14},{12,8},{14,10},{16,20},{18,... | collective-permute-start | bytes 1179656 | tf_op jit(solution)/shard_map/ppermute | solution.py:444
  20.3 12.1 %collective-permute-start.11 = (bf16[48,1536]{1,0:T(8,128)(2,1)S(1)}, bf16[48,1536]{1,0:T(8,128)(2,1)S(1)}, u32[]{:S(2)}, u32[]{:S(2)}) collective-permute-start(bf16[48,1536]{1,0:T(8,128)(2,1)S(1)} %pad_maximum_fusion.4), channel_id=1, source_target_pairs={{0,8},{2,10},{4,12},{6,14},{8,0},{10,2},{12,4},{14,6},{16,24},{18,... | collective-permute-start | bytes 442376 | tf_op jit(solution)/shard_map/ppermute | solution.py:444
  21.9 11.1 %collective-permute-start.12 = (bf16[48,1536]{1,0:T(8,128)(2,1)S(1)}, bf16[48,1536]{1,0:T(8,128)(2,1)}, u32[]{:S(2)}, u32[]{:S(2)}) collective-permute-start(bf16[48,1536]{1,0:T(8,128)(2,1)S(1)} %pad_maximum_fusion.4), channel_id=1, source_target_pairs={{0,16},{2,18},{4,20},{6,22},{8,24},{10,26},{12,28},{14,30},{16,0},... | collective-permute-start | bytes 442376 | tf_op jit(solution)/shard_map/ppermute | solution.py:444
  32.3 11.0 %collective-permute-start.6 = (bf16[4,48,1024]{2,1,0:T(8,128)(2,1)S(1)}, bf16[4,48,1024]{2,1,0:T(8,128)(2,1)S(1)}, u32[]{:S(2)}, u32[]{:S(2)}) collective-permute-start(bf16[4,48,1024]{2,1,0:T(8,128)(2,1)S(1)} %pad_maximum_fusion.2.refs_0_), channel_id=1, source_target_pairs={{0,1},{1,0},{2,3},{3,2},{4,5},{5,4},{6,7},{7,6},{8,9},{9,8},{10,11... | collective-permute-start | bytes 1179656 | tf_op jit(solution)/shard_map/ppermute | solution.py:444
  32.4 8.3 %collective-permute-start.13 = (bf16[48,1536]{1,0:T(8,128)(2,1)S(1)}, bf16[48,1536]{1,0:T(8,128)(2,1)}, u32[]{:S(2)}, u32[]{:S(2)}) collective-permute-start(bf16[48,1536]{1,0:T(8,128)(2,1)S(1)} %pad_maximum_fusion.4), channel_id=1, source_target_pairs={{0,24},{2,26},{4,28},{6,30},{8,16},{10,18},{12,20},{14,22},{16,8},... | collective-permute-start | bytes 442376 | tf_op jit(solution)/shard_map/ppermute | solution.py:444
  33.1 11.8 %collective-permute-start.9 = (bf16[4,48,1024]{2,1,0:T(8,128)(2,1)S(1)}, bf16[4,48,1024]{2,1,0:T(8,128)(2,1)S(1)}, u32[]{:S(2)}, u32[]{:S(2)}) collective-permute-start(bf16[4,48,1024]{2,1,0:T(8,128)(2,1)S(1)} %collective-permute-done.3.refs_3_), channel_id=1, source_target_pairs={{0,1},{1,0},{2,3},{3,2},{4,5},{5,4},{6,7},{7,6},{8,9},{9,8},{10,11... | collective-permute-start | bytes 1179656 | tf_op jit(solution)/shard_map/ppermute | solution.py:444
  37.4 7.9 %collective-permute-start.7 = (bf16[4,48,1024]{2,1,0:T(8,128)(2,1)S(1)}, bf16[4,48,1024]{2,1,0:T(8,128)(2,1)S(1)}, u32[]{:S(2)}, u32[]{:S(2)}) collective-permute-start(bf16[4,48,1024]{2,1,0:T(8,128)(2,1)S(1)} %collective-permute-done.4.refs_1_), channel_id=1, source_target_pairs={{0,1},{1,0},{2,3},{3,2},{4,5},{5,4},{6,7},{7,6},{8,9},{9,8},{10,11... | collective-permute-start | bytes 1179656 | tf_op jit(solution)/shard_map/ppermute | solution.py:444
  37.4 7.9 %collective-permute-start.8 = (bf16[4,48,1024]{2,1,0:T(8,128)(2,1)S(1)}, bf16[4,48,1024]{2,1,0:T(8,128)(2,1)S(1)}, u32[]{:S(2)}, u32[]{:S(2)}) collective-permute-start(bf16[4,48,1024]{2,1,0:T(8,128)(2,1)S(1)} %collective-permute-done.5.refs_2_), channel_id=1, source_target_pairs={{0,1},{1,0},{2,3},{3,2},{4,5},{5,4},{6,7},{7,6},{8,9},{9,8},{10,11... | collective-permute-start | bytes 1179656 | tf_op jit(solution)/shard_map/ppermute | solution.py:444
  41.8 22.5 %collective-permute-start.14 = (bf16[4,48,1536]{2,1,0:T(8,128)(2,1)S(1)}, bf16[4,48,1536]{2,1,0:T(8,128)(2,1)S(1)}, u32[]{:S(2)}, u32[]{:S(2)}) collective-permute-start(bf16[4,48,1536]{2,1,0:T(8,128)(2,1)S(1)} %pad_maximum_fusion.1.refs_0_), channel_id=1, source_target_pairs={{0,2},{2,0},{4,6},{6,4},{8,10},{10,8},{12,14},{14,12},{16,18},{18,... | collective-permute-start | bytes 1769480 | tf_op jit(solution)/shard_map/ppermute | solution.py:444
  43.3 27.2 %collective-permute-start.15 = (bf16[4,48,1536]{2,1,0:T(8,128)(2,1)S(1)}, bf16[4,48,1536]{2,1,0:T(8,128)(2,1)S(1)}, u32[]{:S(2)}, u32[]{:S(2)}) collective-permute-start(bf16[4,48,1536]{2,1,0:T(8,128)(2,1)S(1)} %pad_maximum_fusion.1.refs_0_), channel_id=1, source_target_pairs={{0,4},{2,6},{4,0},{6,2},{8,12},{10,14},{12,8},{14,10},{16,20},{18,... | collective-permute-start | bytes 1769480 | tf_op jit(solution)/shard_map/ppermute | solution.py:444
  44.8 25.7 %collective-permute-start.16 = (bf16[4,48,1536]{2,1,0:T(8,128)(2,1)S(1)}, bf16[4,48,1536]{2,1,0:T(8,128)(2,1)S(1)}, u32[]{:S(2)}, u32[]{:S(2)}) collective-permute-start(bf16[4,48,1536]{2,1,0:T(8,128)(2,1)S(1)} %pad_maximum_fusion.1.refs_0_), channel_id=1, source_target_pairs={{0,6},{2,4},{4,2},{6,0},{8,14},{10,12},{12,10},{14,8},{16,22},{18,... | collective-permute-start | bytes 1769480 | tf_op jit(solution)/shard_map/ppermute | solution.py:444
  70.5 11.5 %collective-permute-start.17 = (bf16[4,48,1536]{2,1,0:T(8,128)(2,1)S(1)}, bf16[4,48,1536]{2,1,0:T(8,128)(2,1)S(1)}, u32[]{:S(2)}, u32[]{:S(2)}) collective-permute-start(bf16[4,48,1536]{2,1,0:T(8,128)(2,1)S(1)} %pad_maximum_fusion.1.refs_0_), channel_id=1, source_target_pairs={{0,1},{1,0},{2,3},{3,2},{4,5},{5,4},{6,7},{7,6},{8,9},{9,8},{10,11... | collective-permute-start | bytes 1769480 | tf_op jit(solution)/shard_map/ppermute | solution.py:444
  70.5 11.5 %collective-permute-start.18 = (bf16[4,48,1536]{2,1,0:T(8,128)(2,1)S(1)}, bf16[4,48,1536]{2,1,0:T(8,128)(2,1)S(1)}, u32[]{:S(2)}, u32[]{:S(2)}) collective-permute-start(bf16[4,48,1536]{2,1,0:T(8,128)(2,1)S(1)} %collective-permute-done.14.refs_1_), channel_id=1, source_target_pairs={{0,1},{1,0},{2,3},{3,2},{4,5},{5,4},{6,7},{7,6},{8,9},{9,8},{10,11... | collective-permute-start | bytes 1769480 | tf_op jit(solution)/shard_map/ppermute | solution.py:444
  71.0 11.0 %collective-permute-start.19 = (bf16[4,48,1536]{2,1,0:T(8,128)(2,1)S(1)}, bf16[4,48,1536]{2,1,0:T(8,128)(2,1)S(1)}, u32[]{:S(2)}, u32[]{:S(2)}) collective-permute-start(bf16[4,48,1536]{2,1,0:T(8,128)(2,1)S(1)} %collective-permute-done.15.refs_2_), channel_id=1, source_target_pairs={{0,1},{1,0},{2,3},{3,2},{4,5},{5,4},{6,7},{7,6},{8,9},{9,8},{10,11... | collective-permute-start | bytes 1769480 | tf_op jit(solution)/shard_map/ppermute | solution.py:444
  71.0 11.1 %collective-permute-start.20 = (bf16[4,48,1536]{2,1,0:T(8,128)(2,1)S(1)}, bf16[4,48,1536]{2,1,0:T(8,128)(2,1)S(1)}, u32[]{:S(2)}, u32[]{:S(2)}) collective-permute-start(bf16[4,48,1536]{2,1,0:T(8,128)(2,1)S(1)} %collective-permute-done.16.refs_3_), channel_id=1, source_target_pairs={{0,1},{1,0},{2,3},{3,2},{4,5},{5,4},{6,7},{7,6},{8,9},{9,8},{10,11... | collective-permute-start | bytes 1769480 | tf_op jit(solution)/shard_map/ppermute | solution.py:444
  110.6 7.4 %collective-permute-start.21 = (bf16[4,192,1536]{2,1,0:T(8,128)(2,1)}, bf16[4,192,1536]{2,1,0:T(8,128)(2,1)}, u32[]{:S(2)}, u32[]{:S(2)}) collective-permute-start(bf16[4,192,1536]{2,1,0:T(8,128)(2,1)} %get-tuple-element.172), channel_id=1, source_target_pairs={{0,1},{1,0},{2,3},{3,2},{4,5},{5,4},{6,7},{7,6},{8,9},{9,8},{10,11... | collective-permute-start | bytes 7077896 | tf_op jit(solution)/shard_map/ppermute | solution.py:444
  121.1 25.8 %collective-permute-start.22 = (bf16[192,1536]{1,0:T(8,128)(2,1)S(1)}, bf16[192,1536]{1,0:T(8,128)(2,1)S(1)}, u32[]{:S(2)}, u32[]{:S(2)}) collective-permute-start(bf16[192,1536]{1,0:T(8,128)(2,1)S(1)} %get-tuple-element.244), channel_id=1, source_target_pairs={{0,2},{2,0},{4,6},{6,4},{8,10},{10,8},{12,14},{14,12},{16,18},{18,... | collective-permute-start | bytes 1769480 | tf_op jit(solution)/shard_map/ppermute | solution.py:444
  122.4 26.5 %collective-permute-start.23 = (bf16[192,1536]{1,0:T(8,128)(2,1)S(1)}, bf16[192,1536]{1,0:T(8,128)(2,1)}, u32[]{:S(2)}, u32[]{:S(2)}) collective-permute-start(bf16[192,1536]{1,0:T(8,128)(2,1)S(1)} %get-tuple-element.246), channel_id=1, source_target_pairs={{0,4},{2,6},{4,0},{6,2},{8,12},{10,14},{12,8},{14,10},{16,20},{18,... | collective-permute-start | bytes 1769480 | tf_op jit(solution)/shard_map/ppermute | solution.py:444
  123.3 27.4 %collective-permute-start.24 = (bf16[192,1536]{1,0:T(8,128)(2,1)S(1)}, bf16[192,1536]{1,0:T(8,128)(2,1)}, u32[]{:S(2)}, u32[]{:S(2)}) collective-permute-start(bf16[192,1536]{1,0:T(8,128)(2,1)S(1)} %get-tuple-element.245), channel_id=1, source_target_pairs={{0,6},{2,4},{4,2},{6,0},{8,14},{10,12},{12,10},{14,8},{16,22},{18,... | collective-permute-start | bytes 1769480 | tf_op jit(solution)/shard_map/ppermute | solution.py:444
  152.2 15.7 %collective-permute-start.25 = (bf16[48,1536]{1,0:T(8,128)(2,1)S(1)}, bf16[48,1536]{1,0:T(8,128)(2,1)S(1)}, u32[]{:S(2)}, u32[]{:S(2)}) collective-permute-start(bf16[48,1536]{1,0:T(8,128)(2,1)S(1)} %get-tuple-element.255), channel_id=1, source_target_pairs={{0,8},{2,10},{4,12},{6,14},{8,0},{10,2},{12,4},{14,6},{16,24},{18,... | collective-permute-start | bytes 442376 | tf_op jit(solution)/shard_map/ppermute | solution.py:444
  154.4 13.6 %collective-permute-start.26 = (bf16[48,1536]{1,0:T(8,128)(2,1)S(1)}, bf16[48,1536]{1,0:T(8,128)(2,1)S(1)}, u32[]{:S(2)}, u32[]{:S(2)}) collective-permute-start(bf16[48,1536]{1,0:T(8,128)(2,1)S(1)} %get-tuple-element.254), channel_id=1, source_target_pairs={{0,16},{2,18},{4,20},{6,22},{8,24},{10,26},{12,28},{14,30},{16,0},... | collective-permute-start | bytes 442376 | tf_op jit(solution)/shard_map/ppermute | solution.py:444
  156.1 11.9 %collective-permute-start.27 = (bf16[48,1536]{1,0:T(8,128)(2,1)S(1)}, bf16[48,1536]{1,0:T(8,128)(2,1)S(1)}, u32[]{:S(2)}, u32[]{:S(2)}) collective-permute-start(bf16[48,1536]{1,0:T(8,128)(2,1)S(1)} %get-tuple-element.253), channel_id=1, source_target_pairs={{0,24},{2,26},{4,28},{6,30},{8,16},{10,18},{12,20},{14,22},{16,8},... | collective-permute-start | bytes 442376 | tf_op jit(solution)/shard_map/ppermute | solution.py:444
  156.9 11.2 %copy-start.4 = (bf16[768,1024]{1,0:T(8,128)(2,1)S(1)}, bf16[768,1024]{1,0:T(8,128)(2,1)}, u32[]{:S(2)}) copy-start(bf16[768,1024]{1,0:T(8,128)(2,1)} %get-tuple-element.160.normed_t) | copy-start | bytes 4718596
  156.9 11.2 %copy-start.7 = (f32[768,128]{1,0:T(8,128)S(1)}, f32[768,128]{1,0:T(8,128)}, u32[]{:S(2)}) copy-start(f32[768,128]{1,0:T(8,128)} %get-tuple-element.196.sums_in) | copy-start | bytes 1179652
  156.9 11.2 %copy-start.15 = (s32[2]{0:T(128)S(1)}, s32[2]{0:T(128)}, u32[]{:S(2)}) copy-start(s32[2]{0:T(128)} %copy-done.14) | copy-start | bytes 28
  174.2 3.9 %collective-permute-start.28 = (bf16[4,192,640]{2,1,0:T(8,128)(2,1)S(1)}, bf16[4,192,640]{2,1,0:T(8,128)(2,1)S(1)}, u32[]{:S(2)}, u32[]{:S(2)}) collective-permute-start(bf16[4,192,640]{2,1,0:T(8,128)(2,1)S(1)} %get-tuple-element.208), channel_id=1, source_target_pairs={{0,1},{1,0},{2,3},{3,2},{4,5},{5,4},{6,7},{7,6},{8,9},{9,8},{10,11... | collective-permute-start | bytes 2949128 | tf_op jit(solution)/shard_map/ppermute | solution.py:444
  178.4 14.4 %collective-permute-start.32 = (bf16[4,224,512]{2,1,0:T(8,128)(2,1)S(1)}, bf16[4,224,512]{2,1,0:T(8,128)(2,1)S(1)}, u32[]{:S(2)}, u32[]{:S(2)}) collective-permute-start(bf16[4,224,512]{2,1,0:T(8,128)(2,1)S(1)} %get-tuple-element.215), channel_id=1, source_target_pairs={{0,1},{1,0},{2,3},{3,2},{4,5},{5,4},{6,7},{7,6},{8,9},{9,8},{10,11... | collective-permute-start | bytes 2752520 | tf_op jit(solution)/shard_map/ppermute | solution.py:444
  179.0 12.9 %collective-permute-start.29 = (bf16[192,640]{1,0:T(8,128)(2,1)S(1)}, bf16[192,640]{1,0:T(8,128)(2,1)S(1)}, u32[]{:S(2)}, u32[]{:S(2)}) collective-permute-start(bf16[192,640]{1,0:T(8,128)(2,1)S(1)} %get-tuple-element.247), channel_id=1, source_target_pairs={{0,2},{2,0},{4,6},{6,4},{8,10},{10,8},{12,14},{14,12},{16,18},{18,... | collective-permute-start | bytes 737288 | tf_op jit(solution)/shard_map/ppermute | solution.py:444
  179.7 12.9 %collective-permute-start.30 = (bf16[192,640]{1,0:T(8,128)(2,1)S(1)}, bf16[192,640]{1,0:T(8,128)(2,1)S(1)}, u32[]{:S(2)}, u32[]{:S(2)}) collective-permute-start(bf16[192,640]{1,0:T(8,128)(2,1)S(1)} %get-tuple-element.249), channel_id=1, source_target_pairs={{0,4},{2,6},{4,0},{6,2},{8,12},{10,14},{12,8},{14,10},{16,20},{18,... | collective-permute-start | bytes 737288 | tf_op jit(solution)/shard_map/ppermute | solution.py:444
  181.2 11.4 %collective-permute-start.31 = (bf16[192,640]{1,0:T(8,128)(2,1)S(1)}, bf16[192,640]{1,0:T(8,128)(2,1)S(1)}, u32[]{:S(2)}, u32[]{:S(2)}) collective-permute-start(bf16[192,640]{1,0:T(8,128)(2,1)S(1)} %get-tuple-element.248), channel_id=1, source_target_pairs={{0,6},{2,4},{4,2},{6,0},{8,14},{10,12},{12,10},{14,8},{16,22},{18,... | collective-permute-start | bytes 737288 | tf_op jit(solution)/shard_map/ppermute | solution.py:444
  193.1 12.8 %collective-permute-start.33 = (bf16[224,512]{1,0:T(8,128)(2,1)S(1)}, bf16[224,512]{1,0:T(8,128)(2,1)S(1)}, u32[]{:S(2)}, u32[]{:S(2)}) collective-permute-start(bf16[224,512]{1,0:T(8,128)(2,1)S(1)} %get-tuple-element.250), channel_id=1, source_target_pairs={{0,2},{2,0},{4,6},{6,4},{8,10},{10,8},{12,14},{14,12},{16,18},{18,... | collective-permute-start | bytes 688136 | tf_op jit(solution)/shard_map/ppermute | solution.py:444
  194.5 12.6 %collective-permute-start.34 = (bf16[224,512]{1,0:T(8,128)(2,1)S(1)}, bf16[224,512]{1,0:T(8,128)(2,1)S(1)}, u32[]{:S(2)}, u32[]{:S(2)}) collective-permute-start(bf16[224,512]{1,0:T(8,128)(2,1)S(1)} %get-tuple-element.252), channel_id=1, source_target_pairs={{0,4},{2,6},{4,0},{6,2},{8,12},{10,14},{12,8},{14,10},{16,20},{18,... | collective-permute-start | bytes 688136 | tf_op jit(solution)/shard_map/ppermute | solution.py:444
  195.2 11.8 %collective-permute-start.35 = (bf16[224,512]{1,0:T(8,128)(2,1)S(1)}, bf16[224,512]{1,0:T(8,128)(2,1)S(1)}, u32[]{:S(2)}, u32[]{:S(2)}) collective-permute-start(bf16[224,512]{1,0:T(8,128)(2,1)S(1)} %get-tuple-element.251), channel_id=1, source_target_pairs={{0,6},{2,4},{4,2},{6,0},{8,14},{10,12},{12,10},{14,8},{16,22},{18,... | collective-permute-start | bytes 688136 | tf_op jit(solution)/shard_map/ppermute | solution.py:444
  196.7 10.6 %collective-permute-start.36 = (bf16[48,640]{1,0:T(8,128)(2,1)S(1)}, bf16[48,640]{1,0:T(8,128)(2,1)S(1)}, u32[]{:S(2)}, u32[]{:S(2)}) collective-permute-start(bf16[48,640]{1,0:T(8,128)(2,1)S(1)} %get-tuple-element.263), channel_id=1, source_target_pairs={{0,8},{2,10},{4,12},{6,14},{8,0},{10,2},{12,4},{14,6},{16,24},{18,... | collective-permute-start | bytes 184328 | tf_op jit(solution)/shard_map/ppermute | solution.py:444
  199.2 8.1 %collective-permute-start.37 = (bf16[48,640]{1,0:T(8,128)(2,1)S(1)}, bf16[48,640]{1,0:T(8,128)(2,1)S(1)}, u32[]{:S(2)}, u32[]{:S(2)}) collective-permute-start(bf16[48,640]{1,0:T(8,128)(2,1)S(1)} %get-tuple-element.262), channel_id=1, source_target_pairs={{0,16},{2,18},{4,20},{6,22},{8,24},{10,26},{12,28},{14,30},{16,0},... | collective-permute-start | bytes 184328 | tf_op jit(solution)/shard_map/ppermute | solution.py:444
  205.9 6.3 %collective-permute-start.38 = (bf16[48,640]{1,0:T(8,128)(2,1)S(1)}, bf16[48,640]{1,0:T(8,128)(2,1)S(1)}, u32[]{:S(2)}, u32[]{:S(2)}) collective-permute-start(bf16[48,640]{1,0:T(8,128)(2,1)S(1)} %get-tuple-element.261), channel_id=1, source_target_pairs={{0,24},{2,26},{4,28},{6,30},{8,16},{10,18},{12,20},{14,22},{16,8},... | collective-permute-start | bytes 184328 | tf_op jit(solution)/shard_map/ppermute | solution.py:444
  207.0 14.7 %copy-start.1 = (bf16[48,256]{1,0:T(8,128)(2,1)S(1)}, bf16[48,256]{1,0:T(8,128)(2,1)}, u32[]{:S(2)}) copy-start(bf16[48,256]{1,0:T(8,128)(2,1)} %param.16) | copy-start | bytes 73732
  212.3 4.5 %collective-permute-start.39 = (bf16[80,512]{1,0:T(8,128)(2,1)S(1)}, bf16[80,512]{1,0:T(8,128)(2,1)S(1)}, u32[]{:S(2)}, u32[]{:S(2)}) collective-permute-start(bf16[80,512]{1,0:T(8,128)(2,1)S(1)} %get-tuple-element.259), channel_id=1, source_target_pairs={{0,8},{2,10},{4,12},{6,14},{8,0},{10,2},{12,4},{14,6},{16,24},{18,... | collective-permute-start | bytes 245768 | tf_op jit(solution)/shard_map/ppermute | solution.py:444
  212.3 5.4 %collective-permute-start.40 = (bf16[80,512]{1,0:T(8,128)(2,1)S(1)}, bf16[80,512]{1,0:T(8,128)(2,1)S(1)}, u32[]{:S(2)}, u32[]{:S(2)}) collective-permute-start(bf16[80,512]{1,0:T(8,128)(2,1)S(1)} %get-tuple-element.258), channel_id=1, source_target_pairs={{0,16},{2,18},{4,20},{6,22},{8,24},{10,26},{12,28},{14,30},{16,0},... | collective-permute-start | bytes 245768 | tf_op jit(solution)/shard_map/ppermute | solution.py:444
  213.9 6.3 %collective-permute-start.41 = (bf16[80,512]{1,0:T(8,128)(2,1)S(1)}, bf16[80,512]{1,0:T(8,128)(2,1)S(1)}, u32[]{:S(2)}, u32[]{:S(2)}) collective-permute-start(bf16[80,512]{1,0:T(8,128)(2,1)S(1)} %get-tuple-element.257), channel_id=1, source_target_pairs={{0,24},{2,26},{4,28},{6,30},{8,16},{10,18},{12,20},{14,22},{16,8},... | collective-permute-start | bytes 245768 | tf_op jit(solution)/shard_map/ppermute | solution.py:444
  (22 other events, 90.3 us)
where the time goes:
time: 223 us; the launch traced here: 222 us
  Pallas kernels  117 us (52%)
  starting transfers between devices  44.3 us (20%)
  waiting for transfers between devices  24.7 us (11%)
  local copies, waits for them, and re-layouts  15.3 us (7%)
  other arithmetic  13.3 us (6%)
  matrix products  6.14 us (3%)
    ppermute x42, starting transfers between devices, swap(): return lax.ppermute(value, axis, [(i, i ^ bit) for i in range(count)])  44.3 us
    pallas_call x3, Pallas kernels, scan_backward(): pl.pallas_call(functools.partial(scan_backward_kernel, per_seq, pairs, ba...  39.6 us
    ppermute x42, waiting for transfers between devices, swap(): return lax.ppermute(value, axis, [(i, i ^ bit) for i in range(count)])  24.7 us
    pallas_call x2, Pallas kernels, scan_forward(): pl.pallas_call(functools.partial(scan_forward_kernel, per_seq, pairs, bas...  19.5 us
    pallas_call x1, Pallas kernels, gate_both(): pl.pallas_call(gate_kernel, grid=(rows // size,), in_specs=[tall(inner),...  12.8 us
    pallas_call x1, Pallas kernels, pack_early(): pl.pallas_call(functools.partial(pack_early_kernel, rows), grid=(4,), in_...  11.9 us
    pallas_call x1, Pallas kernels, token_grads(): pl.pallas_call(token_grads_kernel, grid=(rows // 256,), in_specs=[tall(v)...  9.33 us
    unnamed x59, local copies, waits for them, and re-layouts  9.08 us
  transfers between devices with their start and end apart: 42, of which 11 were waited for; matrix products, arithmetic and copies ran while one was open for 8% of the time, Pallas kernels for 39%

commit v1 on v0

--- a/solution.py
+++ b/solution.py
@@ -128,8 +128,16 @@
     rates_ref[:, :Q] = step
     rates_ref[:, Q:] = cum
     b_turned = bc[:, :STATE].T.astype(b16)
+    leaving = []
     for p in range(pairs):
         sl = slice(p * Q, (p + 1) * Q)
+        if p % 2 == 0:
+            two = slice(p * Q, (p + 2) * Q)
+            entering = state[:, two]
+            held = entering.astype(b16)
+            state_out_ref[0, :, two] = held
+            carried = nn(c_low, held)
+            rises = []
         past = xhalo_ref[:, sl].astype(f32)[8:32] * keep
         pre = conv(with_past(xin_ref[:, sl].astype(f32), past), cx_ref, sl)
         pre_ref[:, sl] = pre.astype(b16)
@@ -145,13 +153,15 @@
             [jnp.where(left, scaled, 0.0).astype(b16), jnp.where(left, 0.0, scaled).astype(b16)], axis=0
         )
         both = jnp.where(left, c0, c1)
-        entering = state[:, sl]
-        held = entering.astype(b16)
-        state_out_ref[0, :, sl] = held
-        y = nn(weights, split) + nn(c_low, held) * jnp.exp(both) + cx_ref[5:6, sl] * x
+        rise = jnp.exp(both)
+        here = carried[:, (p % 2) * Q : (p % 2 + 1) * Q]
+        y = nn(weights, split) + here * rise + cx_ref[5:6, sl] * x
         y_ref[:, sl] = y.astype(b16)
-        leaving = (scaled * jnp.exp(both[Q - 1 : Q, :] - both)).astype(b16)
-        state[:, sl] = entering * jnp.exp(both[Q - 1 : Q, :]) + nn(b_turned, leaving)
+        leaving.append((scaled * jnp.exp(both[Q - 1 : Q, :] - both)).astype(b16))
+        rises.append(rise[Q - 1 : Q, :])
+        if p % 2 == 1:
+            added = nn(b_turned, jnp.concatenate(leaving[-2:], axis=1))
+            state[:, two] = entering * jnp.concatenate(rises, axis=1) + added
 
 
 def scan_forward(xin, bd, cx, cb, heads, base, count, before):
@@ -242,6 +252,17 @@
     col_sums = jnp.zeros((Q, Q), f32)
     for p in range(pairs):
         sl = slice(p * Q, (p + 1) * Q)
+        if p % 2 == 0:
+            two = slice(p * Q, (p + 2) * Q)
+            held = held_ref[0, :, two]
+            lam = adjoint[:, two]
+            lam_here = lam.astype(b16)
+            lam_low[:, two] = lam_here
+            inner_states.append(jnp.sum(lam * held.astype(f32), axis=0, keepdims=True))
+            carried_two = nn(c_low, held)
+            back_two = nn(b_low, lam_here)
+            rises = []
+        half_lanes = slice((p % 2) * Q, (p % 2 + 1) * Q)
         pre = pre_ref[:, sl].astype(f32)
         sig = sigmoid(pre)
         x = pre * sig
@@ -269,21 +290,17 @@
         both = jnp.where(left, c0, c1)
         tail = jnp.exp(both[Q - 1 : Q, :] - both)
         rise = jnp.exp(both)
-        held = held_ref[0, :, sl]
-        lam = adjoint[:, sl]
-        lam_here = lam.astype(b16)
-        lam_low[:, sl] = lam_here
-        inner_states.append(jnp.sum(lam * held.astype(f32), axis=0, keepdims=True))
-        dx_state = nn(b_low, lam_here) * tail
+        dx_state = back_two[:, half_lanes] * tail
         dscaled = nn(jnp.concatenate(weights, axis=1), split) + dx_state
         dye_here = dy * rise
-        products[0:Q, sl] = (dye_here * nn(c_low, held)).astype(b16)
+        products[0:Q, sl] = (dye_here * carried_two[:, half_lanes]).astype(b16)
         products[Q : 2 * Q, sl] = (scaled * dx_state).astype(b16)
         products[2 * Q :, sl] = (dscaled * x).astype(b16)
         xt[:, sl] = (scaled * tail).astype(b16)
-        dye_low = dye_here.astype(b16)
-        dye[:, sl] = dye_low
-        adjoint[:, sl] = lam * rise[Q - 1 : Q, :] + nn(c_turned, dye_low)
+        dye[:, sl] = dye_here.astype(b16)
+        rises.append(rise[Q - 1 : Q, :])
+        if p % 2 == 1:
+            adjoint[:, two] = lam * jnp.concatenate(rises, axis=1) + nn(c_turned, dye[:, two])
         dx = dscaled * step2 + cx_ref[5:6, sl] * dy
         dpre = dx * (sig + x * (1.0 - sig))
         padded = with_future(dpre, xnext[:, sl])
@@ -521,54 +538,47 @@
 TILE = 256
 
 
-def pack_early_kernel(rows, where_ref, normed_t, cot_t, dz, mixed, w_z, keep, send, sums, piece):
+def pack_whole_kernel(rows, weighted, where_ref, left, right, *refs):
     step = pl.program_id(0)
-    width = piece.shape[1]
-
-    @pl.when(step == 0)
-    def _():
-        sums[...] = jnp.zeros_like(sums)
-
-    @pl.when(step < 2)
-    def _():
-        grad = nn(normed_t[...], dz[...])
-        sums[...] += product_sums(w_z, grad)
-        piece[...] = grad.astype(b16)
-
-    @pl.when(step >= 2)
-    def _():
-        piece[...] = nn(cot_t[...], mixed[...]).astype(b16)
-
-    put(where_ref, rows, piece, keep, send, pl.multiple_of((step // 2) * width, 128), width, step % 2)
-
-
-def pack_early(where, normed_t, cot_t, dz, mixed, w_z):
-    model, tokens = normed_t.shape
+    grad = nn(left[...], right[...])
+    if weighted:
+        weight, keep, send, sums, piece = refs
+
+        @pl.when(step == 0)
+        def _():
+            sums[...] = jnp.zeros_like(sums)
+
+        sums[...] += product_sums(weight, grad)
+    else:
+        keep, send, piece = refs
+    piece[...] = grad.astype(b16)
+    put(where_ref, rows, piece, keep, send, 0, piece.shape[1], step)
+
+
+def pack_whole(where, left, right, weight=None):
+    model, tokens = left.shape
     rows = model // 16
-    inner = dz.shape[1]
-    half = inner // 2
+    half = right.shape[1] // 2
     fixed = lambda shape: pl.BlockSpec(shape, lambda t: (0,) * len(shape))
-    first = lambda t: (0, jnp.minimum(t, 1))
-    second = lambda t: (0, jnp.maximum(t - 2, 0))
-    packed = (4, 4 * rows, inner)
+    packed = (4, 4 * rows, half)
+    weights = [] if weight is None else [weight]
+    extra = [(model, 128)] * len(weights)
     return pl.pallas_call(
-        functools.partial(pack_early_kernel, rows),
-        grid=(4,),
+        functools.partial(pack_whole_kernel, rows, bool(weights)),
+        grid=(2,),
         in_specs=[
             pl.BlockSpec(memory_space=pltpu.SMEM),
             fixed((model, tokens)),
-            fixed((model, tokens)),
-            pl.BlockSpec((tokens, half), first),
-            pl.BlockSpec((tokens, half), second),
-            pl.BlockSpec((model, half), first),
-        ],
-        out_specs=[fixed(packed), fixed(packed), fixed((model, 128))],
-        out_shape=[jax.ShapeDtypeStruct(packed, b16)] * 2 + [jax.ShapeDtypeStruct((model, 128), f32)],
+            pl.BlockSpec((tokens, half), lambda t: (0, t)),
+        ]
+        + [pl.BlockSpec((model, half), lambda t: (0, t))] * len(weights),
+        out_specs=[fixed(packed), fixed(packed)] + [fixed(shape) for shape in extra],
+        out_shape=[jax.ShapeDtypeStruct(packed, b16)] * 2 + [jax.ShapeDtypeStruct(shape, f32) for shape in extra],
         scratch_shapes=[pltpu.VMEM((model, half), b16)],
-        compiler_params=pltpu.CompilerParams(vmem_limit_bytes=56 * MIB),
-        cost_estimate=pl.CostEstimate(flops=4 * model * tokens * inner, bytes_accessed=4 * tokens * inner, transcendentals=0),
-        name="pack_early",
-    )(where, normed_t, cot_t, dz, mixed, w_z)
+        compiler_params=pltpu.CompilerParams(vmem_limit_bytes=30 * MIB),
+        cost_estimate=pl.CostEstimate(flops=8 * model * tokens * half, bytes_accessed=8 * tokens * half, transcendentals=0),
+        name="pack_whole",
+    )(where, left, right, *weights)
 
 
 def pack_first_kernel(rows, where_ref, normed_t, dxin, dbd, w_x, w_s, sums_in, keep, send, sums, piece):
@@ -705,14 +715,14 @@
 
 
 def finish_kernel(half, side_ref, *refs):
-    early, first, second, pick = refs[:4], refs[4:8], refs[8:12], refs[12]
-    (z_out, bc_out, dt_out, cx_out, cb_out, alog_out, bias_out, skip_out, norm_out, pre_out, w_out, lines) = refs[13:]
+    early, first, second, pick = refs[:2], refs[2:4], refs[4:8], refs[8]
+    (z_out, bc_out, dt_out, cx_out, cb_out, alog_out, bias_out, skip_out, norm_out, pre_out, w_out, lines) = refs[9:]
     side = side_ref[1]
-    rows = early[0].shape[0]
+    rows = first[0].shape[0]
 
     def total(parts):
         value = parts[0][...].astype(f32)
-        for k in range(1, 4):
+        for k in range(1, len(parts)):
             value = value + parts[k][...].astype(f32)
         return value
 
@@ -753,7 +763,7 @@
 
 
 def finish(where, early, first, second, pick, model, half):
-    rows = early[0].shape[0]
+    rows = first[0].shape[0]
     heads = half // HEAD
     whole = pl.BlockSpec(memory_space=pltpu.VMEM)
     shapes = [
@@ -762,7 +772,7 @@
     ]
     return pl.pallas_call(
         functools.partial(finish_kernel, half),
-        in_specs=[pl.BlockSpec(memory_space=pltpu.SMEM)] + [whole] * 13,
+        in_specs=[pl.BlockSpec(memory_space=pltpu.SMEM)] + [whole] * 9,
         out_specs=[whole] * len(shapes),
         out_shape=[jax.ShapeDtypeStruct(shape, f32) for shape in shapes],
         scratch_shapes=[pltpu.VMEM((8, 2 * half), f32)],
@@ -785,6 +795,10 @@
         shared = jnp.broadcast_to(total[None, 4 * rows :], (4, *total[4 * rows :].shape))
         split = jnp.concatenate([split, shared], axis=1)
     return split.astype(b16)
+
+
+def plus(a, b):
+    return (a.astype(f32) + b.astype(f32)).astype(b16)
 
 
 def along_z_parts(parts):
@@ -954,12 +968,12 @@
     xin = nn(normed, w_x).astype(b16)
     bd = nn(normed, w_s)
     blocks = tokens.shape[0] // Q
-    started = list(scan_forward(xin, bd, cx, cb, heads, 0, blocks // 2, None))
+    started = list(scan_forward(xin, bd, cx, cb, heads, 0, blocks * 3 // 4, None))
     if quick:
         started[4], *mine_second = lax.optimization_barrier((started[4], *mine_second))
         other_second = [swap(part, 1, "tensor") for part in mine_second]
     ssd, held, pre, rates, ended = scan_forward(
-        xin, bd, cx, cb, heads, blocks // 2, blocks - blocks // 2, started
+        xin, bd, cx, cb, heads, blocks * 3 // 4, blocks - blocks * 3 // 4, started
     )
     if quick:
         other_second = lax.optimization_barrier((ended, *other_second))[1:]
@@ -969,17 +983,17 @@
         scan_backward(dssd, xin, pre, bd, held, rates, cx, cb, heads, pick, base, count, before)
     )
     if quick:
-        keep, send, sums = pack_early(where, normed_t, cot_t, dz, mixed, w_z)
-        dssd, keep, send = lax.optimization_barrier((dssd, keep, send))
+        keep_out, send_out = pack_whole(where, cot_t, mixed)
+        dz, keep_out, send_out = lax.optimization_barrier((dz, keep_out, send_out))
+        parts_out = sum_tensor(keep_out, send_out)
+        keep, send, sums = pack_whole(where, normed_t, dz, w_z)
+        dssd, keep, send, parts_out = lax.optimization_barrier((dssd, keep, send, parts_out))
         parts = sum_tensor(keep, send)
-        carry = scan(blocks * 7 // 8, blocks // 8, None)
-        carry[2], parts = lax.optimization_barrier((carry[2], parts))
-        parts = sum_around(parts, shard_rows)
-        carry = scan(blocks // 4, blocks * 5 // 8, carry)
-        carry[2], parts = lax.optimization_barrier((carry[2], parts))
-        early = along_z_parts(parts)
-        carry = scan(0, blocks // 4, carry)
-        carry[0], carry[1], *early = lax.optimization_barrier((carry[0], carry[1], *early))
+        carry = scan(blocks * 3 // 4, blocks // 4, None)
+        carry[2], parts, parts_out = lax.optimization_barrier((carry[2], parts, parts_out))
+        early = sum_around(jnp.concatenate([parts, parts_out], axis=2), shard_rows)
+        carry = scan(0, blocks * 3 // 4, carry)
+        carry[0], carry[1], early = lax.optimization_barrier((carry[0], carry[1], early))
     else:
         early = scatter_plain(
             [nn(normed_t, dz).astype(b16), nn(cot_t, mixed).astype(b16)],
@@ -997,17 +1011,23 @@
         )
         parts_second = sum_tensor(keep, send)
         parts_first = sum_around(parts_first, shard_rows)
+        early = early.reshape(2, 2, *early.shape[1:])
+        early, near = early[:, 0], swap(early[:, 1], 4)
     grad_tokens = token_grads(dz, dxin, dbd, x, cotangent, w_z, w_x, w_s, gain_row)
     if quick:
-        grad_tokens, mixed, parts_first, parts_second = lax.optimization_barrier(
-            (grad_tokens, mixed, parts_first, parts_second)
+        grad_tokens, mixed, parts_first, parts_second, early, near = lax.optimization_barrier(
+            (grad_tokens, mixed, parts_first, parts_second, early, near)
         )
         second = sum_around(parts_second, shard_rows)
-        first = along_z_parts(parts_first)
+        early = plus(early, near)
+        early = [early[0], swap(early[1], 8)]
+        parts_first = parts_first.reshape(2, 2, *parts_first.shape[1:])
+        first = plus(parts_first[:, 0], swap(parts_first[:, 1], 4))
+        mixed, second, first = lax.optimization_barrier((mixed, second, first))
+        first = [first[0], swap(first[1], 8)]
+        second = along_z_parts(second)
     out = add_branch(mixed, x, w_out_t)
     if quick:
-        out, second, *first = lax.optimization_barrier((out, second, *first))
-        second = along_z_parts(second)
         z_out, bc_out, dt_out, cx_out, cb_out, alog, bias, skip, norm, pre_sum, w_out_grad = finish(
             where, early, first, second, pick[:half], model, half
         )

time: 223 us -> 210 us (0.942)
  Pallas kernels: 117 us -> 111 us
  waiting for transfers between devices: 24.7 us -> 19 us
  starting transfers between devices: 44.3 us -> 41.1 us
  local copies, waits for them, and re-layouts: 15.3 us -> 18 us
    ppermute x42 -> x41, waiting for transfers between devices: 24.7 us -> 19 us  [swap(): return lax.ppermute(value, axis, [(i, i ^ bit) for i in range(count)])]
    pallas_call x3 -> x2, Pallas kernels: 39.6 us -> 36.2 us  [scan_backward(): pl.pallas_call(functools.partial(scan_backward_kernel, per_seq, pairs, ba...]
    unnamed x59 -> x68, local copies, waits for them, and re-layouts: 9.08 us -> 12.4 us
    ppermute x42 -> x41, starting transfers between devices: 44.3 us -> 41.1 us  [swap(): return lax.ppermute(value, axis, [(i, i ^ bit) for i in range(count)])]
    pallas_call x1 -> x2, Pallas kernels: 11.9 us -> 9.06 us  [pack_whole(): pl.pallas_call(functools.partial(pack_whole_kernel, rows, bool(weights)),...]
  transfers between devices with their start and end apart: 42 -> 41, of which waited for: 11 -> 9; matrix products, arithmetic and copies ran while one was open for 8% -> 9% of each run, Pallas kernels for 39% -> 42%
where the time goes in v1:
time: 210 us; the launch traced here: 209 us
  Pallas kernels  111 us (53%)
  starting transfers between devices  41.1 us (20%)
  waiting for transfers between devices  19 us (9%)
  local copies, waits for them, and re-layouts  18 us (9%)
  other arithmetic  12.5 us (6%)
  matrix products  6.17 us (3%)
    ppermute x41, starting transfers between devices, swap(): return lax.ppermute(value, axis, [(i, i ^ bit) for i in range(count)])  41.1 us
    pallas_call x2, Pallas kernels, scan_backward(): pl.pallas_call(functools.partial(scan_backward_kernel, per_seq, pairs, ba...  36.2 us
    pallas_call x2, Pallas kernels, scan_forward(): pl.pallas_call(functools.partial(scan_forward_kernel, per_seq, pairs, bas...  19.5 us
    ppermute x41, waiting for transfers between devices, swap(): return lax.ppermute(value, axis, [(i, i ^ bit) for i in range(count)])  19 us
    pallas_call x1, Pallas kernels, gate_both(): pl.pallas_call(gate_kernel, grid=(rows // size,), in_specs=[tall(inner),...  12.9 us
    unnamed x68, local copies, waits for them, and re-layouts  12.4 us
    pallas_call x1, Pallas kernels, token_grads(): pl.pallas_call(token_grads_kernel, grid=(rows // 256,), in_specs=[tall(v)...  9.32 us
    pallas_call x2, Pallas kernels, pack_whole(): pl.pallas_call(functools.partial(pack_whole_kernel, rows, bool(weights)),...  9.06 us
  transfers between devices with their start and end apart: 41, of which 9 were waited for; matrix products, arithmetic and copies ran while one was open for 9% of the time, Pallas kernels for 42%

profile of v1, /device:TPU:0, one launch (start us, length us, event | category | flops | bytes accessed | tf_op | source)
XLA Modules:
  0.0 209.0 jit_solution(12935670583293689969)
XLA Ops:
  3.0 3.1 %collective-permute-start = (bf16[48,1024]{1,0:T(8,128)(2,1)S(1)}, bf16[48,1024]{1,0:T(8,128)(2,1)S(1)}, u32[]{:S(2)}, u32[]{:S(2)}) collective-permute-start(bf16[48,1024]{1,0:T(8,128)(2,1)S(1)} %get-tuple-element.252), channel_id=1, source_target_pairs={{0,8},{2,10},{4,12},{6,14},{8,0},{10,2},{12,4},{14,6},{16,24},{18,... | collective-permute-start | bytes 294920 | tf_op jit(solution)/shard_map/ppermute | solution.py:461
  6.1 2.6 %collective-permute-start.1 = (bf16[48,1024]{1,0:T(8,128)(2,1)S(1)}, bf16[48,1024]{1,0:T(8,128)(2,1)S(1)}, u32[]{:S(2)}, u32[]{:S(2)}) collective-permute-start(bf16[48,1024]{1,0:T(8,128)(2,1)S(1)} %get-tuple-element.252), channel_id=1, source_target_pairs={{0,16},{2,18},{4,20},{6,22},{8,24},{10,26},{12,28},{14,30},{16,0},... | collective-permute-start | bytes 294920 | tf_op jit(solution)/shard_map/ppermute | solution.py:461
  11.0 1.3 pad_convert_fusion.refs_5_.refs_8_
  14.6 2.1 %collective-permute-done.1 = bf16[48,1024]{1,0:T(8,128)(2,1)S(1)} collective-permute-done((bf16[48,1024]{1,0:T(8,128)(2,1)S(1)}, bf16[48,1024]{1,0:T(8,128)(2,1)S(1)}, u32[]{:S(2)}, u32[]{:S(2)}) %collective-permute-start.1) | collective-permute-done | bytes 98336 | tf_op jit(solution)/shard_map/ppermute | solution.py:461
  16.8 2.5 %collective-permute-start.3 = (bf16[4,48,1024]{2,1,0:T(8,128)(2,1)S(1)}, bf16[4,48,1024]{2,1,0:T(8,128)(2,1)S(1)}, u32[]{:S(2)}, u32[]{:S(2)}) collective-permute-start(bf16[4,48,1024]{2,1,0:T(8,128)(2,1)S(1)} %pad_maximum_fusion.2.refs_0_), channel_id=1, source_target_pairs={{0,6},{2,4},{4,2},{6,0},{8,14},{10,12},{12,10},{14,8},{16,22},{18,... | collective-permute-start | bytes 1179656 | tf_op jit(solution)/shard_map/ppermute | solution.py:461
  20.3 1.6 collective-permute-start.11
  22.0 1.4 collective-permute-start.12
  23.4 8.2 %prepare.1 = (bf16[1024,768]{1,0:T(8,128)(2,1)}, bf16[1024,768]{1,0:T(8,128)(2,1)}, bf16[1024,768]{1,0:T(8,128)(2,1)}, bf16[768,1024]{1,0:T(8,128)(2,1)}, bf16[768,1024]{1,0:T(8,128)(2,1)}) custom-call(bf16[1024,768]{1,0:T(8,128)(2,1)} %tokens, bf16[1024,768]{1,0:T(8,128)(2,1)} %cot, f32[1,768]{1,0:T(1,128)} %reshape.106.gain.gain_pre), custom_call_target="tpu_custom_call" | custom-call | tf_op jit(solution)/shard_map/prepare/pallas_call | solution.py:838
  31.7 1.4 collective-permute-start.13
  33.3 2.6 %collective-permute-done.4.refs_1_ = bf16[4,48,1024]{2,1,0:T(8,128)(2,1)S(1)} collective-permute-done((bf16[4,48,1024]{2,1,0:T(8,128)(2,1)S(1)}, bf16[4,48,1024]{2,1,0:T(8,128)(2,1)S(1)}, u32[]{:S(2)}, u32[]{:S(2)}) %collective-permute-start.4) | collective-permute-done | bytes 393248 | tf_op jit(solution)/shard_map/ppermute | solution.py:461
  38.6 1.5 collective-permute-done.13
  41.1 1.6 collective-permute-start.14
  42.6 1.5 collective-permute-start.15
  47.8 4.0 %convolution_convert_fusion.refs_0_.refs_1_ = bf16[1024,1536]{1,0:T(8,128)(2,1)} fusion(bf16[1024,768]{1,0:T(8,128)(2,1)S(1)} %copy-done.31, bf16[768,1536]{1,0:T(8,128)(2,1)S(1)} %get-tuple-element.129.w_x), kind=kOutput, calls=%fused_computation | convolution fusion | flops 2417491968 | bytes 7077888 | tf_op jit(solution)/shard_map/dot_general | solution.py:22
  51.9 2.1 %fusion.15.refs_2_.refs_3_.refs_4_ = f32[1024,384]{1,0:T(8,128)} fusion(bf16[1024,768]{1,0:T(8,128)(2,1)S(1)} %copy-done.31, bf16[768,128]{1,0:T(8,128)(2,1)S(1)} %slice_add_fusion, bf16[768,256]{1,0:T(8,128)(2,1)S(1)} %get-tuple-element.130), kind=kOutput, calls=%fused_computation.85 | convolution fusion | flops 605159424 | bytes 3735552 | tf_op jit(solution)/shard_map/dot_general | solution.py:22
  54.0 13.3 %scan_forward.2 = (bf16[1024,1536]{1,0:T(8,128)(2,1)}, bf16[8,128,1536]{2,1,0:T(8,128)(2,1)}, bf16[1024,1536]{1,0:T(8,128)(2,1)}, f32[1024,256]{1,0:T(8,128)}, f32[128,1536]{1,0:T(8,128)}) custom-call(bf16[1024,1536]{1,0:T(8,128)(2,1)} %convolution_convert_fusion.refs_0_.refs_1_, bf16[1024,1536]{1,0:T(8,128)(2,1)} %convolution_convert_fusion.refs_0_.refs_1_, ...), custom_call_target="tpu_custom_call" | custom-call | flops 7077888000 | bytes 9437184 | tf_op jit(solution)/shard_map/scan_forward/pallas_call | solution.py:172
  67.3 2.6 %collective-permute-done.15.refs_2_ = bf16[4,48,1536]{2,1,0:T(8,128)(2,1)S(1)} collective-permute-done((bf16[4,48,1536]{2,1,0:T(8,128)(2,1)S(1)}, bf16[4,48,1536]{2,1,0:T(8,128)(2,1)S(1)}, u32[]{:S(2)}, u32[]{:S(2)}) %collective-permute-start.15) | collective-permute-done | bytes 589856 | tf_op jit(solution)/shard_map/ppermute | solution.py:461
  71.4 6.3 %scan_forward.3 = (bf16[1024,1536]{1,0:T(8,128)(2,1)}, bf16[8,128,1536]{2,1,0:T(8,128)(2,1)}, bf16[1024,1536]{1,0:T(8,128)(2,1)}, f32[1024,256]{1,0:T(8,128)}, f32[128,1536]{1,0:T(8,128)}) custom-call(bf16[1024,1536]{1,0:T(8,128)(2,1)} %convolution_convert_fusion.refs_0_.refs_1_, ...), custom_call_target="tpu_custom_call", output_to_operand_aliasing={{0}: (8, {}), {1}: (9, {}), {2}: (10, {}), {3}: (11, {})} | custom-call | flops 2359296000 | bytes 3145728 | tf_op jit(solution)/shard_map/scan_forward/pallas_call | solution.py:172
  78.6 1.4 copy-done.13
  80.0 1.4 copy-done.15
  81.4 12.9 %gate_both.1 = (bf16[1024,1536]{1,0:T(8,128)(2,1)}, bf16[1024,1536]{1,0:T(8,128)(2,1)}, bf16[1024,1536]{1,0:T(8,128)(2,1)}, f32[8,1536]{1,0:T(8,128)}) custom-call(bf16[1024,1536]{1,0:T(8,128)(2,1)} %get-tuple-element.140.y, bf16[1024,768]{1,0:T(8,128)(2,1)} %get-tuple-element.127.normed, bf16[1024,768]{1,0:T(8,128)(2,1)} %get-tuple-element.141.cot, ...), custom_call_target="tpu_custom_call" | custom-call | flops 12582912000 | bytes 15728640 | tf_op jit(solution)/shard_map/gate_both/pallas_call | solution.py:446
  94.3 1.9 copy-done.21
  96.2 3.6 %pack_whole.2 = (bf16[4,192,768]{2,1,0:T(8,128)(2,1)S(1)}, bf16[4,192,768]{2,1,0:T(8,128)(2,1)S(1)}) custom-call(s32[2]{0:T(128)S(1)} %pad_add_fusion.where_ref.side_ref, bf16[768,1024]{1,0:T(8,128)(2,1)S(1)} %copy-done.20, bf16[1024,1536]{1,0:T(8,128)(2,1)S(1)} %copy-done.21), custom_call_target="tpu_custom_call" | custom-call | flops 4831838208 | bytes 6291456 | tf_op jit(solution)/shard_map/pack_whole/pallas_call | solution.py:566
  99.9 5.4 %pack_whole.3 = (bf16[4,192,768]{2,1,0:T(8,128)(2,1)S(1)}, bf16[4,192,768]{2,1,0:T(8,128)(2,1)}, f32[768,128]{1,0:T(8,128)S(1)}) custom-call(s32[2]{0:T(128)S(1)} %pad_add_fusion.where_ref.side_ref, bf16[768,1024]{1,0:T(8,128)(2,1)S(1)} %copy-done.4, bf16[1024,1536]{1,0:T(8,128)(2,1)S(1)} %copy-done.23, bf16[768,1536]{1,0:T(8,128)(2,1)S(1)} %copy-done.16), custom_call_target="tpu_custom_call" | custom-call | flops 4831838208 | bytes 6291456 | tf_op jit(solution)/shard_map/pack_whole/pallas_call | solution.py:566
  105.4 1.3 add_convert_fusion.1
  108.3 10.2 %scan_backward.2 = (bf16[1024,1536]{1,0:T(8,128)(2,1)}, bf16[1024,384]{1,0:T(8,128)(2,1)}, f32[128,1536]{1,0:T(8,128)}, f32[24,1536]{1,0:T(8,128)}, f32[24,256]{...) custom-call(bf16[1024,1536]{1,0:T(8,128)(2,1)} %get-tuple-element.164.refs_0_, ...), custom_call_target="tpu_custom_call" | custom-call | flops 4718592000 | bytes 3932160 | tf_op jit(solution)/shard_map/scan_backward/pallas_call | solution.py:361
  118.6 1.5 add_convert_fusion
  121.5 1.4 copy-done.25
  123.0 1.3 collective-permute-start.23
  125.1 1.4 collective-permute-start.25
  126.6 26.0 %scan_backward.3 = (bf16[1024,1536]{1,0:T(8,128)(2,1)}, bf16[1024,384]{1,0:T(8,128)(2,1)}, f32[128,1536]{1,0:T(8,128)}, f32[24,1536]{1,0:T(8,128)}, f32[24,256]{...) custom-call(bf16[1024,1536]{1,0:T(8,128)(2,1)} %get-tuple-element.16, ...), custom_call_target="tpu_custom_call", output_to_operand_aliasing={{0}: (17, {}), {1}: (18, {})} | custom-call | flops 14155776000 | bytes 11796480 | tf_op jit(solution)/shard_map/scan_backward/pallas_call | solution.py:361
  152.6 1.6 fusion.2
  154.2 1.9 copy-done.2
  156.1 3.1 %pack_first.1 = (bf16[4,192,640]{2,1,0:T(8,128)(2,1)S(1)}, bf16[4,192,640]{2,1,0:T(8,128)(2,1)S(1)}, f32[768,128]{1,0:T(8,128)S(1)}) custom-call(s32[2]{0:T(128)S(1)} %pad_add_fusion.where_ref.side_ref, bf16[768,1024]{1,0:T(8,128)(2,1)S(1)} %copy-done.4, bf16[1024,1536]{1,0:T(8,128)(2,1)S(1)} %copy-done.2, bf16[1024,384]{1,0:T(8,128)(2,1)S(1)} %copy-done.5, ...), custom_call_target="tpu_custom_call" | custom-call | flops 1409286144 | bytes 1048576 | tf_op jit(solution)/shard_map/pack_first/pallas_call | solution.py:614
  159.4 3.0 %collective-permute-start.31 = (bf16[2,48,1536]{2,1,0:T(8,128)(2,1)S(1)}, bf16[2,48,1536]{2,1,0:T(8,128)(2,1)S(1)}, u32[]{:S(2)}, u32[]{:S(2)}) collective-permute-start(bf16[2,48,1536]{2,1,0:T(8,128)(2,1)S(1)} %get-tuple-element.239), channel_id=1, source_target_pairs={{0,8},{2,10},{4,12},{6,14},{8,0},{10,2},{12,4},{14,6},{16,24},{18,... | collective-permute-start | bytes 884744 | tf_op jit(solution)/shard_map/ppermute | solution.py:461
  162.4 3.7 %pack_second.1 = (bf16[4,224,512]{2,1,0:T(8,128)(2,1)S(1)}, bf16[4,224,512]{2,1,0:T(8,128)(2,1)S(1)}) custom-call(s32[2]{0:T(128)S(1)} %pad_add_fusion.where_ref.side_ref, bf16[768,1024]{1,0:T(8,128)(2,1)S(1)} %copy-done.4, bf16[1024,1536]{1,0:T(8,128)(2,1)S(1)} %copy-done.3, bf16[768,1536]{1,0:T(8,128)(2,1)S(1)} %get-tuple-element.129.w_x, ...), custom_call_target="tpu_custom_call" | custom-call | flops 1610612736 | bytes 2097152 | tf_op jit(solution)/shard_map/pack_second/pallas_call | solution.py:689
  166.7 1.3 collective-permute-start.27
  168.8 1.4 collective-permute-start.29
  170.3 9.3 %token_grads.1 = bf16[1024,768]{1,0:T(8,128)(2,1)} custom-call(bf16[1024,1536]{1,0:T(8,128)(2,1)S(1)} %copy-done.24, bf16[1024,1536]{1,0:T(8,128)(2,1)S(1)} %copy-done.3, bf16[1024,384]{1,0:T(8,128)(2,1)S(1)} %copy-done.5, bf16[1024,768]{1,0:T(8,128)(2,1)S(1)} %copy-done.18, bf16[1024,768]{1,0:T(8,128)(2,1)S(1)} %copy-done.19, ...), custom_call_target="tpu_custom_call" | custom-call | flops 6291456000 | bytes 15728640 | tf_op jit(solution)/shard_map/token_grads/pallas_call | solution.py:870
  179.6 1.6 collective-permute-done.29
  182.4 1.4 collective-permute-start.35
  184.7 1.5 collective-permute-start.33
  188.0 4.4 %collective-permute-done.32 = bf16[224,512]{1,0:T(8,128)(2,1)S(1)} collective-permute-done((bf16[224,512]{1,0:T(8,128)(2,1)S(1)}, bf16[224,512]{1,0:T(8,128)(2,1)S(1)}, u32[]{:S(2)}, u32[]{:S(2)}) %collective-permute-start.32) | collective-permute-done | bytes 229408 | tf_op jit(solution)/shard_map/ppermute | solution.py:461
  192.4 3.1 %collective-permute-done.33 = bf16[224,512]{1,0:T(8,128)(2,1)S(1)} collective-permute-done((bf16[224,512]{1,0:T(8,128)(2,1)S(1)}, bf16[224,512]{1,0:T(8,128)(2,1)S(1)}, u32[]{:S(2)}, u32[]{:S(2)}) %collective-permute-start.33) | collective-permute-done | bytes 229408 | tf_op jit(solution)/shard_map/ppermute | solution.py:461
  196.8 2.2 %collective-permute-start.39 = (bf16[80,512]{1,0:T(8,128)(2,1)S(1)}, bf16[80,512]{1,0:T(8,128)(2,1)S(1)}, u32[]{:S(2)}, u32[]{:S(2)}) collective-permute-start(bf16[80,512]{1,0:T(8,128)(2,1)S(1)} %get-tuple-element.242), channel_id=1, source_target_pairs={{0,16},{2,18},{4,20},{6,22},{8,24},{10,26},{12,28},{14,30},{16,0},... | collective-permute-start | bytes 245768 | tf_op jit(solution)/shard_map/ppermute | solution.py:461
  198.9 1.4 collective-permute-start.40
  201.3 5.4 %add_branch.1 = bf16[1024,768]{1,0:T(8,128)(2,1)} custom-call(bf16[1024,1536]{1,0:T(8,128)(2,1)S(1)} %copy-done.22, bf16[1024,768]{1,0:T(8,128)(2,1)S(1)} %copy-done.18, bf16[768,1536]{1,0:T(8,128)(2,1)S(1)} %copy-done.14), custom_call_target="tpu_custom_call" | custom-call | flops 3145728000 | bytes 7864320 | tf_op jit(solution)/shard_map/add_branch/pallas_call | solution.py:889
  207.3 1.5 finish.1
  (179 shorter events, 30.2 us)
Async XLA Ops:
  0.7 11.7 %copy-start.28 = (bf16[768,48]{0,1:T(8,128)(2,1)S(1)}, bf16[768,48]{0,1:T(8,128)(2,1)}, u32[]{:S(2)}) copy-start(bf16[768,48]{0,1:T(8,128)(2,1)} %param.24) | copy-start | bytes 221188
  0.7 11.8 %copy-start.29 = (bf16[768]{0:T(1024)(128)(2,1)S(1)}, bf16[768]{0:T(1024)(128)(2,1)}, u32[]{:S(2)}) copy-start(bf16[768]{0:T(1024)(128)(2,1)} %param.14) | copy-start | bytes 4612
  3.0 11.6 %collective-permute-start = (bf16[48,1024]{1,0:T(8,128)(2,1)S(1)}, bf16[48,1024]{1,0:T(8,128)(2,1)S(1)}, u32[]{:S(2)}, u32[]{:S(2)}) collective-permute-start(bf16[48,1024]{1,0:T(8,128)(2,1)S(1)} %get-tuple-element.252), channel_id=1, source_target_pairs={{0,8},{2,10},{4,12},{6,14},{8,0},{10,2},{12,4},{14,6},{16,24},{18,... | collective-permute-start | bytes 294920 | tf_op jit(solution)/shard_map/ppermute | solution.py:461
  6.1 10.6 %collective-permute-start.1 = (bf16[48,1024]{1,0:T(8,128)(2,1)S(1)}, bf16[48,1024]{1,0:T(8,128)(2,1)S(1)}, u32[]{:S(2)}, u32[]{:S(2)}) collective-permute-start(bf16[48,1024]{1,0:T(8,128)(2,1)S(1)} %get-tuple-element.252), channel_id=1, source_target_pairs={{0,16},{2,18},{4,20},{6,22},{8,24},{10,26},{12,28},{14,30},{16,0},... | collective-permute-start | bytes 294920 | tf_op jit(solution)/shard_map/ppermute | solution.py:461
  8.7 8.0 %collective-permute-start.2 = (bf16[48,1024]{1,0:T(8,128)(2,1)S(1)}, bf16[48,1024]{1,0:T(8,128)(2,1)S(1)}, u32[]{:S(2)}, u32[]{:S(2)}) collective-permute-start(bf16[48,1024]{1,0:T(8,128)(2,1)S(1)} %get-tuple-element.252), channel_id=1, source_target_pairs={{0,24},{2,26},{4,28},{6,30},{8,16},{10,18},{12,20},{14,22},{16,8},... | collective-permute-start | bytes 294920 | tf_op jit(solution)/shard_map/ppermute | solution.py:461
  11.0 2.6 %collective-permute-start.10 = (f32[1,8,768]{2,1,0:T(8,128)S(1)}, f32[1,8,768]{2,1,0:T(8,128)S(1)}, u32[]{:S(2)}, u32[]{:S(2)}) collective-permute-start(f32[1,8,768]{2,1,0:T(8,128)S(1)} %maximum_bitcast_fusion), channel_id=1, source_target_pairs={{0,1},{1,0},{2,3},{3,2},{4,5},{5,4},{6,7},{7,6},{8,9},{9,8},{10,11... | collective-permute-start | bytes 73736 | tf_op jit(solution)/shard_map/ppermute | solution.py:461
  16.8 14.9 %collective-permute-start.3 = (bf16[4,48,1024]{2,1,0:T(8,128)(2,1)S(1)}, bf16[4,48,1024]{2,1,0:T(8,128)(2,1)S(1)}, u32[]{:S(2)}, u32[]{:S(2)}) collective-permute-start(bf16[4,48,1024]{2,1,0:T(8,128)(2,1)S(1)} %pad_maximum_fusion.2.refs_0_), channel_id=1, source_target_pairs={{0,6},{2,4},{4,2},{6,0},{8,14},{10,12},{12,10},{14,8},{16,22},{18,... | collective-permute-start | bytes 1179656 | tf_op jit(solution)/shard_map/ppermute | solution.py:461
  19.3 16.6 %collective-permute-start.4 = (bf16[4,48,1024]{2,1,0:T(8,128)(2,1)S(1)}, bf16[4,48,1024]{2,1,0:T(8,128)(2,1)S(1)}, u32[]{:S(2)}, u32[]{:S(2)}) collective-permute-start(bf16[4,48,1024]{2,1,0:T(8,128)(2,1)S(1)} %pad_maximum_fusion.2.refs_0_), channel_id=1, source_target_pairs={{0,2},{2,0},{4,6},{6,4},{8,10},{10,8},{12,14},{14,12},{16,18},{18,... | collective-permute-start | bytes 1179656 | tf_op jit(solution)/shard_map/ppermute | solution.py:461
  19.8 16.1 %collective-permute-start.5 = (bf16[4,48,1024]{2,1,0:T(8,128)(2,1)S(1)}, bf16[4,48,1024]{2,1,0:T(8,128)(2,1)S(1)}, u32[]{:S(2)}, u32[]{:S(2)}) collective-permute-start(bf16[4,48,1024]{2,1,0:T(8,128)(2,1)S(1)} %pad_maximum_fusion.2.refs_0_), channel_id=1, source_target_pairs={{0,4},{2,6},{4,0},{6,2},{8,12},{10,14},{12,8},{14,10},{16,20},{18,... | collective-permute-start | bytes 1179656 | tf_op jit(solution)/shard_map/ppermute | solution.py:461
  20.3 11.4 %collective-permute-start.11 = (bf16[48,1536]{1,0:T(8,128)(2,1)S(1)}, bf16[48,1536]{1,0:T(8,128)(2,1)S(1)}, u32[]{:S(2)}, u32[]{:S(2)}) collective-permute-start(bf16[48,1536]{1,0:T(8,128)(2,1)S(1)} %pad_maximum_fusion.4), channel_id=1, source_target_pairs={{0,8},{2,10},{4,12},{6,14},{8,0},{10,2},{12,4},{14,6},{16,24},{18,... | collective-permute-start | bytes 442376 | tf_op jit(solution)/shard_map/ppermute | solution.py:461
  22.0 11.2 %collective-permute-start.12 = (bf16[48,1536]{1,0:T(8,128)(2,1)S(1)}, bf16[48,1536]{1,0:T(8,128)(2,1)}, u32[]{:S(2)}, u32[]{:S(2)}) collective-permute-start(bf16[48,1536]{1,0:T(8,128)(2,1)S(1)} %pad_maximum_fusion.4), channel_id=1, source_target_pairs={{0,16},{2,18},{4,20},{6,22},{8,24},{10,26},{12,28},{14,30},{16,0},... | collective-permute-start | bytes 442376 | tf_op jit(solution)/shard_map/ppermute | solution.py:461
  23.4 13.0 %copy-start.30 = (f32[8]{0:T(128)S(1)}, f32[8]{0:T(128)}, u32[]{:S(2)}) copy-start(f32[8]{0:T(128)} %pad.30.clone) | copy-start | bytes 100
  31.7 11.0 %collective-permute-start.6 = (bf16[4,48,1024]{2,1,0:T(8,128)(2,1)S(1)}, bf16[4,48,1024]{2,1,0:T(8,128)(2,1)S(1)}, u32[]{:S(2)}, u32[]{:S(2)}) collective-permute-start(bf16[4,48,1024]{2,1,0:T(8,128)(2,1)S(1)} %pad_maximum_fusion.2.refs_0_), channel_id=1, source_target_pairs={{0,1},{1,0},{2,3},{3,2},{4,5},{5,4},{6,7},{7,6},{8,9},{9,8},{10,11... | collective-permute-start | bytes 1179656 | tf_op jit(solution)/shard_map/ppermute | solution.py:461
  31.7 8.3 %collective-permute-start.13 = (bf16[48,1536]{1,0:T(8,128)(2,1)S(1)}, bf16[48,1536]{1,0:T(8,128)(2,1)}, u32[]{:S(2)}, u32[]{:S(2)}) collective-permute-start(bf16[48,1536]{1,0:T(8,128)(2,1)S(1)} %pad_maximum_fusion.4), channel_id=1, source_target_pairs={{0,24},{2,26},{4,28},{6,30},{8,16},{10,18},{12,20},{14,22},{16,8},... | collective-permute-start | bytes 442376 | tf_op jit(solution)/shard_map/ppermute | solution.py:461
  33.2 11.0 %collective-permute-start.9 = (bf16[4,48,1024]{2,1,0:T(8,128)(2,1)S(1)}, bf16[4,48,1024]{2,1,0:T(8,128)(2,1)S(1)}, u32[]{:S(2)}, u32[]{:S(2)}) collective-permute-start(bf16[4,48,1024]{2,1,0:T(8,128)(2,1)S(1)} %collective-permute-done.3.refs_3_), channel_id=1, source_target_pairs={{0,1},{1,0},{2,3},{3,2},{4,5},{5,4},{6,7},{7,6},{8,9},{9,8},{10,11... | collective-permute-start | bytes 1179656 | tf_op jit(solution)/shard_map/ppermute | solution.py:461
  35.9 8.7 %collective-permute-start.7 = (bf16[4,48,1024]{2,1,0:T(8,128)(2,1)S(1)}, bf16[4,48,1024]{2,1,0:T(8,128)(2,1)S(1)}, u32[]{:S(2)}, u32[]{:S(2)}) collective-permute-start(bf16[4,48,1024]{2,1,0:T(8,128)(2,1)S(1)} %collective-permute-done.4.refs_1_), channel_id=1, source_target_pairs={{0,1},{1,0},{2,3},{3,2},{4,5},{5,4},{6,7},{7,6},{8,9},{9,8},{10,11... | collective-permute-start | bytes 1179656 | tf_op jit(solution)/shard_map/ppermute | solution.py:461
  35.9 8.7 %collective-permute-start.8 = (bf16[4,48,1024]{2,1,0:T(8,128)(2,1)S(1)}, bf16[4,48,1024]{2,1,0:T(8,128)(2,1)S(1)}, u32[]{:S(2)}, u32[]{:S(2)}) collective-permute-start(bf16[4,48,1024]{2,1,0:T(8,128)(2,1)S(1)} %collective-permute-done.5.refs_2_), channel_id=1, source_target_pairs={{0,1},{1,0},{2,3},{3,2},{4,5},{5,4},{6,7},{7,6},{8,9},{9,8},{10,11... | collective-permute-start | bytes 1179656 | tf_op jit(solution)/shard_map/ppermute | solution.py:461
  41.1 26.2 %collective-permute-start.14 = (bf16[4,48,1536]{2,1,0:T(8,128)(2,1)S(1)}, bf16[4,48,1536]{2,1,0:T(8,128)(2,1)S(1)}, u32[]{:S(2)}, u32[]{:S(2)}) collective-permute-start(bf16[4,48,1536]{2,1,0:T(8,128)(2,1)S(1)} %pad_maximum_fusion.1.refs_0_), channel_id=1, source_target_pairs={{0,2},{2,0},{4,6},{6,4},{8,10},{10,8},{12,14},{14,12},{16,18},{18,... | collective-permute-start | bytes 1769480 | tf_op jit(solution)/shard_map/ppermute | solution.py:461
  42.6 27.2 %collective-permute-start.15 = (bf16[4,48,1536]{2,1,0:T(8,128)(2,1)S(1)}, bf16[4,48,1536]{2,1,0:T(8,128)(2,1)S(1)}, u32[]{:S(2)}, u32[]{:S(2)}) collective-permute-start(bf16[4,48,1536]{2,1,0:T(8,128)(2,1)S(1)} %pad_maximum_fusion.1.refs_0_), channel_id=1, source_target_pairs={{0,4},{2,6},{4,0},{6,2},{8,12},{10,14},{12,8},{14,10},{16,20},{18,... | collective-permute-start | bytes 1769480 | tf_op jit(solution)/shard_map/ppermute | solution.py:461
  44.2 25.7 %collective-permute-start.16 = (bf16[4,48,1536]{2,1,0:T(8,128)(2,1)S(1)}, bf16[4,48,1536]{2,1,0:T(8,128)(2,1)S(1)}, u32[]{:S(2)}, u32[]{:S(2)}) collective-permute-start(bf16[4,48,1536]{2,1,0:T(8,128)(2,1)S(1)} %pad_maximum_fusion.1.refs_0_), channel_id=1, source_target_pairs={{0,6},{2,4},{4,2},{6,0},{8,14},{10,12},{12,10},{14,8},{16,22},{18,... | collective-permute-start | bytes 1769480 | tf_op jit(solution)/shard_map/ppermute | solution.py:461
  69.8 7.9 %collective-permute-start.17 = (bf16[4,48,1536]{2,1,0:T(8,128)(2,1)S(1)}, bf16[4,48,1536]{2,1,0:T(8,128)(2,1)S(1)}, u32[]{:S(2)}, u32[]{:S(2)}) collective-permute-start(bf16[4,48,1536]{2,1,0:T(8,128)(2,1)S(1)} %pad_maximum_fusion.1.refs_0_), channel_id=1, source_target_pairs={{0,1},{1,0},{2,3},{3,2},{4,5},{5,4},{6,7},{7,6},{8,9},{9,8},{10,11... | collective-permute-start | bytes 1769480 | tf_op jit(solution)/shard_map/ppermute | solution.py:461
  69.8 7.9 %collective-permute-start.18 = (bf16[4,48,1536]{2,1,0:T(8,128)(2,1)S(1)}, bf16[4,48,1536]{2,1,0:T(8,128)(2,1)S(1)}, u32[]{:S(2)}, u32[]{:S(2)}) collective-permute-start(bf16[4,48,1536]{2,1,0:T(8,128)(2,1)S(1)} %collective-permute-done.14.refs_1_), channel_id=1, source_target_pairs={{0,1},{1,0},{2,3},{3,2},{4,5},{5,4},{6,7},{7,6},{8,9},{9,8},{10,11... | collective-permute-start | bytes 1769480 | tf_op jit(solution)/shard_map/ppermute | solution.py:461
  70.3 7.4 %collective-permute-start.19 = (bf16[4,48,1536]{2,1,0:T(8,128)(2,1)S(1)}, bf16[4,48,1536]{2,1,0:T(8,128)(2,1)S(1)}, u32[]{:S(2)}, u32[]{:S(2)}) collective-permute-start(bf16[4,48,1536]{2,1,0:T(8,128)(2,1)S(1)} %collective-permute-done.15.refs_2_), channel_id=1, source_target_pairs={{0,1},{1,0},{2,3},{3,2},{4,5},{5,4},{6,7},{7,6},{8,9},{9,8},{10,11... | collective-permute-start | bytes 1769480 | tf_op jit(solution)/shard_map/ppermute | solution.py:461
  70.3 7.4 %collective-permute-start.20 = (bf16[4,48,1536]{2,1,0:T(8,128)(2,1)S(1)}, bf16[4,48,1536]{2,1,0:T(8,128)(2,1)S(1)}, u32[]{:S(2)}, u32[]{:S(2)}) collective-permute-start(bf16[4,48,1536]{2,1,0:T(8,128)(2,1)S(1)} %collective-permute-done.16.refs_3_), channel_id=1, source_target_pairs={{0,1},{1,0},{2,3},{3,2},{4,5},{5,4},{6,7},{7,6},{8,9},{9,8},{10,11... | collective-permute-start | bytes 1769480 | tf_op jit(solution)/shard_map/ppermute | solution.py:461
  81.4 12.9 %copy-start.20 = (bf16[768,1024]{1,0:T(8,128)(2,1)S(1)}, bf16[768,1024]{1,0:T(8,128)(2,1)}, u32[]{:S(2)}) copy-start(bf16[768,1024]{1,0:T(8,128)(2,1)} %get-tuple-element.155.left) | copy-start | bytes 4718596
  99.8 5.6 %collective-permute-start.21 = (bf16[4,192,768]{2,1,0:T(8,128)(2,1)S(1)}, bf16[4,192,768]{2,1,0:T(8,128)(2,1)S(1)}, u32[]{:S(2)}, u32[]{:S(2)}) collective-permute-start(bf16[4,192,768]{2,1,0:T(8,128)(2,1)S(1)} %get-tuple-element.163), channel_id=1, source_target_pairs={{0,1},{1,0},{2,3},{3,2},{4,5},{5,4},{6,7},{7,6},{8,9},{9,8},{10,11... | collective-permute-start | bytes 3538952 | tf_op jit(solution)/shard_map/ppermute | solution.py:461
  106.7 11.8 %collective-permute-start.22 = (bf16[4,192,768]{2,1,0:T(8,128)(2,1)}, bf16[4,192,768]{2,1,0:T(8,128)(2,1)}, u32[]{:S(2)}, u32[]{:S(2)}) collective-permute-start(bf16[4,192,768]{2,1,0:T(8,128)(2,1)} %get-tuple-element.170), channel_id=1, source_target_pairs={{0,1},{1,0},{2,3},{3,2},{4,5},{5,4},{6,7},{7,6},{8,9},{9,8},{10,11... | collective-permute-start | bytes 3538952 | tf_op jit(solution)/shard_map/ppermute | solution.py:461
  123.0 29.5 %collective-permute-start.23 = (bf16[192,1536]{1,0:T(8,128)(2,1)S(1)}, bf16[192,1536]{1,0:T(8,128)(2,1)S(1)}, u32[]{:S(2)}, u32[]{:S(2)}) collective-permute-start(bf16[192,1536]{1,0:T(8,128)(2,1)S(1)} %get-tuple-element.230), channel_id=1, source_target_pairs={{0,2},{2,0},{4,6},{6,4},{8,10},{10,8},{12,14},{14,12},{16,18},{18,... | collective-permute-start | bytes 1769480 | tf_op jit(solution)/shard_map/ppermute | solution.py:461
  124.3 28.3 %collective-permute-start.24 = (bf16[192,1536]{1,0:T(8,128)(2,1)S(1)}, bf16[192,1536]{1,0:T(8,128)(2,1)S(1)}, u32[]{:S(2)}, u32[]{:S(2)}) collective-permute-start(bf16[192,1536]{1,0:T(8,128)(2,1)S(1)} %get-tuple-element.232), channel_id=1, source_target_pairs={{0,4},{2,6},{4,0},{6,2},{8,12},{10,14},{12,8},{14,10},{16,20},{18,... | collective-permute-start | bytes 1769480 | tf_op jit(solution)/shard_map/ppermute | solution.py:461
  125.1 27.5 %collective-permute-start.25 = (bf16[192,1536]{1,0:T(8,128)(2,1)S(1)}, bf16[192,1536]{1,0:T(8,128)(2,1)}, u32[]{:S(2)}, u32[]{:S(2)}) collective-permute-start(bf16[192,1536]{1,0:T(8,128)(2,1)S(1)} %get-tuple-element.231), channel_id=1, source_target_pairs={{0,6},{2,4},{4,2},{6,0},{8,14},{10,12},{12,10},{14,8},{16,22},{18,... | collective-permute-start | bytes 1769480 | tf_op jit(solution)/shard_map/ppermute | solution.py:461
  159.2 6.9 %collective-permute-start.26 = (bf16[4,192,640]{2,1,0:T(8,128)(2,1)S(1)}, bf16[4,192,640]{2,1,0:T(8,128)(2,1)S(1)}, u32[]{:S(2)}, u32[]{:S(2)}) collective-permute-start(bf16[4,192,640]{2,1,0:T(8,128)(2,1)S(1)} %get-tuple-element.198), channel_id=1, source_target_pairs={{0,1},{1,0},{2,3},{3,2},{4,5},{5,4},{6,7},{7,6},{8,9},{9,8},{10,11... | collective-permute-start | bytes 2949128 | tf_op jit(solution)/shard_map/ppermute | solution.py:461
  159.4 22.2 %collective-permute-start.31 = (bf16[2,48,1536]{2,1,0:T(8,128)(2,1)S(1)}, bf16[2,48,1536]{2,1,0:T(8,128)(2,1)S(1)}, u32[]{:S(2)}, u32[]{:S(2)}) collective-permute-start(bf16[2,48,1536]{2,1,0:T(8,128)(2,1)S(1)} %get-tuple-element.239), channel_id=1, source_target_pairs={{0,8},{2,10},{4,12},{6,14},{8,0},{10,2},{12,4},{14,6},{16,24},{18,... | collective-permute-start | bytes 884744 | tf_op jit(solution)/shard_map/ppermute | solution.py:461
  162.4 7.9 %copy-start.19 = (bf16[1024,768]{1,0:T(8,128)(2,1)S(1)}, bf16[1024,768]{1,0:T(8,128)(2,1)}, u32[]{:S(2)}) copy-start(bf16[1024,768]{1,0:T(8,128)(2,1)} %get-tuple-element.141.cot) | copy-start | bytes 4718596
  166.4 14.9 %collective-permute-start.30 = (bf16[4,224,512]{2,1,0:T(8,128)(2,1)S(1)}, bf16[4,224,512]{2,1,0:T(8,128)(2,1)S(1)}, u32[]{:S(2)}, u32[]{:S(2)}) collective-permute-start(bf16[4,224,512]{2,1,0:T(8,128)(2,1)S(1)} %get-tuple-element.205), channel_id=1, source_target_pairs={{0,1},{1,0},{2,3},{3,2},{4,5},{5,4},{6,7},{7,6},{8,9},{9,8},{10,11... | collective-permute-start | bytes 2752520 | tf_op jit(solution)/shard_map/ppermute | solution.py:461
  166.7 12.9 %collective-permute-start.27 = (bf16[192,640]{1,0:T(8,128)(2,1)S(1)}, bf16[192,640]{1,0:T(8,128)(2,1)S(1)}, u32[]{:S(2)}, u32[]{:S(2)}) collective-permute-start(bf16[192,640]{1,0:T(8,128)(2,1)S(1)} %get-tuple-element.233), channel_id=1, source_target_pairs={{0,2},{2,0},{4,6},{6,4},{8,10},{10,8},{12,14},{14,12},{16,18},{18,... | collective-permute-start | bytes 737288 | tf_op jit(solution)/shard_map/ppermute | solution.py:461
  168.0 11.6 %collective-permute-start.28 = (bf16[192,640]{1,0:T(8,128)(2,1)S(1)}, bf16[192,640]{1,0:T(8,128)(2,1)S(1)}, u32[]{:S(2)}, u32[]{:S(2)}) collective-permute-start(bf16[192,640]{1,0:T(8,128)(2,1)S(1)} %get-tuple-element.235), channel_id=1, source_target_pairs={{0,4},{2,6},{4,0},{6,2},{8,12},{10,14},{12,8},{14,10},{16,20},{18,... | collective-permute-start | bytes 737288 | tf_op jit(solution)/shard_map/ppermute | solution.py:461
  168.8 12.3 %collective-permute-start.29 = (bf16[192,640]{1,0:T(8,128)(2,1)S(1)}, bf16[192,640]{1,0:T(8,128)(2,1)S(1)}, u32[]{:S(2)}, u32[]{:S(2)}) collective-permute-start(bf16[192,640]{1,0:T(8,128)(2,1)S(1)} %get-tuple-element.234), channel_id=1, source_target_pairs={{0,6},{2,4},{4,2},{6,0},{8,14},{10,12},{12,10},{14,8},{16,22},{18,... | collective-permute-start | bytes 737288 | tf_op jit(solution)/shard_map/ppermute | solution.py:461
  181.6 19.7 %copy-start.22 = (bf16[1024,1536]{1,0:T(8,128)(2,1)S(1)}, bf16[1024,1536]{1,0:T(8,128)(2,1)}, u32[]{:S(2)}) copy-start(bf16[1024,1536]{1,0:T(8,128)(2,1)} %get-tuple-element.210.right.mixed) | copy-start | bytes 9437188
  181.7 25.1 %collective-permute-start.36 = (bf16[48,1536]{1,0:T(8,128)(2,1)S(1)}, bf16[48,1536]{1,0:T(8,128)(2,1)S(1)}, u32[]{:S(2)}, u32[]{:S(2)}) collective-permute-start(bf16[48,1536]{1,0:T(8,128)(2,1)S(1)} %get-tuple-element.245), channel_id=1, source_target_pairs={{0,16},{2,18},{4,20},{6,22},{8,24},{10,26},{12,28},{14,30},{16,0},... | collective-permute-start | bytes 442376 | tf_op jit(solution)/shard_map/ppermute | solution.py:461
  182.4 5.6 %collective-permute-start.35 = (bf16[2,48,640]{2,1,0:T(8,128)(2,1)S(1)}, bf16[2,48,640]{2,1,0:T(8,128)(2,1)S(1)}, u32[]{:S(2)}, u32[]{:S(2)}) collective-permute-start(bf16[2,48,640]{2,1,0:T(8,128)(2,1)S(1)} %slice_bitcast_fusion.14), channel_id=1, source_target_pairs={{0,8},{2,10},{4,12},{6,14},{8,0},{10,2},{12,4},{14,6},{16,24},{18,... | collective-permute-start | bytes 368648 | tf_op jit(solution)/shard_map/ppermute | solution.py:461
  183.8 8.6 %collective-permute-start.32 = (bf16[224,512]{1,0:T(8,128)(2,1)S(1)}, bf16[224,512]{1,0:T(8,128)(2,1)S(1)}, u32[]{:S(2)}, u32[]{:S(2)}) collective-permute-start(bf16[224,512]{1,0:T(8,128)(2,1)S(1)} %get-tuple-element.236), channel_id=1, source_target_pairs={{0,2},{2,0},{4,6},{6,4},{8,10},{10,8},{12,14},{14,12},{16,18},{18,... | collective-permute-start | bytes 688136 | tf_op jit(solution)/shard_map/ppermute | solution.py:461
  184.7 10.9 %collective-permute-start.33 = (bf16[224,512]{1,0:T(8,128)(2,1)S(1)}, bf16[224,512]{1,0:T(8,128)(2,1)S(1)}, u32[]{:S(2)}, u32[]{:S(2)}) collective-permute-start(bf16[224,512]{1,0:T(8,128)(2,1)S(1)} %get-tuple-element.238), channel_id=1, source_target_pairs={{0,4},{2,6},{4,0},{6,2},{8,12},{10,14},{12,8},{14,10},{16,20},{18,... | collective-permute-start | bytes 688136 | tf_op jit(solution)/shard_map/ppermute | solution.py:461
  186.2 9.4 %collective-permute-start.34 = (bf16[224,512]{1,0:T(8,128)(2,1)S(1)}, bf16[224,512]{1,0:T(8,128)(2,1)S(1)}, u32[]{:S(2)}, u32[]{:S(2)}) collective-permute-start(bf16[224,512]{1,0:T(8,128)(2,1)S(1)} %get-tuple-element.237), channel_id=1, source_target_pairs={{0,6},{2,4},{4,2},{6,0},{8,14},{10,12},{12,10},{14,8},{16,22},{18,... | collective-permute-start | bytes 688136 | tf_op jit(solution)/shard_map/ppermute | solution.py:461
  188.0 13.3 %copy-start.14 = (bf16[768,1536]{1,0:T(8,128)(2,1)S(1)}, bf16[768,1536]{1,0:T(8,128)(2,1)}, u32[]{:S(2)}) copy-start(bf16[768,1536]{1,0:T(8,128)(2,1)} %copy-done.13) | copy-start | bytes 7077892
  195.8 11.4 %collective-permute-start.38 = (bf16[80,512]{1,0:T(8,128)(2,1)S(1)}, bf16[80,512]{1,0:T(8,128)(2,1)S(1)}, u32[]{:S(2)}, u32[]{:S(2)}) collective-permute-start(bf16[80,512]{1,0:T(8,128)(2,1)S(1)} %get-tuple-element.243), channel_id=1, source_target_pairs={{0,8},{2,10},{4,12},{6,14},{8,0},{10,2},{12,4},{14,6},{16,24},{18,... | collective-permute-start | bytes 245768 | tf_op jit(solution)/shard_map/ppermute | solution.py:461
  196.8 10.5 %collective-permute-start.39 = (bf16[80,512]{1,0:T(8,128)(2,1)S(1)}, bf16[80,512]{1,0:T(8,128)(2,1)S(1)}, u32[]{:S(2)}, u32[]{:S(2)}) collective-permute-start(bf16[80,512]{1,0:T(8,128)(2,1)S(1)} %get-tuple-element.242), channel_id=1, source_target_pairs={{0,16},{2,18},{4,20},{6,22},{8,24},{10,26},{12,28},{14,30},{16,0},... | collective-permute-start | bytes 245768 | tf_op jit(solution)/shard_map/ppermute | solution.py:461
  198.9 8.4 %collective-permute-start.40 = (bf16[80,512]{1,0:T(8,128)(2,1)S(1)}, bf16[80,512]{1,0:T(8,128)(2,1)S(1)}, u32[]{:S(2)}, u32[]{:S(2)}) collective-permute-start(bf16[80,512]{1,0:T(8,128)(2,1)S(1)} %get-tuple-element.241), channel_id=1, source_target_pairs={{0,24},{2,26},{4,28},{6,30},{8,16},{10,18},{12,20},{14,22},{16,8},... | collective-permute-start | bytes 245768 | tf_op jit(solution)/shard_map/ppermute | solution.py:461
  200.3 7.0 %collective-permute-start.37 = (bf16[48,640]{1,0:T(8,128)(2,1)S(1)}, bf16[48,640]{1,0:T(8,128)(2,1)S(1)}, u32[]{:S(2)}, u32[]{:S(2)}) collective-permute-start(bf16[48,640]{1,0:T(8,128)(2,1)S(1)} %get-tuple-element.249), channel_id=1, source_target_pairs={{0,16},{2,18},{4,20},{6,22},{8,24},{10,26},{12,28},{14,30},{16,0},... | collective-permute-start | bytes 184328 | tf_op jit(solution)/shard_map/ppermute | solution.py:461
  (25 other events, 76.5 us)

commit v2 on v1

--- a/solution.py
+++ b/solution.py
@@ -8,6 +8,7 @@
 from jax.sharding import PartitionSpec as P
 
 LEN = 1024
+LOG2E = 1.4426950408889634
 Q = 128
 HEAD = 64
 STATE = 128
@@ -92,7 +93,7 @@
     step = softplus(dt_raw + heads_ref[0:1, :])
     decay = -step * heads_ref[1:2, :]
     sums = nn(low_tri, split_low(decay, 3))
-    cum = sums[:, :Q] + sums[:, Q : 2 * Q] + sums[:, 2 * Q :]
+    cum = (sums[:, :Q] + sums[:, Q : 2 * Q] + sums[:, 2 * Q :]) * LOG2E
     return step, decay, cum
 
 
@@ -146,18 +147,18 @@
         scaled = x * step2
         c0 = jnp.broadcast_to(cum[:, 2 * p : 2 * p + 1], (Q, Q))
         c1 = jnp.broadcast_to(cum[:, 2 * p + 1 : 2 * p + 2], (Q, Q))
-        w0 = jnp.exp(jnp.minimum(c0 - cum_rows[2 * p : 2 * p + 1, :], 0.0)) * gram
-        w1 = jnp.exp(jnp.minimum(c1 - cum_rows[2 * p + 1 : 2 * p + 2, :], 0.0)) * gram
+        w0 = jnp.exp2(jnp.minimum(c0 - cum_rows[2 * p : 2 * p + 1, :], 0.0)) * gram
+        w1 = jnp.exp2(jnp.minimum(c1 - cum_rows[2 * p + 1 : 2 * p + 2, :], 0.0)) * gram
         weights = jnp.concatenate([w0.astype(b16), w1.astype(b16)], axis=1)
         split = jnp.concatenate(
             [jnp.where(left, scaled, 0.0).astype(b16), jnp.where(left, 0.0, scaled).astype(b16)], axis=0
         )
         both = jnp.where(left, c0, c1)
-        rise = jnp.exp(both)
+        rise = jnp.exp2(both)
         here = carried[:, (p % 2) * Q : (p % 2 + 1) * Q]
         y = nn(weights, split) + here * rise + cx_ref[5:6, sl] * x
         y_ref[:, sl] = y.astype(b16)
-        leaving.append((scaled * jnp.exp(both[Q - 1 : Q, :] - both)).astype(b16))
+        leaving.append((scaled * jnp.exp2(both[Q - 1 : Q, :] - both)).astype(b16))
         rises.append(rise[Q - 1 : Q, :])
         if p % 2 == 1:
             added = nn(b_turned, jnp.concatenate(leaving[-2:], axis=1))
@@ -243,6 +244,7 @@
     bc = pre_bc * sig_bc
     b_low, c_low = bc[:, :STATE].astype(b16), bc[:, STATE:].astype(b16)
     gram = jnp.where(upper, nt(b_low, c_low), 0.0)
+    gram_low = gram.astype(b16)
     raw = bd_ref[:, 2 * STATE :]
     step, cum = rates_ref[:, :Q], rates_ref[:, Q:]
     cum_rows = cum.T
@@ -277,8 +279,8 @@
         weights, crossing = [], []
         for half, column in ((0, c0), (1, c1)):
             head = 2 * p + half
-            fade = jnp.exp(jnp.minimum(cum_rows[head : head + 1, :] - column, 0.0))
-            weights.append((fade * gram).astype(b16))
+            fade = jnp.exp2(jnp.minimum(cum_rows[head : head + 1, :] - column, 0.0))
+            weights.append(fade.astype(b16) * gram_low)
             faded = dweights[:, half * Q : (half + 1) * Q] * fade
             dgram = dgram + faded
             crossing.append((faded * gram).astype(b16))
@@ -288,8 +290,8 @@
         row_sums[2 * p + 1 : 2 * p + 2, :] = over_rows[0:1, Q:]
         col_sums = col_sums + nn(crossing, jnp.where(lane_of == 2 * p + half_of, 1.0, 0.0).astype(b16))
         both = jnp.where(left, c0, c1)
-        tail = jnp.exp(both[Q - 1 : Q, :] - both)
-        rise = jnp.exp(both)
+        tail = jnp.exp2(both[Q - 1 : Q, :] - both)
+        rise = jnp.exp2(both)
         dx_state = back_two[:, half_lanes] * tail
         dscaled = nn(jnp.concatenate(weights, axis=1), split) + dx_state
         dye_here = dy * rise
@@ -325,7 +327,7 @@
     low = (inner_states - high.astype(f32)).astype(b16)
     both_states = jnp.concatenate([jnp.broadcast_to(high, (8, high.shape[1])), jnp.broadcast_to(low, (8, low.shape[1]))], axis=0)
     state_sums = nn(both_states, pick)
-    constant = jnp.exp(total) * (state_sums[0:1, :] + state_sums[8:9, :])
+    constant = jnp.exp2(total) * (state_sums[0:1, :] + state_sums[8:9, :])
     up_tri = jnp.where(upper, 1.0, 0.0).astype(b16)
     strict = jnp.where(rows > cols, 1.0, 0.0).astype(b16)
     moved = jnp.concatenate([summed[:Q] - col_sums + row_sums[...].T, summed[Q : 2 * Q]], axis=0)
@@ -450,7 +452,7 @@
         out_specs=[tall(inner)] * 3 + [fixed((8, inner))],
         out_shape=[jax.ShapeDtypeStruct((rows, inner), b16)] * 3 + [jax.ShapeDtypeStruct((8, inner), f32)],
         scratch_shapes=[pltpu.VMEM((size, inner), f32)] * 3,
-        compiler_params=pltpu.CompilerParams(vmem_limit_bytes=56 * MIB),
+        compiler_params=pltpu.CompilerParams(vmem_limit_bytes=44 * MIB),
         cost_estimate=pl.CostEstimate(flops=rows * inner * 8000, bytes_accessed=rows * inner * 10, transcendentals=rows * inner * 2),
         name="gate_both",
     )(y, normed, cot, w_z, w_out_t, gain)
@@ -926,6 +928,7 @@
     first_layout = ((0, half), (half, STATE), (half + STATE, 128))
     second_layout = ((0, half), (half, half))
     gain_row = pre_gain.astype(f32)[None]
+    pick = (jnp.arange(inner)[:, None] // HEAD == jnp.arange(Q)[None, :]).astype(b16)
     if quick:
         column = along_z(first)
         tokens, cotangent, _ = lax.optimization_barrier((tokens, cotangent, column))
@@ -933,7 +936,7 @@
     if quick:
         mine_first = around(column)
         later = along_z(tie(second, column))
-        mine_first[3], *ready = lax.optimization_barrier((mine_first[3], *ready))
+        mine_first[3], pick, *ready = lax.optimization_barrier((mine_first[3], pick, *ready))
         other_first = [swap(part, 1, "tensor") for part in mine_first]
         mine_second = around(tie(later, *mine_first))
         w_x, full_bc, full_dt = merge(where, mine_first, other_first, first_layout)
@@ -961,7 +964,6 @@
     heads = jnp.pad(
         jnp.stack([per_head[1], jnp.exp(per_head[0])]), ((0, 6), (0, Q - heads_count))
     )
-    pick = (jnp.arange(inner)[:, None] // HEAD == jnp.arange(Q)[None, :]).astype(b16)
 
     w_s = jnp.concatenate([full_bc, full_dt[:, :128] + full_dt[:, 128:]], axis=1)
     x, cotangent, normed, normed_t, cot_t = ready

time: 210 us -> 203 us (0.967)
  local copies, waits for them, and re-layouts: 18 us -> 14.1 us
  other arithmetic: 12.5 us -> 10.2 us
    unnamed x68 -> x66, local copies, waits for them, and re-layouts: 12.4 us -> 9.12 us
  transfers between devices with their start and end apart: 41 -> 41, of which waited for: 9 -> 11; matrix products, arithmetic and copies ran while one was open for 9% -> 7% of each run, Pallas kernels for 42% -> 43%
where the time goes in v2:
time: 203 us
  Pallas kernels  109 us (54%)
  starting transfers between devices  41.1 us (20%)
  waiting for transfers between devices  20.9 us (10%)
  local copies, waits for them, and re-layouts  14.1 us (7%)
  other arithmetic  10.2 us (5%)
  matrix products  6.14 us (3%)
    ppermute x41, starting transfers between devices, swap(): return lax.ppermute(value, axis, [(i, i ^ bit) for i in range(count)])  41.1 us
    pallas_call x2, Pallas kernels, scan_backward(): pl.pallas_call(functools.partial(scan_backward_kernel, per_seq, pairs, ba...  35.7 us
    ppermute x41, waiting for transfers between devices, swap(): return lax.ppermute(value, axis, [(i, i ^ bit) for i in range(count)])  20.9 us
    pallas_call x2, Pallas kernels, scan_forward(): pl.pallas_call(functools.partial(scan_forward_kernel, per_seq, pairs, bas...  18.6 us
    pallas_call x1, Pallas kernels, gate_both(): pl.pallas_call(gate_kernel, grid=(rows // size,), in_specs=[tall(inner),...  12.3 us
    pallas_call x1, Pallas kernels, token_grads(): pl.pallas_call(token_grads_kernel, grid=(rows // 256,), in_specs=[tall(v)...  9.32 us
    unnamed x66, local copies, waits for them, and re-layouts  9.12 us
    pallas_call x2, Pallas kernels, pack_whole(): pl.pallas_call(functools.partial(pack_whole_kernel, rows, bool(weights)),...  9.12 us
  transfers between devices with their start and end apart: 41, of which 11 were waited for; matrix products, arithmetic and copies ran while one was open for 7% of the time, Pallas kernels for 43%

profile of v2, /device:TPU:0, one launch (start us, length us, event | category | flops | bytes accessed | tf_op | source)
XLA Modules:
  0.0 202.6 jit_solution(7291232716058858946)
XLA Ops:
  1.5 1.2 fusion.16
  3.0 3.1 %collective-permute-start = (bf16[48,1024]{1,0:T(8,128)(2,1)S(1)}, bf16[48,1024]{1,0:T(8,128)(2,1)S(1)}, u32[]{:S(2)}, u32[]{:S(2)}) collective-permute-start(bf16[48,1024]{1,0:T(8,128)(2,1)S(1)} %get-tuple-element.254), channel_id=1, source_target_pairs={{0,8},{2,10},{4,12},{6,14},{8,0},{10,2},{12,4},{14,6},{16,24},{18,... | collective-permute-start | bytes 294920 | tf_op jit(solution)/shard_map/ppermute | solution.py:463
  6.1 2.6 %collective-permute-start.1 = (bf16[48,1024]{1,0:T(8,128)(2,1)S(1)}, bf16[48,1024]{1,0:T(8,128)(2,1)S(1)}, u32[]{:S(2)}, u32[]{:S(2)}) collective-permute-start(bf16[48,1024]{1,0:T(8,128)(2,1)S(1)} %get-tuple-element.254), channel_id=1, source_target_pairs={{0,16},{2,18},{4,20},{6,22},{8,24},{10,26},{12,28},{14,30},{16,0},... | collective-permute-start | bytes 294920 | tf_op jit(solution)/shard_map/ppermute | solution.py:463
  13.9 2.9 %collective-permute-done.1 = bf16[48,1024]{1,0:T(8,128)(2,1)S(1)} collective-permute-done((bf16[48,1024]{1,0:T(8,128)(2,1)S(1)}, bf16[48,1024]{1,0:T(8,128)(2,1)S(1)}, u32[]{:S(2)}, u32[]{:S(2)}) %collective-permute-start.1) | collective-permute-done | bytes 98336 | tf_op jit(solution)/shard_map/ppermute | solution.py:463
  16.8 2.5 %collective-permute-start.3 = (bf16[4,48,1024]{2,1,0:T(8,128)(2,1)S(1)}, bf16[4,48,1024]{2,1,0:T(8,128)(2,1)S(1)}, u32[]{:S(2)}, u32[]{:S(2)}) collective-permute-start(bf16[4,48,1024]{2,1,0:T(8,128)(2,1)S(1)} %pad_maximum_fusion.2.refs_0_), channel_id=1, source_target_pairs={{0,6},{2,4},{4,2},{6,0},{8,14},{10,12},{12,10},{14,8},{16,22},{18,... | collective-permute-start | bytes 1179656 | tf_op jit(solution)/shard_map/ppermute | solution.py:463
  20.4 1.6 collective-permute-start.11
  22.0 1.4 collective-permute-start.12
  23.4 8.2 %prepare.1 = (bf16[1024,768]{1,0:T(8,128)(2,1)}, bf16[1024,768]{1,0:T(8,128)(2,1)}, bf16[1024,768]{1,0:T(8,128)(2,1)}, bf16[768,1024]{1,0:T(8,128)(2,1)}, bf16[768,1024]{1,0:T(8,128)(2,1)}) custom-call(bf16[1024,768]{1,0:T(8,128)(2,1)} %tokens, bf16[1024,768]{1,0:T(8,128)(2,1)} %cot, f32[1,768]{1,0:T(1,128)} %reshape.106.gain.gain_pre), custom_call_target="tpu_custom_call" | custom-call | tf_op jit(solution)/shard_map/prepare/pallas_call | solution.py:840
  31.7 1.4 collective-permute-start.13
  33.3 2.2 %collective-permute-done.4.refs_1_ = bf16[4,48,1024]{2,1,0:T(8,128)(2,1)S(1)} collective-permute-done((bf16[4,48,1024]{2,1,0:T(8,128)(2,1)S(1)}, bf16[4,48,1024]{2,1,0:T(8,128)(2,1)S(1)}, u32[]{:S(2)}, u32[]{:S(2)}) %collective-permute-start.4) | collective-permute-done | bytes 393248 | tf_op jit(solution)/shard_map/ppermute | solution.py:463
  37.4 2.6 %collective-permute-done.13 = bf16[48,1536]{1,0:T(8,128)(2,1)} collective-permute-done((bf16[48,1536]{1,0:T(8,128)(2,1)S(1)}, bf16[48,1536]{1,0:T(8,128)(2,1)}, u32[]{:S(2)}, u32[]{:S(2)}) %collective-permute-start.13) | collective-permute-done | bytes 147488 | tf_op jit(solution)/shard_map/ppermute | solution.py:463
  41.0 1.6 collective-permute-start.14
  42.6 1.5 collective-permute-start.15
  47.7 4.0 %convolution_convert_fusion.refs_0_.refs_1_ = bf16[1024,1536]{1,0:T(8,128)(2,1)} fusion(bf16[1024,768]{1,0:T(8,128)(2,1)S(1)} %copy-done.20, bf16[768,1536]{1,0:T(8,128)(2,1)S(1)} %get-tuple-element.130.w_x), kind=kOutput, calls=%fused_computation | convolution fusion | flops 2417491968 | bytes 7077888 | tf_op jit(solution)/shard_map/dot_general | solution.py:23
  51.8 2.1 %fusion.15.refs_2_.refs_3_.refs_4_ = f32[1024,384]{1,0:T(8,128)} fusion(bf16[1024,768]{1,0:T(8,128)(2,1)S(1)} %copy-done.20, bf16[768,128]{1,0:T(8,128)(2,1)S(1)} %slice_add_fusion, bf16[768,256]{1,0:T(8,128)(2,1)S(1)} %get-tuple-element.131), kind=kOutput, calls=%fused_computation.85 | convolution fusion | flops 605159424 | bytes 3735552 | tf_op jit(solution)/shard_map/dot_general | solution.py:23
  53.9 12.6 %scan_forward.2 = (bf16[1024,1536]{1,0:T(8,128)(2,1)}, bf16[8,128,1536]{2,1,0:T(8,128)(2,1)}, bf16[1024,1536]{1,0:T(8,128)(2,1)}, f32[1024,256]{1,0:T(8,128)}, f32[128,1536]{1,0:T(8,128)}) custom-call(bf16[1024,1536]{1,0:T(8,128)(2,1)} %convolution_convert_fusion.refs_0_.refs_1_, bf16[1024,1536]{1,0:T(8,128)(2,1)} %convolution_convert_fusion.refs_0_.refs_1_, ...), custom_call_target="tpu_custom_call" | custom-call | flops 7077888000 | bytes 9437184 | tf_op jit(solution)/shard_map/scan_forward/pallas_call | solution.py:173
  66.5 3.3 %collective-permute-done.15.refs_2_ = bf16[4,48,1536]{2,1,0:T(8,128)(2,1)S(1)} collective-permute-done((bf16[4,48,1536]{2,1,0:T(8,128)(2,1)S(1)}, bf16[4,48,1536]{2,1,0:T(8,128)(2,1)S(1)}, u32[]{:S(2)}, u32[]{:S(2)}) %collective-permute-start.15) | collective-permute-done | bytes 589856 | tf_op jit(solution)/shard_map/ppermute | solution.py:463
  70.8 6.0 %scan_forward.3 = (bf16[1024,1536]{1,0:T(8,128)(2,1)}, bf16[8,128,1536]{2,1,0:T(8,128)(2,1)}, bf16[1024,1536]{1,0:T(8,128)(2,1)}, f32[1024,256]{1,0:T(8,128)}, f32[128,1536]{1,0:T(8,128)}) custom-call(bf16[1024,1536]{1,0:T(8,128)(2,1)} %convolution_convert_fusion.refs_0_.refs_1_, ...), custom_call_target="tpu_custom_call", output_to_operand_aliasing={{0}: (8, {}), {1}: (9, {}), {2}: (10, {}), {3}: (11, {})} | custom-call | flops 2359296000 | bytes 3145728 | tf_op jit(solution)/shard_map/scan_forward/pallas_call | solution.py:173
  78.7 12.3 %gate_both.1 = (bf16[1024,1536]{1,0:T(8,128)(2,1)}, bf16[1024,1536]{1,0:T(8,128)(2,1)}, bf16[1024,1536]{1,0:T(8,128)(2,1)}, f32[8,1536]{1,0:T(8,128)S(1)}) custom-call(bf16[1024,1536]{1,0:T(8,128)(2,1)} %get-tuple-element.141.y, bf16[1024,768]{1,0:T(8,128)(2,1)S(1)} %copy-done.21, bf16[1024,768]{1,0:T(8,128)(2,1)S(1)} %copy-done.17, ...), custom_call_target="tpu_custom_call" | custom-call | flops 12582912000 | bytes 15728640 | tf_op jit(solution)/shard_map/gate_both/pallas_call | solution.py:448
  91.0 1.9 copy-done.22
  92.9 3.6 %pack_whole.2 = (bf16[4,192,768]{2,1,0:T(8,128)(2,1)S(1)}, bf16[4,192,768]{2,1,0:T(8,128)(2,1)S(1)}) custom-call(s32[2]{0:T(128)S(1)} %pad_add_fusion.where_ref.side_ref, bf16[768,1024]{1,0:T(8,128)(2,1)S(1)} %copy-done.19, bf16[1024,1536]{1,0:T(8,128)(2,1)S(1)} %copy-done.22), custom_call_target="tpu_custom_call" | custom-call | flops 4831838208 | bytes 6291456 | tf_op jit(solution)/shard_map/pack_whole/pallas_call | solution.py:568
  96.7 5.5 %pack_whole.3 = (bf16[4,192,768]{2,1,0:T(8,128)(2,1)S(1)}, bf16[4,192,768]{2,1,0:T(8,128)(2,1)}, f32[768,128]{1,0:T(8,128)S(1)}) custom-call(s32[2]{0:T(128)S(1)} %pad_add_fusion.where_ref.side_ref, bf16[768,1024]{1,0:T(8,128)(2,1)S(1)} %copy-done.4, bf16[1024,1536]{1,0:T(8,128)(2,1)S(1)} %copy-done.24, bf16[768,1536]{1,0:T(8,128)(2,1)S(1)} %get-tuple-element.151.w_z.refs_0_), custom_call_target="tpu_custom_call" | custom-call | flops 4831838208 | bytes 6291456 | tf_op jit(solution)/shard_map/pack_whole/pallas_call | solution.py:568
  102.2 1.3 add_convert_fusion.1
  104.0 10.1 %scan_backward.2 = (bf16[1024,1536]{1,0:T(8,128)(2,1)}, bf16[1024,384]{1,0:T(8,128)(2,1)}, f32[128,1536]{1,0:T(8,128)}, f32[24,1536]{1,0:T(8,128)}, f32[24,256]{...) custom-call(bf16[1024,1536]{1,0:T(8,128)(2,1)} %get-tuple-element.165.refs_0_, ...), custom_call_target="tpu_custom_call" | custom-call | flops 4718592000 | bytes 3932160 | tf_op jit(solution)/shard_map/scan_backward/pallas_call | solution.py:363
  114.6 1.2 copy-done.26
  115.8 1.2 slice_bitcast_fusion.2
  117.0 1.2 collective-permute-start.23
  119.1 1.4 collective-permute-start.25
  120.5 25.6 %scan_backward.3 = (bf16[1024,1536]{1,0:T(8,128)(2,1)}, bf16[1024,384]{1,0:T(8,128)(2,1)}, f32[128,1536]{1,0:T(8,128)}, f32[24,1536]{1,0:T(8,128)}, f32[24,256]{...) custom-call(bf16[1024,1536]{1,0:T(8,128)(2,1)} %get-tuple-element.16, ...), custom_call_target="tpu_custom_call", output_to_operand_aliasing={{0}: (17, {}), {1}: (18, {})} | custom-call | flops 14155776000 | bytes 11796480 | tf_op jit(solution)/shard_map/scan_backward/pallas_call | solution.py:363
  146.2 1.8 fusion.2
  148.1 1.9 copy-done.2
  149.9 3.0 %pack_first.1 = (bf16[4,192,640]{2,1,0:T(8,128)(2,1)S(1)}, bf16[4,192,640]{2,1,0:T(8,128)(2,1)S(1)}, f32[768,128]{1,0:T(8,128)S(1)}) custom-call(s32[2]{0:T(128)S(1)} %pad_add_fusion.where_ref.side_ref, bf16[768,1024]{1,0:T(8,128)(2,1)S(1)} %copy-done.4, bf16[1024,1536]{1,0:T(8,128)(2,1)S(1)} %copy-done.2, bf16[1024,384]{1,0:T(8,128)(2,1)S(1)} %copy-done.5, ...), custom_call_target="tpu_custom_call" | custom-call | flops 1409286144 | bytes 1048576 | tf_op jit(solution)/shard_map/pack_first/pallas_call | solution.py:616
  153.2 3.0 %collective-permute-start.31 = (bf16[2,48,1536]{2,1,0:T(8,128)(2,1)S(1)}, bf16[2,48,1536]{2,1,0:T(8,128)(2,1)S(1)}, u32[]{:S(2)}, u32[]{:S(2)}) collective-permute-start(bf16[2,48,1536]{2,1,0:T(8,128)(2,1)S(1)} %get-tuple-element.241), channel_id=1, source_target_pairs={{0,8},{2,10},{4,12},{6,14},{8,0},{10,2},{12,4},{14,6},{16,24},{18,... | collective-permute-start | bytes 884744 | tf_op jit(solution)/shard_map/ppermute | solution.py:463
  156.2 3.7 %pack_second.1 = (bf16[4,224,512]{2,1,0:T(8,128)(2,1)S(1)}, bf16[4,224,512]{2,1,0:T(8,128)(2,1)S(1)}) custom-call(s32[2]{0:T(128)S(1)} %pad_add_fusion.where_ref.side_ref, bf16[768,1024]{1,0:T(8,128)(2,1)S(1)} %copy-done.4, bf16[1024,1536]{1,0:T(8,128)(2,1)S(1)} %copy-done.3, bf16[768,1536]{1,0:T(8,128)(2,1)S(1)} %get-tuple-element.130.w_x, ...), custom_call_target="tpu_custom_call" | custom-call | flops 1610612736 | bytes 2097152 | tf_op jit(solution)/shard_map/pack_second/pallas_call | solution.py:691
  160.6 1.2 collective-permute-start.27
  161.8 1.1 collective-permute-start.28
  162.9 1.2 collective-permute-start.29
  164.1 9.3 %token_grads.1 = bf16[1024,768]{1,0:T(8,128)(2,1)} custom-call(bf16[1024,1536]{1,0:T(8,128)(2,1)S(1)} %copy-done.25, bf16[1024,1536]{1,0:T(8,128)(2,1)S(1)} %copy-done.3, bf16[1024,384]{1,0:T(8,128)(2,1)S(1)} %copy-done.5, bf16[1024,768]{1,0:T(8,128)(2,1)S(1)} %copy-done.16, bf16[1024,768]{1,0:T(8,128)(2,1)S(1)} %copy-done.18, ...), custom_call_target="tpu_custom_call" | custom-call | flops 6291456000 | bytes 15728640 | tf_op jit(solution)/shard_map/token_grads/pallas_call | solution.py:872
  173.6 1.4 collective-permute-done.29
  176.2 1.4 collective-permute-start.35
  178.6 1.5 collective-permute-start.33
  180.0 1.2 collective-permute-start.34
  181.9 4.4 %collective-permute-done.32 = bf16[224,512]{1,0:T(8,128)(2,1)S(1)} collective-permute-done((bf16[224,512]{1,0:T(8,128)(2,1)S(1)}, bf16[224,512]{1,0:T(8,128)(2,1)S(1)}, u32[]{:S(2)}, u32[]{:S(2)}) %collective-permute-start.32) | collective-permute-done | bytes 229408 | tf_op jit(solution)/shard_map/ppermute | solution.py:463
  186.2 3.3 %collective-permute-done.33 = bf16[224,512]{1,0:T(8,128)(2,1)S(1)} collective-permute-done((bf16[224,512]{1,0:T(8,128)(2,1)S(1)}, bf16[224,512]{1,0:T(8,128)(2,1)S(1)}, u32[]{:S(2)}, u32[]{:S(2)}) %collective-permute-start.33) | collective-permute-done | bytes 229408 | tf_op jit(solution)/shard_map/ppermute | solution.py:463
  190.8 2.1 %collective-permute-start.39 = (bf16[80,512]{1,0:T(8,128)(2,1)S(1)}, bf16[80,512]{1,0:T(8,128)(2,1)S(1)}, u32[]{:S(2)}, u32[]{:S(2)}) collective-permute-start(bf16[80,512]{1,0:T(8,128)(2,1)S(1)} %get-tuple-element.244), channel_id=1, source_target_pairs={{0,16},{2,18},{4,20},{6,22},{8,24},{10,26},{12,28},{14,30},{16,0},... | collective-permute-start | bytes 245768 | tf_op jit(solution)/shard_map/ppermute | solution.py:463
  192.9 1.4 collective-permute-start.40
  195.3 5.5 %add_branch.1 = bf16[1024,768]{1,0:T(8,128)(2,1)} custom-call(bf16[1024,1536]{1,0:T(8,128)(2,1)S(1)} %copy-done.23, bf16[1024,768]{1,0:T(8,128)(2,1)S(1)} %copy-done.16, bf16[768,1536]{1,0:T(8,128)(2,1)S(1)} %copy-done.13), custom_call_target="tpu_custom_call" | custom-call | flops 3145728000 | bytes 7864320 | tf_op jit(solution)/shard_map/add_branch/pallas_call | solution.py:891
  200.9 1.5 finish.1
  (177 shorter events, 25.0 us)
Async XLA Ops:
  0.7 12.0 %copy-start.28 = (bf16[768,48]{0,1:T(8,128)(2,1)S(1)}, bf16[768,48]{0,1:T(8,128)(2,1)}, u32[]{:S(2)}) copy-start(bf16[768,48]{0,1:T(8,128)(2,1)} %param.24) | copy-start | bytes 221188
  0.7 12.1 %copy-start.30 = (bf16[768]{0:T(1024)(128)(2,1)S(1)}, bf16[768]{0:T(1024)(128)(2,1)}, u32[]{:S(2)}) copy-start(bf16[768]{0:T(1024)(128)(2,1)} %param.14) | copy-start | bytes 4612
  3.0 10.9 %collective-permute-start = (bf16[48,1024]{1,0:T(8,128)(2,1)S(1)}, bf16[48,1024]{1,0:T(8,128)(2,1)S(1)}, u32[]{:S(2)}, u32[]{:S(2)}) collective-permute-start(bf16[48,1024]{1,0:T(8,128)(2,1)S(1)} %get-tuple-element.254), channel_id=1, source_target_pairs={{0,8},{2,10},{4,12},{6,14},{8,0},{10,2},{12,4},{14,6},{16,24},{18,... | collective-permute-start | bytes 294920 | tf_op jit(solution)/shard_map/ppermute | solution.py:463
  6.1 10.6 %collective-permute-start.1 = (bf16[48,1024]{1,0:T(8,128)(2,1)S(1)}, bf16[48,1024]{1,0:T(8,128)(2,1)S(1)}, u32[]{:S(2)}, u32[]{:S(2)}) collective-permute-start(bf16[48,1024]{1,0:T(8,128)(2,1)S(1)} %get-tuple-element.254), channel_id=1, source_target_pairs={{0,16},{2,18},{4,20},{6,22},{8,24},{10,26},{12,28},{14,30},{16,0},... | collective-permute-start | bytes 294920 | tf_op jit(solution)/shard_map/ppermute | solution.py:463
  8.7 8.0 %collective-permute-start.2 = (bf16[48,1024]{1,0:T(8,128)(2,1)S(1)}, bf16[48,1024]{1,0:T(8,128)(2,1)S(1)}, u32[]{:S(2)}, u32[]{:S(2)}) collective-permute-start(bf16[48,1024]{1,0:T(8,128)(2,1)S(1)} %get-tuple-element.254), channel_id=1, source_target_pairs={{0,24},{2,26},{4,28},{6,30},{8,16},{10,18},{12,20},{14,22},{16,8},... | collective-permute-start | bytes 294920 | tf_op jit(solution)/shard_map/ppermute | solution.py:463
  11.0 2.5 %collective-permute-start.10 = (f32[1,8,768]{2,1,0:T(8,128)S(1)}, f32[1,8,768]{2,1,0:T(8,128)S(1)}, u32[]{:S(2)}, u32[]{:S(2)}) collective-permute-start(f32[1,8,768]{2,1,0:T(8,128)S(1)} %maximum_bitcast_fusion), channel_id=1, source_target_pairs={{0,1},{1,0},{2,3},{3,2},{4,5},{5,4},{6,7},{7,6},{8,9},{9,8},{10,11... | collective-permute-start | bytes 73736 | tf_op jit(solution)/shard_map/ppermute | solution.py:463
  16.8 14.8 %collective-permute-start.3 = (bf16[4,48,1024]{2,1,0:T(8,128)(2,1)S(1)}, bf16[4,48,1024]{2,1,0:T(8,128)(2,1)S(1)}, u32[]{:S(2)}, u32[]{:S(2)}) collective-permute-start(bf16[4,48,1024]{2,1,0:T(8,128)(2,1)S(1)} %pad_maximum_fusion.2.refs_0_), channel_id=1, source_target_pairs={{0,6},{2,4},{4,2},{6,0},{8,14},{10,12},{12,10},{14,8},{16,22},{18,... | collective-permute-start | bytes 1179656 | tf_op jit(solution)/shard_map/ppermute | solution.py:463
  19.3 16.1 %collective-permute-start.4 = (bf16[4,48,1024]{2,1,0:T(8,128)(2,1)S(1)}, bf16[4,48,1024]{2,1,0:T(8,128)(2,1)S(1)}, u32[]{:S(2)}, u32[]{:S(2)}) collective-permute-start(bf16[4,48,1024]{2,1,0:T(8,128)(2,1)S(1)} %pad_maximum_fusion.2.refs_0_), channel_id=1, source_target_pairs={{0,2},{2,0},{4,6},{6,4},{8,10},{10,8},{12,14},{14,12},{16,18},{18,... | collective-permute-start | bytes 1179656 | tf_op jit(solution)/shard_map/ppermute | solution.py:463
  19.8 15.6 %collective-permute-start.5 = (bf16[4,48,1024]{2,1,0:T(8,128)(2,1)S(1)}, bf16[4,48,1024]{2,1,0:T(8,128)(2,1)S(1)}, u32[]{:S(2)}, u32[]{:S(2)}) collective-permute-start(bf16[4,48,1024]{2,1,0:T(8,128)(2,1)S(1)} %pad_maximum_fusion.2.refs_0_), channel_id=1, source_target_pairs={{0,4},{2,6},{4,0},{6,2},{8,12},{10,14},{12,8},{14,10},{16,20},{18,... | collective-permute-start | bytes 1179656 | tf_op jit(solution)/shard_map/ppermute | solution.py:463
  20.4 11.3 %collective-permute-start.11 = (bf16[48,1536]{1,0:T(8,128)(2,1)S(1)}, bf16[48,1536]{1,0:T(8,128)(2,1)S(1)}, u32[]{:S(2)}, u32[]{:S(2)}) collective-permute-start(bf16[48,1536]{1,0:T(8,128)(2,1)S(1)} %pad_maximum_fusion.4), channel_id=1, source_target_pairs={{0,8},{2,10},{4,12},{6,14},{8,0},{10,2},{12,4},{14,6},{16,24},{18,... | collective-permute-start | bytes 442376 | tf_op jit(solution)/shard_map/ppermute | solution.py:463
  22.0 11.1 %collective-permute-start.12 = (bf16[48,1536]{1,0:T(8,128)(2,1)S(1)}, bf16[48,1536]{1,0:T(8,128)(2,1)}, u32[]{:S(2)}, u32[]{:S(2)}) collective-permute-start(bf16[48,1536]{1,0:T(8,128)(2,1)S(1)} %pad_maximum_fusion.4), channel_id=1, source_target_pairs={{0,16},{2,18},{4,20},{6,22},{8,24},{10,26},{12,28},{14,30},{16,0},... | collective-permute-start | bytes 442376 | tf_op jit(solution)/shard_map/ppermute | solution.py:463
  31.6 11.0 %collective-permute-start.6 = (bf16[4,48,1024]{2,1,0:T(8,128)(2,1)S(1)}, bf16[4,48,1024]{2,1,0:T(8,128)(2,1)S(1)}, u32[]{:S(2)}, u32[]{:S(2)}) collective-permute-start(bf16[4,48,1024]{2,1,0:T(8,128)(2,1)S(1)} %pad_maximum_fusion.2.refs_0_), channel_id=1, source_target_pairs={{0,1},{1,0},{2,3},{3,2},{4,5},{5,4},{6,7},{7,6},{8,9},{9,8},{10,11... | collective-permute-start | bytes 1179656 | tf_op jit(solution)/shard_map/ppermute | solution.py:463
  31.7 8.3 %collective-permute-start.13 = (bf16[48,1536]{1,0:T(8,128)(2,1)S(1)}, bf16[48,1536]{1,0:T(8,128)(2,1)}, u32[]{:S(2)}, u32[]{:S(2)}) collective-permute-start(bf16[48,1536]{1,0:T(8,128)(2,1)S(1)} %pad_maximum_fusion.4), channel_id=1, source_target_pairs={{0,24},{2,26},{4,28},{6,30},{8,16},{10,18},{12,20},{14,22},{16,8},... | collective-permute-start | bytes 442376 | tf_op jit(solution)/shard_map/ppermute | solution.py:463
  33.1 11.0 %collective-permute-start.9 = (bf16[4,48,1024]{2,1,0:T(8,128)(2,1)S(1)}, bf16[4,48,1024]{2,1,0:T(8,128)(2,1)S(1)}, u32[]{:S(2)}, u32[]{:S(2)}) collective-permute-start(bf16[4,48,1024]{2,1,0:T(8,128)(2,1)S(1)} %collective-permute-done.3.refs_3_), channel_id=1, source_target_pairs={{0,1},{1,0},{2,3},{3,2},{4,5},{5,4},{6,7},{7,6},{8,9},{9,8},{10,11... | collective-permute-start | bytes 1179656 | tf_op jit(solution)/shard_map/ppermute | solution.py:463
  35.4 9.2 %collective-permute-start.7 = (bf16[4,48,1024]{2,1,0:T(8,128)(2,1)S(1)}, bf16[4,48,1024]{2,1,0:T(8,128)(2,1)S(1)}, u32[]{:S(2)}, u32[]{:S(2)}) collective-permute-start(bf16[4,48,1024]{2,1,0:T(8,128)(2,1)S(1)} %collective-permute-done.4.refs_1_), channel_id=1, source_target_pairs={{0,1},{1,0},{2,3},{3,2},{4,5},{5,4},{6,7},{7,6},{8,9},{9,8},{10,11... | collective-permute-start | bytes 1179656 | tf_op jit(solution)/shard_map/ppermute | solution.py:463
  35.4 9.2 %collective-permute-start.8 = (bf16[4,48,1024]{2,1,0:T(8,128)(2,1)S(1)}, bf16[4,48,1024]{2,1,0:T(8,128)(2,1)S(1)}, u32[]{:S(2)}, u32[]{:S(2)}) collective-permute-start(bf16[4,48,1024]{2,1,0:T(8,128)(2,1)S(1)} %collective-permute-done.5.refs_2_), channel_id=1, source_target_pairs={{0,1},{1,0},{2,3},{3,2},{4,5},{5,4},{6,7},{7,6},{8,9},{9,8},{10,11... | collective-permute-start | bytes 1179656 | tf_op jit(solution)/shard_map/ppermute | solution.py:463
  41.0 25.5 %collective-permute-start.14 = (bf16[4,48,1536]{2,1,0:T(8,128)(2,1)S(1)}, bf16[4,48,1536]{2,1,0:T(8,128)(2,1)S(1)}, u32[]{:S(2)}, u32[]{:S(2)}) collective-permute-start(bf16[4,48,1536]{2,1,0:T(8,128)(2,1)S(1)} %pad_maximum_fusion.1.refs_0_), channel_id=1, source_target_pairs={{0,2},{2,0},{4,6},{6,4},{8,10},{10,8},{12,14},{14,12},{16,18},{18,... | collective-permute-start | bytes 1769480 | tf_op jit(solution)/shard_map/ppermute | solution.py:463
  42.6 27.2 %collective-permute-start.15 = (bf16[4,48,1536]{2,1,0:T(8,128)(2,1)S(1)}, bf16[4,48,1536]{2,1,0:T(8,128)(2,1)S(1)}, u32[]{:S(2)}, u32[]{:S(2)}) collective-permute-start(bf16[4,48,1536]{2,1,0:T(8,128)(2,1)S(1)} %pad_maximum_fusion.1.refs_0_), channel_id=1, source_target_pairs={{0,4},{2,6},{4,0},{6,2},{8,12},{10,14},{12,8},{14,10},{16,20},{18,... | collective-permute-start | bytes 1769480 | tf_op jit(solution)/shard_map/ppermute | solution.py:463
  44.1 25.7 %collective-permute-start.16 = (bf16[4,48,1536]{2,1,0:T(8,128)(2,1)S(1)}, bf16[4,48,1536]{2,1,0:T(8,128)(2,1)S(1)}, u32[]{:S(2)}, u32[]{:S(2)}) collective-permute-start(bf16[4,48,1536]{2,1,0:T(8,128)(2,1)S(1)} %pad_maximum_fusion.1.refs_0_), channel_id=1, source_target_pairs={{0,6},{2,4},{4,2},{6,0},{8,14},{10,12},{12,10},{14,8},{16,22},{18,... | collective-permute-start | bytes 1769480 | tf_op jit(solution)/shard_map/ppermute | solution.py:463
  69.8 7.1 %collective-permute-start.17 = (bf16[4,48,1536]{2,1,0:T(8,128)(2,1)S(1)}, bf16[4,48,1536]{2,1,0:T(8,128)(2,1)S(1)}, u32[]{:S(2)}, u32[]{:S(2)}) collective-permute-start(bf16[4,48,1536]{2,1,0:T(8,128)(2,1)S(1)} %pad_maximum_fusion.1.refs_0_), channel_id=1, source_target_pairs={{0,1},{1,0},{2,3},{3,2},{4,5},{5,4},{6,7},{7,6},{8,9},{9,8},{10,11... | collective-permute-start | bytes 1769480 | tf_op jit(solution)/shard_map/ppermute | solution.py:463
  69.8 7.1 %collective-permute-start.18 = (bf16[4,48,1536]{2,1,0:T(8,128)(2,1)S(1)}, bf16[4,48,1536]{2,1,0:T(8,128)(2,1)S(1)}, u32[]{:S(2)}, u32[]{:S(2)}) collective-permute-start(bf16[4,48,1536]{2,1,0:T(8,128)(2,1)S(1)} %collective-permute-done.14.refs_1_), channel_id=1, source_target_pairs={{0,1},{1,0},{2,3},{3,2},{4,5},{5,4},{6,7},{7,6},{8,9},{9,8},{10,11... | collective-permute-start | bytes 1769480 | tf_op jit(solution)/shard_map/ppermute | solution.py:463
  70.3 6.6 %collective-permute-start.19 = (bf16[4,48,1536]{2,1,0:T(8,128)(2,1)S(1)}, bf16[4,48,1536]{2,1,0:T(8,128)(2,1)S(1)}, u32[]{:S(2)}, u32[]{:S(2)}) collective-permute-start(bf16[4,48,1536]{2,1,0:T(8,128)(2,1)S(1)} %collective-permute-done.15.refs_2_), channel_id=1, source_target_pairs={{0,1},{1,0},{2,3},{3,2},{4,5},{5,4},{6,7},{7,6},{8,9},{9,8},{10,11... | collective-permute-start | bytes 1769480 | tf_op jit(solution)/shard_map/ppermute | solution.py:463
  70.3 6.6 %collective-permute-start.20 = (bf16[4,48,1536]{2,1,0:T(8,128)(2,1)S(1)}, bf16[4,48,1536]{2,1,0:T(8,128)(2,1)S(1)}, u32[]{:S(2)}, u32[]{:S(2)}) collective-permute-start(bf16[4,48,1536]{2,1,0:T(8,128)(2,1)S(1)} %collective-permute-done.16.refs_3_), channel_id=1, source_target_pairs={{0,1},{1,0},{2,3},{3,2},{4,5},{5,4},{6,7},{7,6},{8,9},{9,8},{10,11... | collective-permute-start | bytes 1769480 | tf_op jit(solution)/shard_map/ppermute | solution.py:463
  77.8 13.2 %copy-start.12 = (bf16[768,1536]{1,0:T(8,128)(2,1)}, bf16[768,1536]{1,0:T(8,128)(2,1)S(1)}, u32[]{:S(2)}) copy-start(bf16[768,1536]{1,0:T(8,128)(2,1)S(1)} %get-tuple-element.152.w_out_t) | copy-start | bytes 7077892
  77.8 18.9 %copy-start.14 = (bf16[768,1536]{1,0:T(8,128)(2,1)}, bf16[768,1536]{1,0:T(8,128)(2,1)S(1)}, u32[]{:S(2)}) copy-start(bf16[768,1536]{1,0:T(8,128)(2,1)S(1)} %get-tuple-element.151.w_z.refs_0_) | copy-start | bytes 7077892
  78.7 12.3 %copy-start.19 = (bf16[768,1024]{1,0:T(8,128)(2,1)S(1)}, bf16[768,1024]{1,0:T(8,128)(2,1)}, u32[]{:S(2)}) copy-start(bf16[768,1024]{1,0:T(8,128)(2,1)} %get-tuple-element.156.left) | copy-start | bytes 4718596
  96.5 5.6 %collective-permute-start.21 = (bf16[4,192,768]{2,1,0:T(8,128)(2,1)S(1)}, bf16[4,192,768]{2,1,0:T(8,128)(2,1)S(1)}, u32[]{:S(2)}, u32[]{:S(2)}) collective-permute-start(bf16[4,192,768]{2,1,0:T(8,128)(2,1)S(1)} %get-tuple-element.164), channel_id=1, source_target_pairs={{0,1},{1,0},{2,3},{3,2},{4,5},{5,4},{6,7},{7,6},{8,9},{9,8},{10,11... | collective-permute-start | bytes 3538952 | tf_op jit(solution)/shard_map/ppermute | solution.py:463
  103.5 10.7 %collective-permute-start.22 = (bf16[4,192,768]{2,1,0:T(8,128)(2,1)}, bf16[4,192,768]{2,1,0:T(8,128)(2,1)S(1)}, u32[]{:S(2)}, u32[]{:S(2)}) collective-permute-start(bf16[4,192,768]{2,1,0:T(8,128)(2,1)} %get-tuple-element.172), channel_id=1, source_target_pairs={{0,1},{1,0},{2,3},{3,2},{4,5},{5,4},{6,7},{7,6},{8,9},{9,8},{10,11... | collective-permute-start | bytes 3538952 | tf_op jit(solution)/shard_map/ppermute | solution.py:463
  117.0 29.1 %collective-permute-start.23 = (bf16[192,1536]{1,0:T(8,128)(2,1)}, bf16[192,1536]{1,0:T(8,128)(2,1)}, u32[]{:S(2)}, u32[]{:S(2)}) collective-permute-start(bf16[192,1536]{1,0:T(8,128)(2,1)} %get-tuple-element.232), channel_id=1, source_target_pairs={{0,2},{2,0},{4,6},{6,4},{8,10},{10,8},{12,14},{14,12},{16,18},{18,... | collective-permute-start | bytes 1769480 | tf_op jit(solution)/shard_map/ppermute | solution.py:463
  118.2 27.9 %collective-permute-start.24 = (bf16[192,1536]{1,0:T(8,128)(2,1)}, bf16[192,1536]{1,0:T(8,128)(2,1)}, u32[]{:S(2)}, u32[]{:S(2)}) collective-permute-start(bf16[192,1536]{1,0:T(8,128)(2,1)} %get-tuple-element.234), channel_id=1, source_target_pairs={{0,4},{2,6},{4,0},{6,2},{8,12},{10,14},{12,8},{14,10},{16,20},{18,... | collective-permute-start | bytes 1769480 | tf_op jit(solution)/shard_map/ppermute | solution.py:463
  119.1 27.1 %collective-permute-start.25 = (bf16[192,1536]{1,0:T(8,128)(2,1)S(1)}, bf16[192,1536]{1,0:T(8,128)(2,1)}, u32[]{:S(2)}, u32[]{:S(2)}) collective-permute-start(bf16[192,1536]{1,0:T(8,128)(2,1)S(1)} %get-tuple-element.233), channel_id=1, source_target_pairs={{0,6},{2,4},{4,2},{6,0},{8,14},{10,12},{12,10},{14,8},{16,22},{18,... | collective-permute-start | bytes 1769480 | tf_op jit(solution)/shard_map/ppermute | solution.py:463
  153.0 6.9 %collective-permute-start.26 = (bf16[4,192,640]{2,1,0:T(8,128)(2,1)S(1)}, bf16[4,192,640]{2,1,0:T(8,128)(2,1)S(1)}, u32[]{:S(2)}, u32[]{:S(2)}) collective-permute-start(bf16[4,192,640]{2,1,0:T(8,128)(2,1)S(1)} %get-tuple-element.200), channel_id=1, source_target_pairs={{0,1},{1,0},{2,3},{3,2},{4,5},{5,4},{6,7},{7,6},{8,9},{9,8},{10,11... | collective-permute-start | bytes 2949128 | tf_op jit(solution)/shard_map/ppermute | solution.py:463
  153.2 22.2 %collective-permute-start.31 = (bf16[2,48,1536]{2,1,0:T(8,128)(2,1)S(1)}, bf16[2,48,1536]{2,1,0:T(8,128)(2,1)S(1)}, u32[]{:S(2)}, u32[]{:S(2)}) collective-permute-start(bf16[2,48,1536]{2,1,0:T(8,128)(2,1)S(1)} %get-tuple-element.241), channel_id=1, source_target_pairs={{0,8},{2,10},{4,12},{6,14},{8,0},{10,2},{12,4},{14,6},{16,24},{18,... | collective-permute-start | bytes 884744 | tf_op jit(solution)/shard_map/ppermute | solution.py:463
  160.2 14.9 %collective-permute-start.30 = (bf16[4,224,512]{2,1,0:T(8,128)(2,1)S(1)}, bf16[4,224,512]{2,1,0:T(8,128)(2,1)S(1)}, u32[]{:S(2)}, u32[]{:S(2)}) collective-permute-start(bf16[4,224,512]{2,1,0:T(8,128)(2,1)S(1)} %get-tuple-element.207), channel_id=1, source_target_pairs={{0,1},{1,0},{2,3},{3,2},{4,5},{5,4},{6,7},{7,6},{8,9},{9,8},{10,11... | collective-permute-start | bytes 2752520 | tf_op jit(solution)/shard_map/ppermute | solution.py:463
  160.6 12.9 %collective-permute-start.27 = (bf16[192,640]{1,0:T(8,128)(2,1)S(1)}, bf16[192,640]{1,0:T(8,128)(2,1)S(1)}, u32[]{:S(2)}, u32[]{:S(2)}) collective-permute-start(bf16[192,640]{1,0:T(8,128)(2,1)S(1)} %get-tuple-element.235), channel_id=1, source_target_pairs={{0,2},{2,0},{4,6},{6,4},{8,10},{10,8},{12,14},{14,12},{16,18},{18,... | collective-permute-start | bytes 737288 | tf_op jit(solution)/shard_map/ppermute | solution.py:463
  161.8 11.8 %collective-permute-start.28 = (bf16[192,640]{1,0:T(8,128)(2,1)S(1)}, bf16[192,640]{1,0:T(8,128)(2,1)S(1)}, u32[]{:S(2)}, u32[]{:S(2)}) collective-permute-start(bf16[192,640]{1,0:T(8,128)(2,1)S(1)} %get-tuple-element.237), channel_id=1, source_target_pairs={{0,4},{2,6},{4,0},{6,2},{8,12},{10,14},{12,8},{14,10},{16,20},{18,... | collective-permute-start | bytes 737288 | tf_op jit(solution)/shard_map/ppermute | solution.py:463
  162.9 12.1 %collective-permute-start.29 = (bf16[192,640]{1,0:T(8,128)(2,1)S(1)}, bf16[192,640]{1,0:T(8,128)(2,1)S(1)}, u32[]{:S(2)}, u32[]{:S(2)}) collective-permute-start(bf16[192,640]{1,0:T(8,128)(2,1)S(1)} %get-tuple-element.236), channel_id=1, source_target_pairs={{0,6},{2,4},{4,2},{6,0},{8,14},{10,12},{12,10},{14,8},{16,22},{18,... | collective-permute-start | bytes 737288 | tf_op jit(solution)/shard_map/ppermute | solution.py:463
  175.4 19.9 %copy-start.23 = (bf16[1024,1536]{1,0:T(8,128)(2,1)S(1)}, bf16[1024,1536]{1,0:T(8,128)(2,1)}, u32[]{:S(2)}) copy-start(bf16[1024,1536]{1,0:T(8,128)(2,1)} %get-tuple-element.212.right.mixed) | copy-start | bytes 9437188
  175.5 25.3 %collective-permute-start.36 = (bf16[48,1536]{1,0:T(8,128)(2,1)S(1)}, bf16[48,1536]{1,0:T(8,128)(2,1)S(1)}, u32[]{:S(2)}, u32[]{:S(2)}) collective-permute-start(bf16[48,1536]{1,0:T(8,128)(2,1)S(1)} %get-tuple-element.247), channel_id=1, source_target_pairs={{0,16},{2,18},{4,20},{6,22},{8,24},{10,26},{12,28},{14,30},{16,0},... | collective-permute-start | bytes 442376 | tf_op jit(solution)/shard_map/ppermute | solution.py:463
  176.2 5.6 %collective-permute-start.35 = (bf16[2,48,640]{2,1,0:T(8,128)(2,1)S(1)}, bf16[2,48,640]{2,1,0:T(8,128)(2,1)S(1)}, u32[]{:S(2)}, u32[]{:S(2)}) collective-permute-start(bf16[2,48,640]{2,1,0:T(8,128)(2,1)S(1)} %slice_bitcast_fusion.14), channel_id=1, source_target_pairs={{0,8},{2,10},{4,12},{6,14},{8,0},{10,2},{12,4},{14,6},{16,24},{18,... | collective-permute-start | bytes 368648 | tf_op jit(solution)/shard_map/ppermute | solution.py:463
  177.6 8.6 %collective-permute-start.32 = (bf16[224,512]{1,0:T(8,128)(2,1)S(1)}, bf16[224,512]{1,0:T(8,128)(2,1)S(1)}, u32[]{:S(2)}, u32[]{:S(2)}) collective-permute-start(bf16[224,512]{1,0:T(8,128)(2,1)S(1)} %get-tuple-element.238), channel_id=1, source_target_pairs={{0,2},{2,0},{4,6},{6,4},{8,10},{10,8},{12,14},{14,12},{16,18},{18,... | collective-permute-start | bytes 688136 | tf_op jit(solution)/shard_map/ppermute | solution.py:463
  178.6 11.0 %collective-permute-start.33 = (bf16[224,512]{1,0:T(8,128)(2,1)S(1)}, bf16[224,512]{1,0:T(8,128)(2,1)S(1)}, u32[]{:S(2)}, u32[]{:S(2)}) collective-permute-start(bf16[224,512]{1,0:T(8,128)(2,1)S(1)} %get-tuple-element.240), channel_id=1, source_target_pairs={{0,4},{2,6},{4,0},{6,2},{8,12},{10,14},{12,8},{14,10},{16,20},{18,... | collective-permute-start | bytes 688136 | tf_op jit(solution)/shard_map/ppermute | solution.py:463
  180.0 9.6 %collective-permute-start.34 = (bf16[224,512]{1,0:T(8,128)(2,1)S(1)}, bf16[224,512]{1,0:T(8,128)(2,1)S(1)}, u32[]{:S(2)}, u32[]{:S(2)}) collective-permute-start(bf16[224,512]{1,0:T(8,128)(2,1)S(1)} %get-tuple-element.239), channel_id=1, source_target_pairs={{0,6},{2,4},{4,2},{6,0},{8,14},{10,12},{12,10},{14,8},{16,22},{18,... | collective-permute-start | bytes 688136 | tf_op jit(solution)/shard_map/ppermute | solution.py:463
  181.9 13.5 %copy-start.13 = (bf16[768,1536]{1,0:T(8,128)(2,1)S(1)}, bf16[768,1536]{1,0:T(8,128)(2,1)}, u32[]{:S(2)}) copy-start(bf16[768,1536]{1,0:T(8,128)(2,1)} %copy-done.12) | copy-start | bytes 7077892
  189.8 11.1 %collective-permute-start.38 = (bf16[80,512]{1,0:T(8,128)(2,1)S(1)}, bf16[80,512]{1,0:T(8,128)(2,1)S(1)}, u32[]{:S(2)}, u32[]{:S(2)}) collective-permute-start(bf16[80,512]{1,0:T(8,128)(2,1)S(1)} %get-tuple-element.245), channel_id=1, source_target_pairs={{0,8},{2,10},{4,12},{6,14},{8,0},{10,2},{12,4},{14,6},{16,24},{18,... | collective-permute-start | bytes 245768 | tf_op jit(solution)/shard_map/ppermute | solution.py:463
  190.8 10.1 %collective-permute-start.39 = (bf16[80,512]{1,0:T(8,128)(2,1)S(1)}, bf16[80,512]{1,0:T(8,128)(2,1)S(1)}, u32[]{:S(2)}, u32[]{:S(2)}) collective-permute-start(bf16[80,512]{1,0:T(8,128)(2,1)S(1)} %get-tuple-element.244), channel_id=1, source_target_pairs={{0,16},{2,18},{4,20},{6,22},{8,24},{10,26},{12,28},{14,30},{16,0},... | collective-permute-start | bytes 245768 | tf_op jit(solution)/shard_map/ppermute | solution.py:463
  192.9 8.0 %collective-permute-start.40 = (bf16[80,512]{1,0:T(8,128)(2,1)S(1)}, bf16[80,512]{1,0:T(8,128)(2,1)S(1)}, u32[]{:S(2)}, u32[]{:S(2)}) collective-permute-start(bf16[80,512]{1,0:T(8,128)(2,1)S(1)} %get-tuple-element.243), channel_id=1, source_target_pairs={{0,24},{2,26},{4,28},{6,30},{8,16},{10,18},{12,20},{14,22},{16,8},... | collective-permute-start | bytes 245768 | tf_op jit(solution)/shard_map/ppermute | solution.py:463
  194.3 6.6 %collective-permute-start.37 = (bf16[48,640]{1,0:T(8,128)(2,1)S(1)}, bf16[48,640]{1,0:T(8,128)(2,1)S(1)}, u32[]{:S(2)}, u32[]{:S(2)}) collective-permute-start(bf16[48,640]{1,0:T(8,128)(2,1)S(1)} %get-tuple-element.251), channel_id=1, source_target_pairs={{0,16},{2,18},{4,20},{6,22},{8,24},{10,26},{12,28},{14,30},{16,0},... | collective-permute-start | bytes 184328 | tf_op jit(solution)/shard_map/ppermute | solution.py:463
  (24 other events, 88.0 us)

commit v3 on v2

--- a/solution.py
+++ b/solution.py
@@ -395,7 +395,7 @@
             pltpu.VMEM((3 * Q, inner), b16),
             pltpu.VMEM((Q, Q), f32),
         ],
-        compiler_params=pltpu.CompilerParams(vmem_limit_bytes=56 * MIB),
+        compiler_params=pltpu.CompilerParams(vmem_limit_bytes=46 * MIB),
         cost_estimate=pl.CostEstimate(flops=count * Q * inner * 12000, bytes_accessed=count * Q * inner * 10, transcendentals=count * Q * inner * 8),
         name="scan_backward",
     )(dy, xin, pre, bd, bd, held, rates, cx, cb, heads, pick, *kept)

time: 203 us -> 200 us (0.985)
  Pallas kernels: 109 us -> 105 us
  local copies, waits for them, and re-layouts: 14.1 us -> 16.4 us
    pallas_call x2, Pallas kernels: 35.7 us -> 33.1 us  [scan_backward(): pl.pallas_call(functools.partial(scan_backward_kernel, per_seq, pairs, ba...]
    unnamed x66 -> x82, local copies, waits for them, and re-layouts: 9.12 us -> 10.8 us
  transfers between devices with their start and end apart: 41 -> 41, of which waited for: 11 -> 9; matrix products, arithmetic and copies ran while one was open for 7% -> 8% of each run, Pallas kernels for 43% -> 42%
where the time goes in v3:
time: 200 us; the launch traced here: 199 us
  Pallas kernels  105 us (52%)
  starting transfers between devices  40.9 us (20%)
  waiting for transfers between devices  20.8 us (10%)
  local copies, waits for them, and re-layouts  16.4 us (8%)
  other arithmetic  8.66 us (4%)
  matrix products  6.15 us (3%)
    ppermute x41, starting transfers between devices, swap(): return lax.ppermute(value, axis, [(i, i ^ bit) for i in range(count)])  40.9 us
    pallas_call x2, Pallas kernels, scan_backward(): pl.pallas_call(functools.partial(scan_backward_kernel, per_seq, pairs, ba...  33.1 us
    ppermute x41, waiting for transfers between devices, swap(): return lax.ppermute(value, axis, [(i, i ^ bit) for i in range(count)])  20.8 us
    pallas_call x2, Pallas kernels, scan_forward(): pl.pallas_call(functools.partial(scan_forward_kernel, per_seq, pairs, bas...  18.7 us
    pallas_call x1, Pallas kernels, gate_both(): pl.pallas_call(gate_kernel, grid=(rows // size,), in_specs=[tall(inner),...  11.6 us
    unnamed x82, local copies, waits for them, and re-layouts  10.8 us
    pallas_call x1, Pallas kernels, token_grads(): pl.pallas_call(token_grads_kernel, grid=(rows // 256,), in_specs=[tall(v)...  9.39 us
    pallas_call x1, Pallas kernels, prepare(): pl.pallas_call(prepare_kernel, grid=(rows // Q,), in_specs=[tall, tall, p...  8.22 us
  transfers between devices with their start and end apart: 41, of which 9 were waited for; matrix products, arithmetic and copies ran while one was open for 8% of the time, Pallas kernels for 42%

profile of v3, /device:TPU:0, one launch (start us, length us, event | category | flops | bytes accessed | tf_op | source)
XLA Modules:
  0.0 199.0 jit_solution(3652244348005755804)
XLA Ops:
  1.5 1.2 fusion.16
  3.0 3.1 %collective-permute-start = (bf16[48,1024]{1,0:T(8,128)(2,1)S(1)}, bf16[48,1024]{1,0:T(8,128)(2,1)S(1)}, u32[]{:S(2)}, u32[]{:S(2)}) collective-permute-start(bf16[48,1024]{1,0:T(8,128)(2,1)S(1)} %get-tuple-element.254), channel_id=1, source_target_pairs={{0,8},{2,10},{4,12},{6,14},{8,0},{10,2},{12,4},{14,6},{16,24},{18,... | collective-permute-start | bytes 294920 | tf_op jit(solution)/shard_map/ppermute | solution.py:463
  6.1 2.6 %collective-permute-start.1 = (bf16[48,1024]{1,0:T(8,128)(2,1)S(1)}, bf16[48,1024]{1,0:T(8,128)(2,1)S(1)}, u32[]{:S(2)}, u32[]{:S(2)}) collective-permute-start(bf16[48,1024]{1,0:T(8,128)(2,1)S(1)} %get-tuple-element.254), channel_id=1, source_target_pairs={{0,16},{2,18},{4,20},{6,22},{8,24},{10,26},{12,28},{14,30},{16,0},... | collective-permute-start | bytes 294920 | tf_op jit(solution)/shard_map/ppermute | solution.py:463
  14.9 1.9 collective-permute-done.1
  16.8 2.5 %collective-permute-start.3 = (bf16[4,48,1024]{2,1,0:T(8,128)(2,1)S(1)}, bf16[4,48,1024]{2,1,0:T(8,128)(2,1)S(1)}, u32[]{:S(2)}, u32[]{:S(2)}) collective-permute-start(bf16[4,48,1024]{2,1,0:T(8,128)(2,1)S(1)} %pad_maximum_fusion.2.refs_0_), channel_id=1, source_target_pairs={{0,6},{2,4},{4,2},{6,0},{8,14},{10,12},{12,10},{14,8},{16,22},{18,... | collective-permute-start | bytes 1179656 | tf_op jit(solution)/shard_map/ppermute | solution.py:463
  20.4 1.7 collective-permute-start.11
  22.1 1.4 collective-permute-start.12
  23.5 8.2 %prepare.1 = (bf16[1024,768]{1,0:T(8,128)(2,1)}, bf16[1024,768]{1,0:T(8,128)(2,1)}, bf16[1024,768]{1,0:T(8,128)(2,1)}, bf16[768,1024]{1,0:T(8,128)(2,1)}, bf16[768,1024]{1,0:T(8,128)(2,1)}) custom-call(bf16[1024,768]{1,0:T(8,128)(2,1)} %tokens, bf16[1024,768]{1,0:T(8,128)(2,1)} %cot, f32[1,768]{1,0:T(1,128)} %reshape.106.gain.gain_pre), custom_call_target="tpu_custom_call" | custom-call | tf_op jit(solution)/shard_map/prepare/pallas_call | solution.py:840
  31.8 1.4 collective-permute-start.13
  33.4 2.8 %collective-permute-done.4.refs_1_ = bf16[4,48,1024]{2,1,0:T(8,128)(2,1)S(1)} collective-permute-done((bf16[4,48,1024]{2,1,0:T(8,128)(2,1)S(1)}, bf16[4,48,1024]{2,1,0:T(8,128)(2,1)S(1)}, u32[]{:S(2)}, u32[]{:S(2)}) %collective-permute-start.4) | collective-permute-done | bytes 393248 | tf_op jit(solution)/shard_map/ppermute | solution.py:463
  38.8 1.5 collective-permute-done.13
  40.3 1.2 pad_maximum_fusion.1.refs_0_
  41.5 1.5 collective-permute-start.14
  43.0 1.5 collective-permute-start.15
  48.2 4.0 %convolution_convert_fusion.refs_0_.refs_1_ = bf16[1024,1536]{1,0:T(8,128)(2,1)} fusion(bf16[1024,768]{1,0:T(8,128)(2,1)S(1)} %copy-done.22, bf16[768,1536]{1,0:T(8,128)(2,1)S(1)} %get-tuple-element.130.w_x), kind=kOutput, calls=%fused_computation | convolution fusion | flops 2417491968 | bytes 7077888 | tf_op jit(solution)/shard_map/dot_general | solution.py:23
  52.2 2.2 %fusion.15.refs_2_.refs_3_.refs_4_ = f32[1024,384]{1,0:T(8,128)} fusion(bf16[1024,768]{1,0:T(8,128)(2,1)S(1)} %copy-done.22, bf16[768,128]{1,0:T(8,128)(2,1)S(1)} %slice_add_fusion, bf16[768,256]{1,0:T(8,128)(2,1)S(1)} %get-tuple-element.131), kind=kOutput, calls=%fused_computation.85 | convolution fusion | flops 605159424 | bytes 3735552 | tf_op jit(solution)/shard_map/dot_general | solution.py:23
  54.4 12.7 %scan_forward.2 = (bf16[1024,1536]{1,0:T(8,128)(2,1)}, bf16[8,128,1536]{2,1,0:T(8,128)(2,1)}, bf16[1024,1536]{1,0:T(8,128)(2,1)}, f32[1024,256]{1,0:T(8,128)}, f32[128,1536]{1,0:T(8,128)}) custom-call(bf16[1024,1536]{1,0:T(8,128)(2,1)} %convolution_convert_fusion.refs_0_.refs_1_, bf16[1024,1536]{1,0:T(8,128)(2,1)} %convolution_convert_fusion.refs_0_.refs_1_, ...), custom_call_target="tpu_custom_call" | custom-call | flops 7077888000 | bytes 9437184 | tf_op jit(solution)/shard_map/scan_forward/pallas_call | solution.py:173
  67.0 3.2 %collective-permute-done.15.refs_2_ = bf16[4,48,1536]{2,1,0:T(8,128)(2,1)S(1)} collective-permute-done((bf16[4,48,1536]{2,1,0:T(8,128)(2,1)S(1)}, bf16[4,48,1536]{2,1,0:T(8,128)(2,1)S(1)}, u32[]{:S(2)}, u32[]{:S(2)}) %collective-permute-start.15) | collective-permute-done | bytes 589856 | tf_op jit(solution)/shard_map/ppermute | solution.py:463
  71.3 6.1 %scan_forward.3 = (bf16[1024,1536]{1,0:T(8,128)(2,1)}, bf16[8,128,1536]{2,1,0:T(8,128)(2,1)}, bf16[1024,1536]{1,0:T(8,128)(2,1)}, f32[1024,256]{1,0:T(8,128)}, f32[128,1536]{1,0:T(8,128)}) custom-call(bf16[1024,1536]{1,0:T(8,128)(2,1)} %convolution_convert_fusion.refs_0_.refs_1_, ...), custom_call_target="tpu_custom_call", output_to_operand_aliasing={{0}: (8, {}), {1}: (9, {}), {2}: (10, {}), {3}: (11, {})} | custom-call | flops 2359296000 | bytes 3145728 | tf_op jit(solution)/shard_map/scan_forward/pallas_call | solution.py:173
  79.2 11.6 %gate_both.1 = (bf16[1024,1536]{1,0:T(8,128)(2,1)}, bf16[1024,1536]{1,0:T(8,128)(2,1)}, bf16[1024,1536]{1,0:T(8,128)(2,1)}, f32[8,1536]{1,0:T(8,128)S(1)}) custom-call(bf16[1024,1536]{1,0:T(8,128)(2,1)} %get-tuple-element.141.y, bf16[1024,768]{1,0:T(8,128)(2,1)S(1)} %copy-done.23, bf16[1024,768]{1,0:T(8,128)(2,1)S(1)} %copy-done.19, ...), custom_call_target="tpu_custom_call" | custom-call | flops 12582912000 | bytes 15728640 | tf_op jit(solution)/shard_map/gate_both/pallas_call | solution.py:448
  90.9 1.9 copy-done.24
  92.8 3.6 %pack_whole.2 = (bf16[4,192,768]{2,1,0:T(8,128)(2,1)S(1)}, bf16[4,192,768]{2,1,0:T(8,128)(2,1)S(1)}) custom-call(s32[2]{0:T(128)S(1)} %pad_add_fusion.where_ref.side_ref, bf16[768,1024]{1,0:T(8,128)(2,1)S(1)} %copy-done.21, bf16[1024,1536]{1,0:T(8,128)(2,1)S(1)} %copy-done.24), custom_call_target="tpu_custom_call" | custom-call | flops 4831838208 | bytes 6291456 | tf_op jit(solution)/shard_map/pack_whole/pallas_call | solution.py:568
  96.5 4.5 %pack_whole.3 = (bf16[4,192,768]{2,1,0:T(8,128)(2,1)S(1)}, bf16[4,192,768]{2,1,0:T(8,128)(2,1)S(1)}, f32[768,128]{1,0:T(8,128)S(1)}) custom-call(s32[2]{0:T(128)S(1)} %pad_add_fusion.where_ref.side_ref, bf16[768,1024]{1,0:T(8,128)(2,1)S(1)} %copy-done.6, bf16[1024,1536]{1,0:T(8,128)(2,1)S(1)} %copy-done.26, bf16[768,1536]{1,0:T(8,128)(2,1)S(1)} %get-tuple-element.151.w_z.refs_0_), custom_call_target="tpu_custom_call" | custom-call | flops 4831838208 | bytes 6291456 | tf_op jit(solution)/shard_map/pack_whole/pallas_call | solution.py:568
  101.0 1.3 add_convert_fusion.1
  103.2 8.9 %scan_backward.2 = (bf16[1024,1536]{1,0:T(8,128)(2,1)S(1)}, bf16[1024,384]{1,0:T(8,128)(2,1)S(1)}, f32[128,1536]{1,0:T(8,128)S(1)}, f32[24,1536]{1,0:T(8,128)S(1...) custom-call(bf16[1024,1536]{1,0:T(8,128)(2,1)} %get-tuple-element.165.refs_0_,, ...), custom_call_target="tpu_custom_call" | custom-call | flops 4718592000 | bytes 3932160 | tf_op jit(solution)/shard_map/scan_backward/pallas_call | solution.py:363
  112.4 1.3 copy-done.2
  113.8 1.2 copy-done.28
  115.2 1.3 collective-permute-start.23
  117.3 1.4 collective-permute-start.25
  118.8 24.2 %scan_backward.3 = (bf16[1024,1536]{1,0:T(8,128)(2,1)}, bf16[1024,384]{1,0:T(8,128)(2,1)S(1)}, f32[128,1536]{1,0:T(8,128)}, f32[24,1536]{1,0:T(8,128)}, f32[24,2...) custom-call(bf16[1024,1536]{1,0:T(8,128)(2,1)} %get-tuple-element.16, ...), custom_call_target="tpu_custom_call", output_to_operand_aliasing={{0}: (17, {}), {1}: (18, {})} | custom-call | flops 14155776000 | bytes 11796480 | tf_op jit(solution)/shard_map/scan_backward/pallas_call | solution.py:363
  143.0 1.6 collective-permute-done.25
  144.9 1.9 copy-done.3
  146.8 3.0 %pack_first.1 = (bf16[4,192,640]{2,1,0:T(8,128)(2,1)S(1)}, bf16[4,192,640]{2,1,0:T(8,128)(2,1)S(1)}, f32[768,128]{1,0:T(8,128)S(1)}) custom-call(s32[2]{0:T(128)S(1)} %pad_add_fusion.where_ref.side_ref, bf16[768,1024]{1,0:T(8,128)(2,1)S(1)} %copy-done.6, bf16[1024,1536]{1,0:T(8,128)(2,1)S(1)} %copy-done.3, bf16[1024,384]{1,0:T(8,128)(2,1)S(1)} %get-tuple-element.187.dbd, ...), custom_call_target="tpu_custom_call" | custom-call | flops 1409286144 | bytes 1048576 | tf_op jit(solution)/shard_map/pack_first/pallas_call | solution.py:616
  150.0 3.0 %collective-permute-start.31 = (bf16[2,48,1536]{2,1,0:T(8,128)(2,1)S(1)}, bf16[2,48,1536]{2,1,0:T(8,128)(2,1)S(1)}, u32[]{:S(2)}, u32[]{:S(2)}) collective-permute-start(bf16[2,48,1536]{2,1,0:T(8,128)(2,1)S(1)} %get-tuple-element.241), channel_id=1, source_target_pairs={{0,8},{2,10},{4,12},{6,14},{8,0},{10,2},{12,4},{14,6},{16,24},{18,... | collective-permute-start | bytes 884744 | tf_op jit(solution)/shard_map/ppermute | solution.py:463
  153.0 3.7 %pack_second.1 = (bf16[4,224,512]{2,1,0:T(8,128)(2,1)S(1)}, bf16[4,224,512]{2,1,0:T(8,128)(2,1)S(1)}) custom-call(s32[2]{0:T(128)S(1)} %pad_add_fusion.where_ref.side_ref, bf16[768,1024]{1,0:T(8,128)(2,1)S(1)} %copy-done.6, bf16[1024,1536]{1,0:T(8,128)(2,1)S(1)} %copy-done.4, bf16[768,1536]{1,0:T(8,128)(2,1)S(1)} %get-tuple-element.130.w_x, ...), custom_call_target="tpu_custom_call" | custom-call | flops 1610612736 | bytes 2097152 | tf_op jit(solution)/shard_map/pack_second/pallas_call | solution.py:691
  158.2 1.5 collective-permute-start.28
  159.7 1.2 collective-permute-start.29
  160.9 9.4 %token_grads.1 = bf16[1024,768]{1,0:T(8,128)(2,1)} custom-call(bf16[1024,1536]{1,0:T(8,128)(2,1)S(1)} %copy-done.27, bf16[1024,1536]{1,0:T(8,128)(2,1)S(1)} %copy-done.4, bf16[1024,384]{1,0:T(8,128)(2,1)S(1)} %get-tuple-element.187.dbd, bf16[1024,768]{1,0:T(8,128)(2,1)S(1)} %copy-done.18, bf16[1024,768]{1,0:T(8,128)(2,1)S(1)} %copy-done.20, ...), custom_call_target="tpu_custom_call" | custom-call | flops 6291456000 | bytes 15728640 | tf_op jit(solution)/shard_map/token_grads/pallas_call | solution.py:872
  170.3 1.0 collective-permute-done.28
  172.3 1.6 collective-permute-start.35
  174.0 1.3 collective-permute-start.32
  176.1 1.4 collective-permute-start.34
  178.0 4.6 %collective-permute-done.32 = bf16[224,512]{1,0:T(8,128)(2,1)S(1)} collective-permute-done((bf16[224,512]{1,0:T(8,128)(2,1)S(1)}, bf16[224,512]{1,0:T(8,128)(2,1)S(1)}, u32[]{:S(2)}, u32[]{:S(2)}) %collective-permute-start.32) | collective-permute-done | bytes 229408 | tf_op jit(solution)/shard_map/ppermute | solution.py:463
  182.6 3.8 %collective-permute-done.33 = bf16[224,512]{1,0:T(8,128)(2,1)S(1)} collective-permute-done((bf16[224,512]{1,0:T(8,128)(2,1)S(1)}, bf16[224,512]{1,0:T(8,128)(2,1)S(1)}, u32[]{:S(2)}, u32[]{:S(2)}) %collective-permute-start.33) | collective-permute-done | bytes 229408 | tf_op jit(solution)/shard_map/ppermute | solution.py:463
  187.2 2.5 %collective-permute-start.39 = (bf16[80,512]{1,0:T(8,128)(2,1)S(1)}, bf16[80,512]{1,0:T(8,128)(2,1)S(1)}, u32[]{:S(2)}, u32[]{:S(2)}) collective-permute-start(bf16[80,512]{1,0:T(8,128)(2,1)S(1)} %get-tuple-element.244), channel_id=1, source_target_pairs={{0,16},{2,18},{4,20},{6,22},{8,24},{10,26},{12,28},{14,30},{16,0},... | collective-permute-start | bytes 245768 | tf_op jit(solution)/shard_map/ppermute | solution.py:463
  189.7 1.4 collective-permute-start.40
  191.9 5.4 %add_branch.1 = bf16[1024,768]{1,0:T(8,128)(2,1)} custom-call(bf16[1024,1536]{1,0:T(8,128)(2,1)S(1)} %copy-done.25, bf16[1024,768]{1,0:T(8,128)(2,1)S(1)} %copy-done.18, bf16[768,1536]{1,0:T(8,128)(2,1)S(1)} %copy-done.15), custom_call_target="tpu_custom_call" | custom-call | flops 3145728000 | bytes 7864320 | tf_op jit(solution)/shard_map/add_branch/pallas_call | solution.py:891
  197.3 1.5 finish.1
  (193 shorter events, 25.7 us)
Async XLA Ops:
  3.0 11.8 %collective-permute-start = (bf16[48,1024]{1,0:T(8,128)(2,1)S(1)}, bf16[48,1024]{1,0:T(8,128)(2,1)S(1)}, u32[]{:S(2)}, u32[]{:S(2)}) collective-permute-start(bf16[48,1024]{1,0:T(8,128)(2,1)S(1)} %get-tuple-element.254), channel_id=1, source_target_pairs={{0,8},{2,10},{4,12},{6,14},{8,0},{10,2},{12,4},{14,6},{16,24},{18,... | collective-permute-start | bytes 294920 | tf_op jit(solution)/shard_map/ppermute | solution.py:463
  6.1 10.6 %collective-permute-start.1 = (bf16[48,1024]{1,0:T(8,128)(2,1)S(1)}, bf16[48,1024]{1,0:T(8,128)(2,1)S(1)}, u32[]{:S(2)}, u32[]{:S(2)}) collective-permute-start(bf16[48,1024]{1,0:T(8,128)(2,1)S(1)} %get-tuple-element.254), channel_id=1, source_target_pairs={{0,16},{2,18},{4,20},{6,22},{8,24},{10,26},{12,28},{14,30},{16,0},... | collective-permute-start | bytes 294920 | tf_op jit(solution)/shard_map/ppermute | solution.py:463
  8.7 8.0 %collective-permute-start.2 = (bf16[48,1024]{1,0:T(8,128)(2,1)S(1)}, bf16[48,1024]{1,0:T(8,128)(2,1)S(1)}, u32[]{:S(2)}, u32[]{:S(2)}) collective-permute-start(bf16[48,1024]{1,0:T(8,128)(2,1)S(1)} %get-tuple-element.254), channel_id=1, source_target_pairs={{0,24},{2,26},{4,28},{6,30},{8,16},{10,18},{12,20},{14,22},{16,8},... | collective-permute-start | bytes 294920 | tf_op jit(solution)/shard_map/ppermute | solution.py:463
  11.0 2.9 %collective-permute-start.10 = (f32[1,8,768]{2,1,0:T(8,128)S(1)}, f32[1,8,768]{2,1,0:T(8,128)S(1)}, u32[]{:S(2)}, u32[]{:S(2)}) collective-permute-start(f32[1,8,768]{2,1,0:T(8,128)S(1)} %maximum_bitcast_fusion), channel_id=1, source_target_pairs={{0,1},{1,0},{2,3},{3,2},{4,5},{5,4},{6,7},{7,6},{8,9},{9,8},{10,11... | collective-permute-start | bytes 73736 | tf_op jit(solution)/shard_map/ppermute | solution.py:463
  16.8 14.9 %collective-permute-start.3 = (bf16[4,48,1024]{2,1,0:T(8,128)(2,1)S(1)}, bf16[4,48,1024]{2,1,0:T(8,128)(2,1)S(1)}, u32[]{:S(2)}, u32[]{:S(2)}) collective-permute-start(bf16[4,48,1024]{2,1,0:T(8,128)(2,1)S(1)} %pad_maximum_fusion.2.refs_0_), channel_id=1, source_target_pairs={{0,6},{2,4},{4,2},{6,0},{8,14},{10,12},{12,10},{14,8},{16,22},{18,... | collective-permute-start | bytes 1179656 | tf_op jit(solution)/shard_map/ppermute | solution.py:463
  19.3 16.8 %collective-permute-start.4 = (bf16[4,48,1024]{2,1,0:T(8,128)(2,1)S(1)}, bf16[4,48,1024]{2,1,0:T(8,128)(2,1)S(1)}, u32[]{:S(2)}, u32[]{:S(2)}) collective-permute-start(bf16[4,48,1024]{2,1,0:T(8,128)(2,1)S(1)} %pad_maximum_fusion.2.refs_0_), channel_id=1, source_target_pairs={{0,2},{2,0},{4,6},{6,4},{8,10},{10,8},{12,14},{14,12},{16,18},{18,... | collective-permute-start | bytes 1179656 | tf_op jit(solution)/shard_map/ppermute | solution.py:463
  19.8 16.3 %collective-permute-start.5 = (bf16[4,48,1024]{2,1,0:T(8,128)(2,1)S(1)}, bf16[4,48,1024]{2,1,0:T(8,128)(2,1)S(1)}, u32[]{:S(2)}, u32[]{:S(2)}) collective-permute-start(bf16[4,48,1024]{2,1,0:T(8,128)(2,1)S(1)} %pad_maximum_fusion.2.refs_0_), channel_id=1, source_target_pairs={{0,4},{2,6},{4,0},{6,2},{8,12},{10,14},{12,8},{14,10},{16,20},{18,... | collective-permute-start | bytes 1179656 | tf_op jit(solution)/shard_map/ppermute | solution.py:463
  20.4 11.4 %collective-permute-start.11 = (bf16[48,1536]{1,0:T(8,128)(2,1)}, bf16[48,1536]{1,0:T(8,128)(2,1)}, u32[]{:S(2)}, u32[]{:S(2)}) collective-permute-start(bf16[48,1536]{1,0:T(8,128)(2,1)} %pad_maximum_fusion.4), channel_id=1, source_target_pairs={{0,8},{2,10},{4,12},{6,14},{8,0},{10,2},{12,4},{14,6},{16,24},{18,... | collective-permute-start | bytes 442376 | tf_op jit(solution)/shard_map/ppermute | solution.py:463
  22.1 11.1 %collective-permute-start.12 = (bf16[48,1536]{1,0:T(8,128)(2,1)}, bf16[48,1536]{1,0:T(8,128)(2,1)}, u32[]{:S(2)}, u32[]{:S(2)}) collective-permute-start(bf16[48,1536]{1,0:T(8,128)(2,1)} %pad_maximum_fusion.4), channel_id=1, source_target_pairs={{0,16},{2,18},{4,20},{6,22},{8,24},{10,26},{12,28},{14,30},{16,0},... | collective-permute-start | bytes 442376 | tf_op jit(solution)/shard_map/ppermute | solution.py:463
  23.5 13.2 %copy-start.38 = (f32[8]{0:T(128)S(1)}, f32[8]{0:T(128)}, u32[]{:S(2)}) copy-start(f32[8]{0:T(128)} %pad.30.clone) | copy-start | bytes 100
  31.7 11.3 %collective-permute-start.6 = (bf16[4,48,1024]{2,1,0:T(8,128)(2,1)S(1)}, bf16[4,48,1024]{2,1,0:T(8,128)(2,1)S(1)}, u32[]{:S(2)}, u32[]{:S(2)}) collective-permute-start(bf16[4,48,1024]{2,1,0:T(8,128)(2,1)S(1)} %pad_maximum_fusion.2.refs_0_), channel_id=1, source_target_pairs={{0,1},{1,0},{2,3},{3,2},{4,5},{5,4},{6,7},{7,6},{8,9},{9,8},{10,11... | collective-permute-start | bytes 1179656 | tf_op jit(solution)/shard_map/ppermute | solution.py:463
  31.8 8.5 %collective-permute-start.13 = (bf16[48,1536]{1,0:T(8,128)(2,1)}, bf16[48,1536]{1,0:T(8,128)(2,1)}, u32[]{:S(2)}, u32[]{:S(2)}) collective-permute-start(bf16[48,1536]{1,0:T(8,128)(2,1)} %pad_maximum_fusion.4), channel_id=1, source_target_pairs={{0,24},{2,26},{4,28},{6,30},{8,16},{10,18},{12,20},{14,22},{16,8},... | collective-permute-start | bytes 442376 | tf_op jit(solution)/shard_map/ppermute | solution.py:463
  33.2 11.4 %collective-permute-start.9 = (bf16[4,48,1024]{2,1,0:T(8,128)(2,1)S(1)}, bf16[4,48,1024]{2,1,0:T(8,128)(2,1)S(1)}, u32[]{:S(2)}, u32[]{:S(2)}) collective-permute-start(bf16[4,48,1024]{2,1,0:T(8,128)(2,1)S(1)} %collective-permute-done.3.refs_3_), channel_id=1, source_target_pairs={{0,1},{1,0},{2,3},{3,2},{4,5},{5,4},{6,7},{7,6},{8,9},{9,8},{10,11... | collective-permute-start | bytes 1179656 | tf_op jit(solution)/shard_map/ppermute | solution.py:463
  36.2 8.9 %collective-permute-start.7 = (bf16[4,48,1024]{2,1,0:T(8,128)(2,1)S(1)}, bf16[4,48,1024]{2,1,0:T(8,128)(2,1)S(1)}, u32[]{:S(2)}, u32[]{:S(2)}) collective-permute-start(bf16[4,48,1024]{2,1,0:T(8,128)(2,1)S(1)} %collective-permute-done.4.refs_1_), channel_id=1, source_target_pairs={{0,1},{1,0},{2,3},{3,2},{4,5},{5,4},{6,7},{7,6},{8,9},{9,8},{10,11... | collective-permute-start | bytes 1179656 | tf_op jit(solution)/shard_map/ppermute | solution.py:463
  36.2 8.9 %collective-permute-start.8 = (bf16[4,48,1024]{2,1,0:T(8,128)(2,1)S(1)}, bf16[4,48,1024]{2,1,0:T(8,128)(2,1)S(1)}, u32[]{:S(2)}, u32[]{:S(2)}) collective-permute-start(bf16[4,48,1024]{2,1,0:T(8,128)(2,1)S(1)} %collective-permute-done.5.refs_2_), channel_id=1, source_target_pairs={{0,1},{1,0},{2,3},{3,2},{4,5},{5,4},{6,7},{7,6},{8,9},{9,8},{10,11... | collective-permute-start | bytes 1179656 | tf_op jit(solution)/shard_map/ppermute | solution.py:463
  41.5 25.5 %collective-permute-start.14 = (bf16[4,48,1536]{2,1,0:T(8,128)(2,1)S(1)}, bf16[4,48,1536]{2,1,0:T(8,128)(2,1)S(1)}, u32[]{:S(2)}, u32[]{:S(2)}) collective-permute-start(bf16[4,48,1536]{2,1,0:T(8,128)(2,1)S(1)} %pad_maximum_fusion.1.refs_0_), channel_id=1, source_target_pairs={{0,2},{2,0},{4,6},{6,4},{8,10},{10,8},{12,14},{14,12},{16,18},{18,... | collective-permute-start | bytes 1769480 | tf_op jit(solution)/shard_map/ppermute | solution.py:463
  43.0 27.2 %collective-permute-start.15 = (bf16[4,48,1536]{2,1,0:T(8,128)(2,1)S(1)}, bf16[4,48,1536]{2,1,0:T(8,128)(2,1)S(1)}, u32[]{:S(2)}, u32[]{:S(2)}) collective-permute-start(bf16[4,48,1536]{2,1,0:T(8,128)(2,1)S(1)} %pad_maximum_fusion.1.refs_0_), channel_id=1, source_target_pairs={{0,4},{2,6},{4,0},{6,2},{8,12},{10,14},{12,8},{14,10},{16,20},{18,... | collective-permute-start | bytes 1769480 | tf_op jit(solution)/shard_map/ppermute | solution.py:463
  44.6 25.7 %collective-permute-start.16 = (bf16[4,48,1536]{2,1,0:T(8,128)(2,1)S(1)}, bf16[4,48,1536]{2,1,0:T(8,128)(2,1)S(1)}, u32[]{:S(2)}, u32[]{:S(2)}) collective-permute-start(bf16[4,48,1536]{2,1,0:T(8,128)(2,1)S(1)} %pad_maximum_fusion.1.refs_0_), channel_id=1, source_target_pairs={{0,6},{2,4},{4,2},{6,0},{8,14},{10,12},{12,10},{14,8},{16,22},{18,... | collective-permute-start | bytes 1769480 | tf_op jit(solution)/shard_map/ppermute | solution.py:463
  54.4 16.9 %copy-start.32 = (f32[6,768]{1,0:T(8,128)S(1)}, f32[6,768]{1,0:T(8,128)}, u32[]{:S(2)}) copy-start(f32[6,768]{1,0:T(8,128)} %copy-done.31) | copy-start | bytes 55300
  54.4 16.9 %copy-start.34 = (f32[6,768]{1,0:T(8,128)S(1)}, f32[6,768]{1,0:T(8,128)}, u32[]{:S(2)}) copy-start(f32[6,768]{1,0:T(8,128)} %copy-done.33) | copy-start | bytes 55300
  70.2 7.1 %collective-permute-start.17 = (bf16[4,48,1536]{2,1,0:T(8,128)(2,1)S(1)}, bf16[4,48,1536]{2,1,0:T(8,128)(2,1)S(1)}, u32[]{:S(2)}, u32[]{:S(2)}) collective-permute-start(bf16[4,48,1536]{2,1,0:T(8,128)(2,1)S(1)} %pad_maximum_fusion.1.refs_0_), channel_id=1, source_target_pairs={{0,1},{1,0},{2,3},{3,2},{4,5},{5,4},{6,7},{7,6},{8,9},{9,8},{10,11... | collective-permute-start | bytes 1769480 | tf_op jit(solution)/shard_map/ppermute | solution.py:463
  70.2 7.1 %collective-permute-start.18 = (bf16[4,48,1536]{2,1,0:T(8,128)(2,1)S(1)}, bf16[4,48,1536]{2,1,0:T(8,128)(2,1)S(1)}, u32[]{:S(2)}, u32[]{:S(2)}) collective-permute-start(bf16[4,48,1536]{2,1,0:T(8,128)(2,1)S(1)} %collective-permute-done.14.refs_1_), channel_id=1, source_target_pairs={{0,1},{1,0},{2,3},{3,2},{4,5},{5,4},{6,7},{7,6},{8,9},{9,8},{10,11... | collective-permute-start | bytes 1769480 | tf_op jit(solution)/shard_map/ppermute | solution.py:463
  70.7 6.6 %collective-permute-start.19 = (bf16[4,48,1536]{2,1,0:T(8,128)(2,1)S(1)}, bf16[4,48,1536]{2,1,0:T(8,128)(2,1)S(1)}, u32[]{:S(2)}, u32[]{:S(2)}) collective-permute-start(bf16[4,48,1536]{2,1,0:T(8,128)(2,1)S(1)} %collective-permute-done.15.refs_2_), channel_id=1, source_target_pairs={{0,1},{1,0},{2,3},{3,2},{4,5},{5,4},{6,7},{7,6},{8,9},{9,8},{10,11... | collective-permute-start | bytes 1769480 | tf_op jit(solution)/shard_map/ppermute | solution.py:463
  70.7 6.7 %collective-permute-start.20 = (bf16[4,48,1536]{2,1,0:T(8,128)(2,1)S(1)}, bf16[4,48,1536]{2,1,0:T(8,128)(2,1)S(1)}, u32[]{:S(2)}, u32[]{:S(2)}) collective-permute-start(bf16[4,48,1536]{2,1,0:T(8,128)(2,1)S(1)} %collective-permute-done.16.refs_3_), channel_id=1, source_target_pairs={{0,1},{1,0},{2,3},{3,2},{4,5},{5,4},{6,7},{7,6},{8,9},{9,8},{10,11... | collective-permute-start | bytes 1769480 | tf_op jit(solution)/shard_map/ppermute | solution.py:463
  78.3 12.6 %copy-start.14 = (bf16[768,1536]{1,0:T(8,128)(2,1)}, bf16[768,1536]{1,0:T(8,128)(2,1)S(1)}, u32[]{:S(2)}) copy-start(bf16[768,1536]{1,0:T(8,128)(2,1)S(1)} %get-tuple-element.152.w_out_t) | copy-start | bytes 7077892
  78.3 18.2 %copy-start.16 = (bf16[768,1536]{1,0:T(8,128)(2,1)}, bf16[768,1536]{1,0:T(8,128)(2,1)S(1)}, u32[]{:S(2)}) copy-start(bf16[768,1536]{1,0:T(8,128)(2,1)S(1)} %get-tuple-element.151.w_z.refs_0_) | copy-start | bytes 7077892
  96.4 4.6 %collective-permute-start.21 = (bf16[4,192,768]{2,1,0:T(8,128)(2,1)S(1)}, bf16[4,192,768]{2,1,0:T(8,128)(2,1)S(1)}, u32[]{:S(2)}, u32[]{:S(2)}) collective-permute-start(bf16[4,192,768]{2,1,0:T(8,128)(2,1)S(1)} %get-tuple-element.164), channel_id=1, source_target_pairs={{0,1},{1,0},{2,3},{3,2},{4,5},{5,4},{6,7},{7,6},{8,9},{9,8},{10,11... | collective-permute-start | bytes 3538952 | tf_op jit(solution)/shard_map/ppermute | solution.py:463
  102.4 9.7 %collective-permute-start.22 = (bf16[4,192,768]{2,1,0:T(8,128)(2,1)S(1)}, bf16[4,192,768]{2,1,0:T(8,128)(2,1)S(1)}, u32[]{:S(2)}, u32[]{:S(2)}) collective-permute-start(bf16[4,192,768]{2,1,0:T(8,128)(2,1)S(1)} %get-tuple-element.172), channel_id=1, source_target_pairs={{0,1},{1,0},{2,3},{3,2},{4,5},{5,4},{6,7},{7,6},{8,9},{9,8},{10,11... | collective-permute-start | bytes 3538952 | tf_op jit(solution)/shard_map/ppermute | solution.py:463
  115.2 27.8 %collective-permute-start.23 = (bf16[192,1536]{1,0:T(8,128)(2,1)S(1)}, bf16[192,1536]{1,0:T(8,128)(2,1)S(1)}, u32[]{:S(2)}, u32[]{:S(2)}) collective-permute-start(bf16[192,1536]{1,0:T(8,128)(2,1)S(1)} %get-tuple-element.232), channel_id=1, source_target_pairs={{0,2},{2,0},{4,6},{6,4},{8,10},{10,8},{12,14},{14,12},{16,18},{18,... | collective-permute-start | bytes 1769480 | tf_op jit(solution)/shard_map/ppermute | solution.py:463
  116.5 26.5 %collective-permute-start.24 = (bf16[192,1536]{1,0:T(8,128)(2,1)S(1)}, bf16[192,1536]{1,0:T(8,128)(2,1)S(1)}, u32[]{:S(2)}, u32[]{:S(2)}) collective-permute-start(bf16[192,1536]{1,0:T(8,128)(2,1)S(1)} %get-tuple-element.234), channel_id=1, source_target_pairs={{0,4},{2,6},{4,0},{6,2},{8,12},{10,14},{12,8},{14,10},{16,20},{18,... | collective-permute-start | bytes 1769480 | tf_op jit(solution)/shard_map/ppermute | solution.py:463
  117.3 27.2 %collective-permute-start.25 = (bf16[192,1536]{1,0:T(8,128)(2,1)S(1)}, bf16[192,1536]{1,0:T(8,128)(2,1)S(1)}, u32[]{:S(2)}, u32[]{:S(2)}) collective-permute-start(bf16[192,1536]{1,0:T(8,128)(2,1)S(1)} %get-tuple-element.233), channel_id=1, source_target_pairs={{0,6},{2,4},{4,2},{6,0},{8,14},{10,12},{12,10},{14,8},{16,22},{18,... | collective-permute-start | bytes 1769480 | tf_op jit(solution)/shard_map/ppermute | solution.py:463
  149.8 6.9 %collective-permute-start.26 = (bf16[4,192,640]{2,1,0:T(8,128)(2,1)S(1)}, bf16[4,192,640]{2,1,0:T(8,128)(2,1)S(1)}, u32[]{:S(2)}, u32[]{:S(2)}) collective-permute-start(bf16[4,192,640]{2,1,0:T(8,128)(2,1)S(1)} %get-tuple-element.200), channel_id=1, source_target_pairs={{0,1},{1,0},{2,3},{3,2},{4,5},{5,4},{6,7},{7,6},{8,9},{9,8},{10,11... | collective-permute-start | bytes 2949128 | tf_op jit(solution)/shard_map/ppermute | solution.py:463
  150.0 21.8 %collective-permute-start.31 = (bf16[2,48,1536]{2,1,0:T(8,128)(2,1)S(1)}, bf16[2,48,1536]{2,1,0:T(8,128)(2,1)S(1)}, u32[]{:S(2)}, u32[]{:S(2)}) collective-permute-start(bf16[2,48,1536]{2,1,0:T(8,128)(2,1)S(1)} %get-tuple-element.241), channel_id=1, source_target_pairs={{0,8},{2,10},{4,12},{6,14},{8,0},{10,2},{12,4},{14,6},{16,24},{18,... | collective-permute-start | bytes 884744 | tf_op jit(solution)/shard_map/ppermute | solution.py:463
  157.0 14.5 %collective-permute-start.30 = (bf16[4,224,512]{2,1,0:T(8,128)(2,1)S(1)}, bf16[4,224,512]{2,1,0:T(8,128)(2,1)S(1)}, u32[]{:S(2)}, u32[]{:S(2)}) collective-permute-start(bf16[4,224,512]{2,1,0:T(8,128)(2,1)S(1)} %get-tuple-element.207), channel_id=1, source_target_pairs={{0,1},{1,0},{2,3},{3,2},{4,5},{5,4},{6,7},{7,6},{8,9},{9,8},{10,11... | collective-permute-start | bytes 2752520 | tf_op jit(solution)/shard_map/ppermute | solution.py:463
  157.3 13.0 %collective-permute-start.27 = (bf16[192,640]{1,0:T(8,128)(2,1)S(1)}, bf16[192,640]{1,0:T(8,128)(2,1)S(1)}, u32[]{:S(2)}, u32[]{:S(2)}) collective-permute-start(bf16[192,640]{1,0:T(8,128)(2,1)S(1)} %get-tuple-element.235), channel_id=1, source_target_pairs={{0,2},{2,0},{4,6},{6,4},{8,10},{10,8},{12,14},{14,12},{16,18},{18,... | collective-permute-start | bytes 737288 | tf_op jit(solution)/shard_map/ppermute | solution.py:463
  158.2 13.2 %collective-permute-start.28 = (bf16[192,640]{1,0:T(8,128)(2,1)S(1)}, bf16[192,640]{1,0:T(8,128)(2,1)S(1)}, u32[]{:S(2)}, u32[]{:S(2)}) collective-permute-start(bf16[192,640]{1,0:T(8,128)(2,1)S(1)} %get-tuple-element.237), channel_id=1, source_target_pairs={{0,4},{2,6},{4,0},{6,2},{8,12},{10,14},{12,8},{14,10},{16,20},{18,... | collective-permute-start | bytes 737288 | tf_op jit(solution)/shard_map/ppermute | solution.py:463
  159.7 11.6 %collective-permute-start.29 = (bf16[192,640]{1,0:T(8,128)(2,1)S(1)}, bf16[192,640]{1,0:T(8,128)(2,1)S(1)}, u32[]{:S(2)}, u32[]{:S(2)}) collective-permute-start(bf16[192,640]{1,0:T(8,128)(2,1)S(1)} %get-tuple-element.236), channel_id=1, source_target_pairs={{0,6},{2,4},{4,2},{6,0},{8,14},{10,12},{12,10},{14,8},{16,22},{18,... | collective-permute-start | bytes 737288 | tf_op jit(solution)/shard_map/ppermute | solution.py:463
  171.8 20.0 %copy-start.25 = (bf16[1024,1536]{1,0:T(8,128)(2,1)S(1)}, bf16[1024,1536]{1,0:T(8,128)(2,1)}, u32[]{:S(2)}) copy-start(bf16[1024,1536]{1,0:T(8,128)(2,1)} %get-tuple-element.212.right.mixed) | copy-start | bytes 9437188
  171.9 25.4 %collective-permute-start.36 = (bf16[48,1536]{1,0:T(8,128)(2,1)S(1)}, bf16[48,1536]{1,0:T(8,128)(2,1)S(1)}, u32[]{:S(2)}, u32[]{:S(2)}) collective-permute-start(bf16[48,1536]{1,0:T(8,128)(2,1)S(1)} %get-tuple-element.247), channel_id=1, source_target_pairs={{0,16},{2,18},{4,20},{6,22},{8,24},{10,26},{12,28},{14,30},{16,0},... | collective-permute-start | bytes 442376 | tf_op jit(solution)/shard_map/ppermute | solution.py:463
  172.3 5.7 %collective-permute-start.35 = (bf16[2,48,640]{2,1,0:T(8,128)(2,1)S(1)}, bf16[2,48,640]{2,1,0:T(8,128)(2,1)S(1)}, u32[]{:S(2)}, u32[]{:S(2)}) collective-permute-start(bf16[2,48,640]{2,1,0:T(8,128)(2,1)S(1)} %slice_bitcast_fusion.14), channel_id=1, source_target_pairs={{0,8},{2,10},{4,12},{6,14},{8,0},{10,2},{12,4},{14,6},{16,24},{18,... | collective-permute-start | bytes 368648 | tf_op jit(solution)/shard_map/ppermute | solution.py:463
  174.0 8.6 %collective-permute-start.32 = (bf16[224,512]{1,0:T(8,128)(2,1)S(1)}, bf16[224,512]{1,0:T(8,128)(2,1)S(1)}, u32[]{:S(2)}, u32[]{:S(2)}) collective-permute-start(bf16[224,512]{1,0:T(8,128)(2,1)S(1)} %get-tuple-element.238), channel_id=1, source_target_pairs={{0,2},{2,0},{4,6},{6,4},{8,10},{10,8},{12,14},{14,12},{16,18},{18,... | collective-permute-start | bytes 688136 | tf_op jit(solution)/shard_map/ppermute | solution.py:463
  175.3 11.1 %collective-permute-start.33 = (bf16[224,512]{1,0:T(8,128)(2,1)S(1)}, bf16[224,512]{1,0:T(8,128)(2,1)S(1)}, u32[]{:S(2)}, u32[]{:S(2)}) collective-permute-start(bf16[224,512]{1,0:T(8,128)(2,1)S(1)} %get-tuple-element.240), channel_id=1, source_target_pairs={{0,4},{2,6},{4,0},{6,2},{8,12},{10,14},{12,8},{14,10},{16,20},{18,... | collective-permute-start | bytes 688136 | tf_op jit(solution)/shard_map/ppermute | solution.py:463
  176.1 10.3 %collective-permute-start.34 = (bf16[224,512]{1,0:T(8,128)(2,1)S(1)}, bf16[224,512]{1,0:T(8,128)(2,1)S(1)}, u32[]{:S(2)}, u32[]{:S(2)}) collective-permute-start(bf16[224,512]{1,0:T(8,128)(2,1)S(1)} %get-tuple-element.239), channel_id=1, source_target_pairs={{0,6},{2,4},{4,2},{6,0},{8,14},{10,12},{12,10},{14,8},{16,22},{18,... | collective-permute-start | bytes 688136 | tf_op jit(solution)/shard_map/ppermute | solution.py:463
  178.0 13.8 %copy-start.15 = (bf16[768,1536]{1,0:T(8,128)(2,1)S(1)}, bf16[768,1536]{1,0:T(8,128)(2,1)}, u32[]{:S(2)}) copy-start(bf16[768,1536]{1,0:T(8,128)(2,1)} %copy-done.14) | copy-start | bytes 7077892
  186.6 10.7 %collective-permute-start.38 = (bf16[80,512]{1,0:T(8,128)(2,1)S(1)}, bf16[80,512]{1,0:T(8,128)(2,1)S(1)}, u32[]{:S(2)}, u32[]{:S(2)}) collective-permute-start(bf16[80,512]{1,0:T(8,128)(2,1)S(1)} %get-tuple-element.245), channel_id=1, source_target_pairs={{0,8},{2,10},{4,12},{6,14},{8,0},{10,2},{12,4},{14,6},{16,24},{18,... | collective-permute-start | bytes 245768 | tf_op jit(solution)/shard_map/ppermute | solution.py:463
  187.2 10.1 %collective-permute-start.39 = (bf16[80,512]{1,0:T(8,128)(2,1)S(1)}, bf16[80,512]{1,0:T(8,128)(2,1)S(1)}, u32[]{:S(2)}, u32[]{:S(2)}) collective-permute-start(bf16[80,512]{1,0:T(8,128)(2,1)S(1)} %get-tuple-element.244), channel_id=1, source_target_pairs={{0,16},{2,18},{4,20},{6,22},{8,24},{10,26},{12,28},{14,30},{16,0},... | collective-permute-start | bytes 245768 | tf_op jit(solution)/shard_map/ppermute | solution.py:463
  189.7 7.6 %collective-permute-start.40 = (bf16[80,512]{1,0:T(8,128)(2,1)S(1)}, bf16[80,512]{1,0:T(8,128)(2,1)S(1)}, u32[]{:S(2)}, u32[]{:S(2)}) collective-permute-start(bf16[80,512]{1,0:T(8,128)(2,1)S(1)} %get-tuple-element.243), channel_id=1, source_target_pairs={{0,24},{2,26},{4,28},{6,30},{8,16},{10,18},{12,20},{14,22},{16,8},... | collective-permute-start | bytes 245768 | tf_op jit(solution)/shard_map/ppermute | solution.py:463
  191.1 6.2 %collective-permute-start.37 = (bf16[48,640]{1,0:T(8,128)(2,1)S(1)}, bf16[48,640]{1,0:T(8,128)(2,1)S(1)}, u32[]{:S(2)}, u32[]{:S(2)}) collective-permute-start(bf16[48,640]{1,0:T(8,128)(2,1)S(1)} %get-tuple-element.251), channel_id=1, source_target_pairs={{0,16},{2,18},{4,20},{6,22},{8,24},{10,26},{12,28},{14,30},{16,0},... | collective-permute-start | bytes 184328 | tf_op jit(solution)/shard_map/ppermute | solution.py:463
  (32 other events, 148.8 us)
